TPU v7x, 32 devices: a whole 2x2x4 slice. The times are simulated.
32 devices in a mesh: grp: 4 (over y, x), band: 8 (over z, core).
Axes of the slice: x: 2, y: 2, z: 4, core: 2. Of those that a mesh axis runs over, the one named last changes fastest.
Arguments:
- raw: bfloat16 [2, 256, 16384], P(None, 'band', 'grp'), may hold values from -6 to 6
- taps: int32 [5, 2, 4, 512], replicated, may hold values from 0 to 255, as said below
- weights: float32 [5, 2, 4, 512], replicated, may hold values from -0.11 to 1.6, as said below
- shifts: float32 [5], replicated, may hold values from 1 to 3
Outputs:
- image: bfloat16 [2, 16384, 256], P(None, ('grp', 'band'))
Inputs may be any that keep to these rules, and one draw needn't show every extreme that they name: taps[l, h, s, j] = c - 1 + s clipped to the half sector, where c is j / 2 or (j + 1) / 2 rounded down, clipped likewise. `weights`: each group of four coefficients is a cubic Lagrange stencil times a positive factor.
All inputs are finite; a program needn't handle non-finite values.
Results may differ from a plain program's by a relative error of at most 0.011.
Values may be sent and summed in bfloat16 or wider, within the bound.
No kernel may reach another device: no remote copies, remote signals or barrier semaphores. Data moves between devices by JAX's collectives and lax.ppermute only.
A program may use at most 64 MiB of HBM per device.

v0:
```python
import math

import jax
import jax.numpy as jnp
from jax import lax
from jax.sharding import PartitionSpec as P

ANGLES = 512
BAND_LEVELS = 3
LEVELS = 5


inv_root_two = 0.7071067811865476


def swapped(block, axis, apart):
    count = lax.axis_size(axis)
    route = []
    for low in range(count):
        high = low | 1 << apart
        if high != low and high < count:
            route += [(low, high), (high, low)]
    return lax.ppermute(block, axis, route)


def range_table(freq_count):
    column = jnp.arange(freq_count, dtype=jnp.int32)
    phases = (column[:, None] * column[None, :] % freq_count).astype(jnp.float32) * (
        2.0 * math.pi / freq_count
    )
    cosine = jnp.cos(phases)
    sine_map = jnp.sin(phases)
    real_rows = jnp.stack([cosine, -sine_map], axis=1)
    imag_rows = jnp.stack([sine_map, cosine], axis=1)
    return jnp.stack([real_rows, imag_rows], axis=0).astype(jnp.bfloat16)


def beam_table(angles, pulses):
    angle_ids = jnp.arange(angles, dtype=jnp.int32)
    pulse_ids = jnp.arange(pulses, dtype=jnp.int32)
    phases = (angle_ids[:, None] * pulse_ids[None, :] % angles).astype(jnp.float32) * (
        2.0 * math.pi / angles
    )
    cosine = jnp.cos(phases)
    sine_map = jnp.sin(phases)
    real_rows = jnp.stack([cosine, sine_map], axis=1)
    imag_rows = jnp.stack([-sine_map, cosine], axis=1)
    return jnp.stack([real_rows, imag_rows], axis=0).astype(jnp.bfloat16)


def interp_matrix(tap_rows, weight_rows, half_len):
    onehot = tap_rows[:, :, None] == jnp.arange(half_len, dtype=jnp.int32)[None, None, :]
    matrix = jnp.sum(
        jnp.where(onehot, weight_rows[:, :, None], jnp.zeros((), weight_rows.dtype)), axis=0
    )
    return matrix.astype(jnp.bfloat16)


def phase_angle(shift_now, half_bit, angles, freq_count):
    angle_pos = (half_bit * angles + jnp.arange(angles, dtype=jnp.int32)).astype(jnp.float32)
    across = (angle_pos + 0.5) / (2.0 * angles) - 0.5
    ranges = (jnp.arange(freq_count, dtype=jnp.int32) + freq_count).astype(jnp.float32) / freq_count
    return 2.0 * math.pi * shift_now * across[:, None] * ranges[None, :]


def rotate(real_part, imag_part, cosine, sine_map):
    return (cosine * real_part - sine_map * imag_part, cosine * imag_part + sine_map * real_part)


def swap_half(piece_half, section_no):
    if section_no == 0:
        return swapped(piece_half, "band", 0)
    if section_no < BAND_LEVELS:
        return swapped(piece_half, "band", section_no)
    return swapped(piece_half, "grp", section_no - BAND_LEVELS)


def merge_level(section_no, half_bit, own_half, fetch_half, taps, weights, shifts):
    half_len = own_half.shape[1]
    angles = 2 * half_len
    freq_count = own_half.shape[2]
    tap_rows = lax.dynamic_index_in_dim(taps[section_no], half_bit, 0, keepdims=False)
    weight_rows = lax.dynamic_index_in_dim(weights[section_no], half_bit, 0, keepdims=False)
    matrix = interp_matrix(tap_rows, weight_rows, half_len)
    angle_map = phase_angle(shifts[section_no], half_bit, angles, freq_count)
    cosine = jnp.cos(angle_map)
    sine_map = jnp.sin(angle_map)
    own_sign = (1 - 2 * half_bit).astype(jnp.float32)
    partner = fetch_half()
    stacked = jnp.einsum(
        "jk,ncks->ncjs", matrix, jnp.stack([own_half, partner]), preferred_element_type=jnp.float32
    )
    own_prod = stacked[0]
    partner_prod = stacked[1]
    own_sine = own_sign * sine_map
    own_re, own_im = rotate(own_prod[0], own_prod[1], cosine, own_sine)
    partner_re, partner_im = rotate(partner_prod[0], partner_prod[1], cosine, -own_sine)
    merged = jnp.stack([own_re + partner_re, own_im + partner_im]) * inv_root_two
    return merged.astype(jnp.bfloat16)


def later_fetch(sent_half, section_no):

    def fetch_half():
        return swap_half(sent_half, section_no)

    return fetch_half


def on_device(raw, taps, weights, shifts):
    samples = lax.all_to_all(raw, "band", split_axis=2, concat_axis=1, tiled=True)
    freq_count = samples.shape[1]
    pulses = samples.shape[2]
    half_len = ANGLES // 2
    profile = (
        jnp.einsum(
            "cfq,cfds->dqs", samples, range_table(freq_count), preferred_element_type=jnp.float32
        )
        * (1.0 / math.sqrt(freq_count))
    ).astype(jnp.bfloat16)
    beam_full = beam_table(ANGLES, pulses)
    band_pos = lax.axis_index("band")
    grp_pos = lax.axis_index("grp")

    def bit_of(section_no):
        if section_no < BAND_LEVELS:
            return band_pos >> section_no & 1
        return grp_pos >> section_no - BAND_LEVELS & 1

    half_bit = bit_of(0)
    product = jnp.einsum("dacq,cqr->dar", beam_full, profile, preferred_element_type=jnp.float32)
    whole = (product * (1.0 / math.sqrt(pulses))).astype(jnp.bfloat16)
    kept_half = lax.dynamic_slice_in_dim(whole, half_bit * half_len, half_len, 1)
    sent_half = lax.dynamic_slice_in_dim(whole, (1 - half_bit) * half_len, half_len, 1)
    images = merge_level(
        0, half_bit, kept_half, lambda: swap_half(sent_half, 0), taps, weights, shifts
    )
    for section_no in range(1, LEVELS):
        level_bit = bit_of(section_no)
        kept_half = lax.dynamic_slice_in_dim(images, level_bit * half_len, half_len, 1)
        sent_half = lax.dynamic_slice_in_dim(images, (1 - level_bit) * half_len, half_len, 1)
        images = merge_level(
            section_no,
            level_bit,
            kept_half,
            later_fetch(sent_half, section_no),
            taps,
            weights,
            shifts,
        )
    return images


def solution(mesh):
    in_specs = (P(None, "band", "grp"), P(), P(), P())
    out_specs = P(None, ("grp", "band"), None)
    return jax.shard_map(
        on_device, mesh=mesh, in_specs=in_specs, out_specs=out_specs, check_vma=False
    )
```

profile of v0, /device:TPU:0, one launch (start us, length us, event | category | flops | bytes accessed | tf_op | source)
XLA Modules:
  0.0 92.5 jit_solution(3884369756378337783)
XLA Ops:
  0.0 4.9 %copy.22 = bf16[2,32,4096]{1,0,2:T(2,128)(2,1)S(1)} copy(bf16[2,32,4096]{2,1,0:T(8,128)(2,1)} %param.4) | data formatting | bytes 1048576 | tf_op args[0]
  4.9 2.7 %reshape.1270 = bf16[8,2,16384]{2,1,0:T(2,128)(2,1)} reshape(bf16[4096,2,32]{2,1,0:T(2,128)(2,1)S(1)} %bitcast.240) | data formatting | bytes 1048576
  7.6 6.3 %all-to-all-start = ((bf16[8,2,16384]{2,1,0:T(2,128)(2,1)}), bf16[8,2,16384]{2,1,0:T(2,128)(2,1)S(1)}, u32[]{:S(2)}, u32[]{:S(2)}) async-start(bf16[8,2,16384]{2,1,0:T(2,128)(2,1)} %reshape.1270), calls=%async_computation | async-start | bytes 1048576 | tf_op jit(solution)/shard_map/all_to_all | solution.py:111
  18.8 1.1 %negate_convert_fusion.1 = (bf16[256,1,256]{0,2,1:T(8,128)(2,1)S(1)}, bf16[256,1,256]{0,2,1:T(8,128)(2,1)S(1)}) fusion(), kind=kLoop, calls=%fused_computation.203 | loop fusion | flops 1114112 | bytes 262144 | tf_op jit(solution)/shard_map/convert.7
  19.9 4.0 %fusion.130 = bf16[512,1,512]{2,0,1:T(8,128)(2,1)S(1)} fusion(), kind=kLoop, calls=%fused_computation.179 | loop fusion | flops 3932160 | bytes 524288 | tf_op jit(solution)/shard_map/convert.15
  24.6 4.3 %negate_convert_fusion = (bf16[512,1,512]{2,0,1:T(8,128)(2,1)S(1)}, bf16[512,1,512]{2,0,1:T(8,128)(2,1)S(1)}) fusion(), kind=kLoop, calls=%fused_computation.44 | loop fusion | flops 4456448 | bytes 1048576 | tf_op jit(solution)/shard_map/convert.11
  28.9 1.5 %maximum_bitcast_fusion = (bf16[1,512,2,512]{3,1,2,0:T(8,128)(2,1)}, bf16[1,512,2,512]{3,1,2,0:T(8,128)(2,1)}) fusion(bf16[512,1,512]{2,0,1:T(8,128)(2,1)S(1)} %fusion.130, bf16[512,1,512]{2,0,1:T(8,128)(2,1)S(1)} %get-tuple-element.45, bf16[512,1,512]{2,0,1:T(8,128)(2,1)S(1)} %get-tuple-element.44), kind=kLoop, calls=%fused_computation.32 | loop fusion | flops 1048576 | bytes 3670016 | tf_op jit(solution)/shard_map/stack | solution.py:48
  30.4 1.0 %reshape.1271 = bf16[4096,2,32]{2,1,0:T(2,128)(2,1)S(1)} reshape(bf16[8,2,16384]{2,1,0:T(2,128)(2,1)S(1)} %all-to-all-done) | data formatting | bytes 1048576
  31.5 3.3 %copy.38 = bf16[2,32,8,512]{3,1,2,0:T(8,128)(2,1)} copy(bf16[2,32,8,512]{1,0,3,2:T(2,128)(2,1)S(1)} %bitcast.239) | data formatting | bytes 1048576 | tf_op jit(solution)/shard_map/all_to_all | solution.py:111
  34.8 2.5 %fusion.11 = bf16[2,512,256]{2,1,0:T(8,128)(2,1)S(1)} fusion(bf16[1,512,2,512]{3,1,2,0:T(8,128)(2,1)} %get-tuple-element.26, bf16[1,512,2,512]{3,1,2,0:T(8,128)(2,1)S(1)} %copy-done, bf16[2,256,512,1]{2,1,0,3:T(8,128)(2,1)} %bitcast.241, bf16[1,256,2,256]{1,3,0,2:T(8,128)(2,1)} %get-tuple-element.28, bf16[1,256,2,256]{1,3,0,2:T(8,128)(2,1)S(1)} %get-tuple-element.27), kind=kOutput, calls=%fused_computation.26 | convolution fusion | flops 807665664 | bytes 3670016 | tf_op jit(solution)/shard_map/dacq,cqr->dar/dot_general | solution.py:131
  39.6 2.5 %fusion.96 = (f32[1,512,256]{1,2,0:T(8,128)S(1)}, f32[1,512,256]{1,2,0:T(8,128)S(1)}) fusion(f32[2,2,512,256]{2,3,1,0:T(8,128)S(1)} %convolution_bitcast_fusion.4, f32[]{:T(128)S(6)} %convert_element_type.170, f32[512]{0:T(512)S(1)} %add_multiply_fusion, f32[256]{0:T(256)S(1)} %convert_multiply_fusion), kind=kLoop, calls=%fused_computation.128 | loop fusion | flops 2228224 | bytes 3148804 | tf_op jit(solution)/shard_map/add | solution.py:98
  42.3 2.0 %collective-permute-start.1 = (bf16[2,256,256]{1,2,0:T(8,128)(2,1)S(1)}, bf16[2,256,256]{1,2,0:T(8,128)(2,1)S(1)}, u32[]{:S(2)}, u32[]{:S(2)}) collective-permute-start(bf16[2,256,256]{1,2,0:T(8,128)(2,1)S(1)} %get-tuple-element.22), channel_id=1, source_target_pairs={{0,2},{2,0},{1,3},{3,1},{4,6},{6,4},{5,7},{7,5},{8,10},{10,8},{9,1... | collective-permute-start | bytes 786440 | tf_op jit(solution)/shard_map/ppermute | solution.py:23
  45.0 5.9 %collective-permute-done.1 = bf16[2,256,256]{1,2,0:T(8,128)(2,1)S(1)} collective-permute-done((bf16[2,256,256]{1,2,0:T(8,128)(2,1)S(1)}, bf16[2,256,256]{1,2,0:T(8,128)(2,1)S(1)}, u32[]{:S(2)}, u32[]{:S(2)}) %collective-permute-start.1) | collective-permute-done | bytes 262176 | tf_op jit(solution)/shard_map/ppermute | solution.py:23
  51.4 2.5 %fusion.84 = (f32[1,512,256]{1,2,0:T(8,128)S(1)}, f32[1,512,256]{1,2,0:T(8,128)S(1)}) fusion(f32[2,2,512,256]{2,3,1,0:T(8,128)S(1)} %convolution_bitcast_fusion.3, f32[]{:T(128)S(6)} %convert_element_type.173, f32[512]{0:T(512)S(1)} %add_multiply_fusion.1, f32[256]{0:T(256)S(1)} %convert_multiply_fusion), kind=kLoop, calls=%fused_computation.116 | loop fusion | flops 2228224 | bytes 3148804 | tf_op jit(solution)/shard_map/add | solution.py:98
  54.1 2.6 %collective-permute-start.2 = (bf16[2,256,256]{1,2,0:T(8,128)(2,1)S(1)}, bf16[2,256,256]{1,2,0:T(8,128)(2,1)S(1)}, u32[]{:S(2)}, u32[]{:S(2)}) collective-permute-start(bf16[2,256,256]{1,2,0:T(8,128)(2,1)S(1)} %get-tuple-element.20), channel_id=1, source_target_pairs={{0,4},{4,0},{1,5},{5,1},{2,6},{6,2},{3,7},{7,3},{8,12},{12,8},{9,1... | collective-permute-start | bytes 786440 | tf_op jit(solution)/shard_map/ppermute | solution.py:23
  57.5 11.0 %collective-permute-done.2 = bf16[2,256,256]{1,2,0:T(8,128)(2,1)S(1)} collective-permute-done((bf16[2,256,256]{1,2,0:T(8,128)(2,1)S(1)}, bf16[2,256,256]{1,2,0:T(8,128)(2,1)S(1)}, u32[]{:S(2)}, u32[]{:S(2)}) %collective-permute-start.2) | collective-permute-done | bytes 262176 | tf_op jit(solution)/shard_map/ppermute | solution.py:23
  68.9 2.5 %fusion.72 = (f32[1,512,256]{1,2,0:T(8,128)S(1)}, f32[1,512,256]{1,2,0:T(8,128)S(1)}) fusion(f32[2,2,512,256]{2,3,1,0:T(8,128)S(1)} %convolution_bitcast_fusion.2, f32[]{:T(128)S(6)} %convert_element_type.176, f32[512]{0:T(512)S(1)} %add_multiply_fusion.2, f32[256]{0:T(256)S(1)} %convert_multiply_fusion), kind=kLoop, calls=%fused_computation.104 | loop fusion | flops 2228224 | bytes 3148804 | tf_op jit(solution)/shard_map/add | solution.py:98
  71.5 1.6 %collective-permute-start.3 = (bf16[2,256,256]{1,2,0:T(8,128)(2,1)S(1)}, bf16[2,256,256]{1,2,0:T(8,128)(2,1)S(1)}, u32[]{:S(2)}, u32[]{:S(2)}) collective-permute-start(bf16[2,256,256]{1,2,0:T(8,128)(2,1)S(1)} %get-tuple-element.18), channel_id=1, source_target_pairs={{0,8},{8,0},{16,24},{24,16},{1,9},{9,1},{17,25},{25,17},{2,10},{10... | collective-permute-start | bytes 786440 | tf_op jit(solution)/shard_map/ppermute | solution.py:23
  73.9 5.0 %collective-permute-done.3 = bf16[2,256,256]{1,2,0:T(8,128)(2,1)S(1)} collective-permute-done((bf16[2,256,256]{1,2,0:T(8,128)(2,1)S(1)}, bf16[2,256,256]{1,2,0:T(8,128)(2,1)S(1)}, u32[]{:S(2)}, u32[]{:S(2)}) %collective-permute-start.3) | collective-permute-done | bytes 262176 | tf_op jit(solution)/shard_map/ppermute | solution.py:23
  79.4 2.5 %fusion.60 = (f32[1,512,256]{1,2,0:T(8,128)S(1)}, f32[1,512,256]{1,2,0:T(8,128)S(1)}) fusion(f32[2,2,512,256]{2,3,1,0:T(8,128)S(1)} %convolution_bitcast_fusion.1, f32[]{:T(128)S(6)} %convert_element_type.179, f32[512]{0:T(512)S(1)} %add_multiply_fusion.3, f32[256]{0:T(256)S(1)} %convert_multiply_fusion), kind=kLoop, calls=%fused_computation.92 | loop fusion | flops 2228224 | bytes 3148804 | tf_op jit(solution)/shard_map/add | solution.py:98
  82.0 1.6 %collective-permute-start.4 = (bf16[2,256,256]{1,2,0:T(8,128)(2,1)S(1)}, bf16[2,256,256]{1,2,0:T(8,128)(2,1)S(1)}, u32[]{:S(2)}, u32[]{:S(2)}) collective-permute-start(bf16[2,256,256]{1,2,0:T(8,128)(2,1)S(1)} %get-tuple-element.16), channel_id=1, source_target_pairs={{0,16},{16,0},{8,24},{24,8},{1,17},{17,1},{9,25},{25,9},{2,18},{18... | collective-permute-start | bytes 786440 | tf_op jit(solution)/shard_map/ppermute | solution.py:23
  84.4 4.1 %collective-permute-done.4 = bf16[2,256,256]{1,2,0:T(8,128)(2,1)S(1)} collective-permute-done((bf16[2,256,256]{1,2,0:T(8,128)(2,1)S(1)}, bf16[2,256,256]{1,2,0:T(8,128)(2,1)S(1)}, u32[]{:S(2)}, u32[]{:S(2)}) %collective-permute-start.4) | collective-permute-done | bytes 262176 | tf_op jit(solution)/shard_map/ppermute | solution.py:23
  88.9 2.5 %fusion.48 = (f32[1,512,256]{1,2,0:T(8,128)S(1)}, f32[1,512,256]{1,2,0:T(8,128)S(1)}) fusion(f32[2,2,512,256]{2,3,1,0:T(8,128)S(1)} %convolution_bitcast_fusion, f32[]{:T(128)S(6)} %convert_element_type.182, f32[256]{0:T(256)S(1)} %convert_multiply_fusion, f32[512]{0:T(512)S(1)} %add_multiply_fusion.4), kind=kLoop, calls=%fused_computation.80 | loop fusion | flops 2228224 | bytes 3148804 | tf_op jit(solution)/shard_map/add | solution.py:98
  91.5 1.0 %copy.27 = bf16[2,512,256]{2,1,0:T(8,128)(2,1)} copy(bf16[2,512,256]{1,2,0:T(8,128)(2,1)S(1)} %fusion.23) | data formatting | bytes 1048576 | tf_op jit(solution)/shard_map/convert_element_type | solution.py:99
  (52 shorter events, 10.4 us)
Async XLA Ops:
  4.9 9.0 %copy-start.1 = (f32[5,2,4,512]{3,2,1,0:T(4,128)S(1)}, f32[5,2,4,512]{3,2,1,0:T(4,128)}, u32[]{:S(2)}) copy-start(f32[5,2,4,512]{3,2,1,0:T(4,128)} %param.6) | copy-start | bytes 245764
  4.9 9.0 %copy-start.2 = (s32[5,2,4,512]{3,2,1,0:T(4,128)S(1)}, s32[5,2,4,512]{3,2,1,0:T(4,128)}, u32[]{:S(2)}) copy-start(s32[5,2,4,512]{3,2,1,0:T(4,128)} %param.5) | copy-start | bytes 245764
  4.9 9.1 %copy-start.3 = (f32[5]{0:T(128)S(1)}, f32[5]{0:T(128)}, u32[]{:S(2)}) copy-start(f32[5]{0:T(128)} %param.7) | copy-start | bytes 64
  7.6 22.9 %all-to-all-start = ((bf16[8,2,16384]{2,1,0:T(2,128)(2,1)}), bf16[8,2,16384]{2,1,0:T(2,128)(2,1)S(1)}, u32[]{:S(2)}, u32[]{:S(2)}) async-start(bf16[8,2,16384]{2,1,0:T(2,128)(2,1)} %reshape.1270), calls=%async_computation | async-start | bytes 1048576 | tf_op jit(solution)/shard_map/all_to_all | solution.py:111
  31.5 3.4 %copy-start = (bf16[1,512,2,512]{3,1,2,0:T(8,128)(2,1)S(1)}, bf16[1,512,2,512]{3,1,2,0:T(8,128)(2,1)}, u32[]{:S(2)}) copy-start(bf16[1,512,2,512]{3,1,2,0:T(8,128)(2,1)} %get-tuple-element.25) | copy-start | bytes 3145732
  37.4 1.7 %collective-permute-start = (bf16[2,256,256]{2,1,0:T(8,128)(2,1)S(1)}, bf16[2,256,256]{2,1,0:T(8,128)(2,1)S(1)}, u32[]{:S(2)}, u32[]{:S(2)}) collective-permute-start(bf16[2,256,256]{2,1,0:T(8,128)(2,1)S(1)} %get-tuple-element.24), channel_id=1, source_target_pairs={{0,1},{1,0},{2,3},{3,2},{4,5},{5,4},{6,7},{7,6},{8,9},{9,8},{10,11... | collective-permute-start | bytes 786440 | tf_op jit(solution)/shard_map/ppermute | solution.py:23
  42.3 8.7 %collective-permute-start.1 = (bf16[2,256,256]{1,2,0:T(8,128)(2,1)S(1)}, bf16[2,256,256]{1,2,0:T(8,128)(2,1)S(1)}, u32[]{:S(2)}, u32[]{:S(2)}) collective-permute-start(bf16[2,256,256]{1,2,0:T(8,128)(2,1)S(1)} %get-tuple-element.22), channel_id=1, source_target_pairs={{0,2},{2,0},{1,3},{3,1},{4,6},{6,4},{5,7},{7,5},{8,10},{10,8},{9,1... | collective-permute-start | bytes 786440 | tf_op jit(solution)/shard_map/ppermute | solution.py:23
  54.1 14.3 %collective-permute-start.2 = (bf16[2,256,256]{1,2,0:T(8,128)(2,1)S(1)}, bf16[2,256,256]{1,2,0:T(8,128)(2,1)S(1)}, u32[]{:S(2)}, u32[]{:S(2)}) collective-permute-start(bf16[2,256,256]{1,2,0:T(8,128)(2,1)S(1)} %get-tuple-element.20), channel_id=1, source_target_pairs={{0,4},{4,0},{1,5},{5,1},{2,6},{6,2},{3,7},{7,3},{8,12},{12,8},{9,1... | collective-permute-start | bytes 786440 | tf_op jit(solution)/shard_map/ppermute | solution.py:23
  71.5 7.4 %collective-permute-start.3 = (bf16[2,256,256]{1,2,0:T(8,128)(2,1)S(1)}, bf16[2,256,256]{1,2,0:T(8,128)(2,1)S(1)}, u32[]{:S(2)}, u32[]{:S(2)}) collective-permute-start(bf16[2,256,256]{1,2,0:T(8,128)(2,1)S(1)} %get-tuple-element.18), channel_id=1, source_target_pairs={{0,8},{8,0},{16,24},{24,16},{1,9},{9,1},{17,25},{25,17},{2,10},{10... | collective-permute-start | bytes 786440 | tf_op jit(solution)/shard_map/ppermute | solution.py:23
  82.0 6.4 %collective-permute-start.4 = (bf16[2,256,256]{1,2,0:T(8,128)(2,1)S(1)}, bf16[2,256,256]{1,2,0:T(8,128)(2,1)S(1)}, u32[]{:S(2)}, u32[]{:S(2)}) collective-permute-start(bf16[2,256,256]{1,2,0:T(8,128)(2,1)S(1)} %get-tuple-element.16), channel_id=1, source_target_pairs={{0,16},{16,0},{8,24},{24,8},{1,17},{17,1},{9,25},{25,9},{2,18},{18... | collective-permute-start | bytes 786440 | tf_op jit(solution)/shard_map/ppermute | solution.py:23
where the time goes:
time: 93.1 us; the launch traced here: 92.5 us
  other arithmetic  29.4 us (32%)
  waiting for transfers between devices  26.4 us (28%)
  starting transfers between devices  14.6 us (16%)
  local copies, waits for them, and re-layouts  13.9 us (15%)
  matrix products  4.89 us (5%)
  between operations  3.39 us (4%)
    ppermute x5, waiting for transfers between devices, swapped(): return lax.ppermute(block, axis, route)  26.4 us
    add x5, other arithmetic, merge_level(): own_re + partner_re  12.3 us
    another operation x4, other arithmetic  10.4 us
    unnamed x11, local copies, waits for them, and re-layouts  8.57 us
    ppermute x5, starting transfers between devices, swapped(): return lax.ppermute(block, axis, route)  8.29 us
    all_to_all x1, starting transfers between devices, on_device(): lax.all_to_all(raw, 'band', split_axis=2, concat_axis=1, tiled=True)  6.33 us
    reduce_sum x5, other arithmetic, interp_matrix(): jnp.sum(jnp.where(onehot, weight_rows[:, :, None], jnp.zeros((), weight_r...  3.74 us
    all_to_all x1, local copies, waits for them, and re-layouts, on_device(): lax.all_to_all(raw, 'band', split_axis=2, concat_axis=1, tiled=True)  3.35 us
  transfers between devices with their start and end apart: 6, of which 5 were waited for; matrix products, arithmetic and copies ran while one was open for 19% of the time, Pallas kernels for 0%

commit v1 on v0

v1 whole, which is shorter than its diff:
```python
import functools
import math

import jax
import jax.numpy as jnp
import ml_dtypes
import numpy as np
from jax import lax
from jax.experimental import pallas as pl
from jax.experimental.pallas import tpu as pltpu
from jax.sharding import PartitionSpec as P

ANGLES = 512
HALF = ANGLES // 2
BAND_LEVELS = 3
GRP_LEVELS = 2
LEVELS = BAND_LEVELS + GRP_LEVELS
SUBS = 1 << BAND_LEVELS
MATES = 1 << GRP_LEVELS
ROOT_HALF = 0.7071067811865476


def up_to(value, unit):
    return -(-value // unit) * unit


def rows_read(low, high):
    return max(0, low // 2 - 1), min(HALF - 1, (high + 1) // 2 + 2)


WIDE = up_to(rows_read(0, HALF - 1)[1] + 1, 16)
WIDE_STEP = HALF - WIDE


def first_windows():
    spans = []
    for h2 in (0, 1):
        low, high = rows_read(h2 * HALF, h2 * HALF + HALF - 1)
        for h1 in (0, 1):
            spans.append(rows_read(h1 * HALF + low, h1 * HALF + high))
    rows = up_to(max(high - low + 1 for low, high in spans), 8)
    return [min(low, HALF - rows) for low, high in spans], rows


FIRST_STARTS, FIRST = first_windows()
FIRST_PAD = up_to(FIRST, 16)


def beam_rows(pulses):
    pulse_ids = np.arange(pulses)
    sectors = []
    for sector in range(SUBS):
        start = (sector & 1) * HALF + FIRST_STARTS[sector >> 1]
        angle_ids = start + np.arange(FIRST)
        phases = (angle_ids[:, None] * pulse_ids[None, :] % ANGLES) * (2.0 * math.pi / ANGLES)
        sectors.append(np.concatenate([np.cos(phases), np.sin(phases)], axis=1))
    return np.concatenate(sectors, axis=0).astype(ml_dtypes.bfloat16)


def range_rows(freq_count, freq_local):
    ids = np.arange(freq_count)
    phases = (ids[:, None] * ids[None, :] % freq_count) * (2.0 * math.pi / freq_count)
    cosine, sine = np.cos(phases), np.sin(phases)
    table = np.stack(
        [np.concatenate([cosine, -sine], axis=1), np.concatenate([sine, cosine], axis=1)]
    )
    table = table.reshape(2, freq_count // freq_local, freq_local, 2 * freq_count)
    table = table.transpose(1, 0, 2, 3).reshape(-1, 2 * freq_local, 2 * freq_count)
    return table.astype(ml_dtypes.bfloat16)


def beam_kernel(pos, raw, table, *rest, pulses):
    outs, (rhs, acc) = rest[:-2], rest[-2:]
    freqs = raw.shape[1]
    band_pos = pos[0]
    scale = 1.0 / math.sqrt(pulses)
    for upper in range(len(outs) // SUBS):
        block = band_pos // SUBS ^ upper
        for t in range(SUBS):
            at = pl.multiple_of((block * SUBS + t) * pulses, pulses)
            real = raw[0, :, pl.ds(at, pulses)]
            imag = raw[1, :, pl.ds(at, pulses)]
            row = t * 2 * freqs
            rhs[row : row + freqs, :pulses] = real
            rhs[row : row + freqs, pulses:] = imag
            rhs[row + freqs : row + 2 * freqs, :pulses] = imag
            rhs[row + freqs : row + 2 * freqs, pulses:] = -real
        acc[...] = lax.dot_general(
            table[...], rhs[...], (((1,), (1,)), ((), ())), preferred_element_type=jnp.float32
        )
        for low in range(SUBS):
            sector = (band_pos ^ low) & (SUBS - 1)
            start = pl.multiple_of(sector * FIRST, 8)
            outs[upper * SUBS + low][...] = (acc[pl.ds(start, FIRST), :] * scale).astype(
                jnp.bfloat16
            )


def interp_t(taps, weights, start, rows):
    row_ids = lax.broadcasted_iota(jnp.int32, (rows, ANGLES), 0) + start
    total = jnp.zeros((rows, ANGLES), jnp.float32)
    for s in range(taps.shape[0]):
        total += jnp.where(row_ids == taps[s : s + 1, :], weights[s : s + 1, :], 0.0)
    return total


def phase_rows(cos_ref, sin_ref, shift, first, count, sign):
    freqs = cos_ref.shape[1]
    ranges = (
        (lax.broadcasted_iota(jnp.int32, (1, freqs), 1) + freqs).astype(jnp.float32)
        * (2.0 * math.pi / freqs)
        * shift
    )
    groups = count // 8
    coarse_ids = lax.broadcasted_iota(jnp.int32, (groups, 1), 0) * 8 + first
    coarse = ((coarse_ids.astype(jnp.float32) + 0.5) / (2.0 * ANGLES) - 0.5) * ranges
    fine_ids = lax.broadcasted_iota(jnp.int32, (8, 1), 0)
    fine = (fine_ids.astype(jnp.float32) / (2.0 * ANGLES)) * ranges
    coarse_cos, coarse_sin = jnp.cos(coarse) * ROOT_HALF, jnp.sin(coarse) * ROOT_HALF
    fine_cos, fine_sin = jnp.cos(fine), jnp.sin(fine)
    for group in range(groups):
        c, s = coarse_cos[group : group + 1], coarse_sin[group : group + 1]
        cos_ref[group * 8 : group * 8 + 8, :] = c * fine_cos - s * fine_sin
        sin_ref[group * 8 : group * 8 + 8, :] = sign * (s * fine_cos + c * fine_sin)


def table_kernel(
    pos, shifts, taps, weights, ranges,
    range_out, m0, m1, m2, m3, m4, c0, s0, c1, s1, c2, s2, c3, s3, c4, s4, turned,
):
    band_pos, grp_pos = pos[0], pos[1]
    h0, h1, h2 = band_pos & 1, band_pos >> 1 & 1, band_pos >> 2 & 1
    h3, h4 = grp_pos & 1, grp_pos >> 1 & 1
    count = ranges.shape[0]
    depth = ranges.shape[1]
    for k in range(count):
        range_out[k * depth : (k + 1) * depth, :] = ranges[band_pos ^ k]

    def fill(out, level, half, start, rows, first, count, row=0):
        turned[:, :rows] = interp_t(taps[level, half], weights[level, half], start, rows).T
        out[row : row + count, :rows] = turned[pl.ds(first, count), :rows].astype(jnp.bfloat16)

    first_start = FIRST_STARTS[0]
    for combo in range(1, len(FIRST_STARTS)):
        first_start = jnp.where(h1 + 2 * h2 == combo, FIRST_STARTS[combo], first_start)
    wide1 = pl.multiple_of(h1 * HALF + h2 * WIDE_STEP, 16)
    sum_rows = interp_t(taps[0, h0], weights[0, h0], first_start, FIRST_PAD)
    turned[:, :FIRST_PAD] = sum_rows.T
    window = turned[pl.ds(wide1, WIDE), :FIRST_PAD].astype(jnp.bfloat16)
    m0[:WIDE, :FIRST_PAD] = window
    m0[:WIDE, FIRST_PAD:] = window
    m0[WIDE:, :FIRST_PAD] = window
    m0[WIDE:, FIRST_PAD:] = -window
    phase_rows(c0, s0, shifts[0], h0 * ANGLES + wide1, WIDE, 1.0)

    half2 = pl.multiple_of(h2 * HALF, HALF)
    fill(m1, 1, h1, h2 * WIDE_STEP, WIDE, half2, HALF)
    phase_rows(c1, s1, shifts[1], h1 * ANGLES + half2, HALF, 1.0)

    turned[...] = interp_t(taps[2, h2], weights[2, h2], 0, HALF).T
    for k in range(MATES):
        mate = grp_pos ^ k
        at = pl.multiple_of((mate & 1) * HALF + (mate >> 1 & 1) * WIDE_STEP, 16)
        m2[k * WIDE : (k + 1) * WIDE, :] = turned[pl.ds(at, WIDE), :].astype(jnp.bfloat16)
        rows = pl.ds(k * WIDE, WIDE)
        phase_rows(c2.at[rows], s2.at[rows], shifts[2], h2 * ANGLES + at, WIDE, 1.0)

    half4 = pl.multiple_of(h4 * HALF, HALF)
    fill(m3, 3, h3, h4 * WIDE_STEP, WIDE, half4, HALF)
    sign3 = (1 - 2 * h3).astype(jnp.float32)
    phase_rows(c3, s3, shifts[3], h3 * ANGLES + half4, HALF, sign3)
    fill(m4, 4, h4, 0, HALF, 0, ANGLES)
    sign4 = (1 - 2 * h4).astype(jnp.float32)
    phase_rows(c4, s4, shifts[4], h4 * ANGLES, ANGLES, sign4)


def dot(left, right):
    return jnp.dot(left, right, preferred_element_type=jnp.float32)


def turn(out, rows, total, diff, cosine, sine):
    freqs = cosine.shape[1]
    out[rows, :freqs] = (cosine * total[:, :freqs] - sine * diff[:, freqs:]).astype(out.dtype)
    out[rows, freqs:] = (cosine * total[:, freqs:] + sine * diff[:, :freqs]).astype(out.dtype)


def band_kernel(*refs, sources):
    blocks = refs[:sources]
    ranges, m0, m1, m2, c0, s0, c1, s1, c2, s2 = refs[sources : sources + 10]
    outs = refs[sources + 10 : sources + 10 + MATES]
    wide, sub0, sub1, sub2 = refs[sources + 10 + MATES :]
    depth = blocks[0].shape[1] // SUBS
    freqs = c0.shape[1]
    scale = 1.0 / math.sqrt(freqs)
    for t in range(SUBS):
        row = t * FIRST_PAD
        if FIRST_PAD > FIRST:
            wide[row + FIRST : row + FIRST_PAD, :] = jnp.zeros(
                (FIRST_PAD - FIRST, wide.shape[1]), wide.dtype
            )
        for k in range(sources):
            wide[row : row + FIRST, k * depth : (k + 1) * depth] = blocks[k][
                :, t * depth : (t + 1) * depth
            ]
    sub0[...] = (dot(wide[...], ranges[...]) * scale).astype(sub0.dtype)
    for p in range(SUBS // 2):
        both = dot(m0[...], sub0[2 * p * FIRST_PAD : 2 * (p + 1) * FIRST_PAD, :])
        turn(sub1, slice(p * WIDE, (p + 1) * WIDE), both[:WIDE], both[WIDE:], c0[...], s0[...])
    for p in range(SUBS // 4):
        low = dot(m1[...], sub1[2 * p * WIDE : (2 * p + 1) * WIDE, :])
        high = dot(m1[...], sub1[(2 * p + 1) * WIDE : (2 * p + 2) * WIDE, :])
        rows = slice(p * HALF, (p + 1) * HALF)
        turn(sub2, rows, low + high, low - high, c1[...], s1[...])
    for k in range(MATES):
        rows = slice(k * WIDE, (k + 1) * WIDE)
        low = dot(m2[rows, :], sub2[:HALF, :])
        high = dot(m2[rows, :], sub2[HALF:, :])
        turn(outs[k], slice(None), low + high, low - high, c2[rows, :], s2[rows, :])


def grp_kernel(own, along, across, both, m3, m4, c3, s3, c4, s4, out, sub4):
    freqs = c3.shape[1]
    for q, (mine, other) in enumerate(((own, along), (across, both))):
        low = dot(m3[...], mine[...])
        high = dot(m3[...], other[...])
        turn(sub4, slice(q * HALF, (q + 1) * HALF), low + high, low - high, c3[...], s3[...])
    low = dot(m4[...], sub4[:HALF, :])
    high = dot(m4[...], sub4[HALF:, :])
    total, diff = low + high, low - high
    cosine, sine = c4[...], s4[...]
    out[0] = (cosine * total[:, :freqs] - sine * diff[:, freqs:]).astype(out.dtype)
    out[1] = (cosine * total[:, freqs:] + sine * diff[:, :freqs]).astype(out.dtype)


VMEM = pl.BlockSpec(memory_space=pltpu.VMEM)
SMEM = pl.BlockSpec(memory_space=pltpu.SMEM)
PARAMS = pltpu.CompilerParams(vmem_limit_bytes=48 * 1024 * 1024)


def swapped(block, axis, mask):
    count = lax.axis_size(axis)
    return lax.ppermute(block, axis, [(low, low ^ mask) for low in range(count)])


def on_device(raw, taps, weights, shifts):
    n_band = lax.axis_size("band")
    freqs = raw.shape[1]
    freq_count = freqs * n_band
    pulses = raw.shape[2] // n_band
    bf16, f32 = jnp.bfloat16, jnp.float32
    shape = jax.ShapeDtypeStruct
    pos = jnp.stack([lax.axis_index("band"), lax.axis_index("grp")]).astype(jnp.int32)
    lanes = SUBS * 2 * freqs

    beams = pl.pallas_call(
        functools.partial(beam_kernel, pulses=pulses),
        out_shape=[shape((FIRST, lanes), bf16)] * n_band,
        in_specs=[SMEM, VMEM, VMEM],
        out_specs=[VMEM] * n_band,
        scratch_shapes=[
            pltpu.VMEM((lanes, 2 * pulses), bf16),
            pltpu.VMEM((SUBS * FIRST, lanes), f32),
        ],
        compiler_params=PARAMS,
        cost_estimate=pl.CostEstimate(
            flops=2 * SUBS * FIRST * 2 * pulses * lanes, bytes_accessed=1 << 21, transcendentals=0
        ),
        name="beam",
    )(pos, raw, jnp.asarray(beam_rows(pulses)))

    wide2 = 2 * freq_count
    tables = pl.pallas_call(
        table_kernel,
        out_shape=[
            shape((wide2, wide2), bf16),
            shape((2 * WIDE, 2 * FIRST_PAD), bf16),
            shape((HALF, WIDE), bf16),
            shape((MATES * WIDE, HALF), bf16),
            shape((HALF, WIDE), bf16),
            shape((ANGLES, HALF), bf16),
        ]
        + [
            shape((rows, freq_count), f32)
            for rows in (WIDE, HALF, MATES * WIDE, HALF, ANGLES)
            for _ in range(2)
        ],
        in_specs=[SMEM, SMEM, VMEM, VMEM, VMEM],
        out_specs=[VMEM] * 16,
        scratch_shapes=[pltpu.VMEM((ANGLES, HALF), f32)],
        compiler_params=PARAMS,
        cost_estimate=pl.CostEstimate(
            flops=1 << 24, bytes_accessed=1 << 23, transcendentals=1 << 18
        ),
        name="tables",
    )(pos, shifts, taps, weights, jnp.asarray(range_rows(freq_count, freqs)))
    ranges, m0, m1, m2, m3, m4, c0, s0, c1, s1, c2, s2, c3, s3, c4, s4 = tables

    blocks = [beams[0]] + [swapped(beams[k], "band", k) for k in range(1, n_band)]
    pieces = pl.pallas_call(
        functools.partial(band_kernel, sources=n_band),
        out_shape=[shape((WIDE, wide2), bf16)] * MATES,
        in_specs=[VMEM] * (n_band + 10),
        out_specs=[VMEM] * MATES,
        scratch_shapes=[
            pltpu.VMEM((SUBS * FIRST_PAD, wide2), bf16),
            pltpu.VMEM((SUBS * FIRST_PAD, wide2), bf16),
            pltpu.VMEM((SUBS // 2 * WIDE, wide2), bf16),
            pltpu.VMEM((SUBS // 4 * HALF, wide2), bf16),
        ],
        compiler_params=PARAMS,
        cost_estimate=pl.CostEstimate(flops=1 << 31, bytes_accessed=1 << 22, transcendentals=0),
        name="band_merges",
    )(*blocks, ranges, m0, m1, m2, c0, s0, c1, s1, c2, s2)

    halves = [pieces[0]] + [swapped(pieces[k], "grp", k) for k in range(1, MATES)]
    return pl.pallas_call(
        grp_kernel,
        out_shape=shape((2, ANGLES, freq_count), bf16),
        in_specs=[VMEM] * 10,
        out_specs=VMEM,
        scratch_shapes=[pltpu.VMEM((2 * HALF, wide2), bf16)],
        compiler_params=PARAMS,
        cost_estimate=pl.CostEstimate(flops=1 << 30, bytes_accessed=1 << 22, transcendentals=0),
        name="grp_merges",
    )(*halves, m3, m4, c3, s3, c4, s4)


def solution(mesh):
    in_specs = (P(None, "band", "grp"), P(), P(), P())
    out_specs = P(None, ("grp", "band"), None)
    return jax.shard_map(
        on_device, mesh=mesh, in_specs=in_specs, out_specs=out_specs, check_vma=False
    )
```

time: 93.1 us -> 36.1 us (0.39)
  the two profiles are of different devices: /device:TPU:0 before, /device:TPU:16 now
where the time goes in v1:
time: 36.1 us; the launch traced here: 35.9 us
  waiting for transfers between devices  15 us (42%)
  starting transfers between devices  9.89 us (27%)
  Pallas kernels  8.53 us (24%)
  local copies, waits for them, and re-layouts  2.38 us (7%)
    ppermute x10, waiting for transfers between devices, swapped(): lax.ppermute(block, axis, [(low, low ^ mask) for low in range(count)])  15 us
    ppermute x10, starting transfers between devices, swapped(): lax.ppermute(block, axis, [(low, low ^ mask) for low in range(count)])  9.89 us
    pallas_call x1, Pallas kernels, on_device(): pl.pallas_call(table_kernel, out_shape=[shape((wide2, wide2), bf16), shap...  3.59 us
    unnamed x12, local copies, waits for them, and re-layouts  2.38 us
    pallas_call x1, Pallas kernels, on_device(): pl.pallas_call(functools.partial(band_kernel, sources=n_band), out_shape=...  1.81 us
    pallas_call x1, Pallas kernels, on_device(): pl.pallas_call(grp_kernel, out_shape=shape((2, ANGLES, freq_count), bf16)...  1.65 us
    pallas_call x1, Pallas kernels, on_device(): pl.pallas_call(functools.partial(beam_kernel, pulses=pulses), out_shape=[...  1.47 us
  transfers between devices with their start and end apart: 10, of which 5 were waited for; matrix products, arithmetic and copies ran while one was open for 0% of the time, Pallas kernels for 10%

profile of v1, /device:TPU:16, one launch (start us, length us, event | category | flops | bytes accessed | tf_op | source)
XLA Modules:
  0.0 35.9 jit_solution(16742995991440681920)
XLA Ops:
  0.0 0.1 pad_add_fusion.pos
  0.1 1.1 %copy-done.4 = bf16[2,32,4096]{2,1,0:T(8,128)(2,1)S(1)} copy-done((bf16[2,32,4096]{2,1,0:T(8,128)(2,1)S(1)}, bf16[2,32,4096]{2,1,0:T(8,128)(2,1)}, u32[]{:S(2)}) %copy-start.4) | copy-done | bytes 524312
  1.2 1.3 %copy-done.5 = bf16[576,1024]{1,0:T(8,128)(2,1)S(1)} copy-done((bf16[576,1024]{1,0:T(8,128)(2,1)S(1)}, bf16[576,1024]{1,0:T(8,128)(2,1)}, u32[]{:S(2)}) %copy-start.5) | copy-done | bytes 1179672
  2.5 1.5 %beam.1 = (bf16[72,512]{1,0:T(8,128)(2,1)S(1)}, bf16[72,512]{1,0:T(8,128)(2,1)S(1)}, bf16[72,512]{1,0:T(8,128)(2,1)S(1)}, bf16[72,512]{1,0:T(8,128)(2,1)S(1)}, b...) custom-call(s32[2]{0:T(128)S(1)} %pad_add_fusion.pos, ...), custom_call_target="tpu_custom_call" | custom-call | flops 603979776 | bytes 2097152 | tf_op jit(solution)/shard_map/beam/pallas_call | solution.py:255
  3.9 0.1 collective-permute-start
  4.0 1.6 %collective-permute-start.1 = (bf16[72,512]{1,0:T(8,128)(2,1)S(1)}, bf16[72,512]{1,0:T(8,128)(2,1)S(1)}, u32[]{:S(2)}, u32[]{:S(2)}) collective-permute-start(bf16[72,512]{1,0:T(8,128)(2,1)S(1)} %get-tuple-element.35), channel_id=1, source_target_pairs={{0,2},{1,3},{2,0},{3,1},{4,6},{5,7},{6,4},{7,5},{8,10},{9,11},{10,... | collective-permute-start | bytes 221192 | tf_op jit(solution)/shard_map/ppermute | solution.py:242
  5.7 0.2 collective-permute-start.2
  5.9 0.2 collective-permute-start.3
  6.1 2.4 %collective-permute-start.4 = (bf16[72,512]{1,0:T(8,128)(2,1)S(1)}, bf16[72,512]{1,0:T(8,128)(2,1)S(1)}, u32[]{:S(2)}, u32[]{:S(2)}) collective-permute-start(bf16[72,512]{1,0:T(8,128)(2,1)S(1)} %get-tuple-element.38), channel_id=1, source_target_pairs={{0,5},{1,4},{2,7},{3,6},{4,1},{5,0},{6,3},{7,2},{8,13},{9,12},{10,... | collective-permute-start | bytes 221192 | tf_op jit(solution)/shard_map/ppermute | solution.py:242
  8.5 0.5 %collective-permute-start.5 = (bf16[72,512]{1,0:T(8,128)(2,1)S(1)}, bf16[72,512]{1,0:T(8,128)(2,1)S(1)}, u32[]{:S(2)}, u32[]{:S(2)}) collective-permute-start(bf16[72,512]{1,0:T(8,128)(2,1)S(1)} %get-tuple-element.39), channel_id=1, source_target_pairs={{0,6},{1,7},{2,4},{3,5},{4,2},{5,3},{6,0},{7,1},{8,14},{9,15},{10,... | collective-permute-start | bytes 221192 | tf_op jit(solution)/shard_map/ppermute | solution.py:242
  9.0 1.3 %collective-permute-start.6 = (bf16[72,512]{1,0:T(8,128)(2,1)S(1)}, bf16[72,512]{1,0:T(8,128)(2,1)S(1)}, u32[]{:S(2)}, u32[]{:S(2)}) collective-permute-start(bf16[72,512]{1,0:T(8,128)(2,1)S(1)} %get-tuple-element.40), channel_id=1, source_target_pairs={{0,7},{1,6},{2,5},{3,4},{4,3},{5,2},{6,1},{7,0},{8,15},{9,14},{10,... | collective-permute-start | bytes 221192 | tf_op jit(solution)/shard_map/ppermute | solution.py:242
  10.3 3.6 %tables.1 = (bf16[512,512]{1,0:T(8,128)(2,1)S(1)}, bf16[288,160]{1,0:T(8,128)(2,1)S(1)}, bf16[256,144]{1,0:T(8,128)(2,1)S(1)}, bf16[576,256]{1,0:T(8,128)(2,1)S(...) custom-call(s32[2]{0:T(128)S(1)} %pad_add_fusion.pos, ...), custom_call_target="tpu_custom_call" | custom-call | flops 16777216 | bytes 8388608 | tf_op jit(solution)/shard_map/tables/pallas_call | solution.py:272
  13.9 0.0 collective-permute-done.2.refs_3_
  13.9 0.0 collective-permute-done.3.refs_4_
  13.9 3.2 %collective-permute-done.4.refs_5_ = bf16[72,512]{1,0:T(8,128)(2,1)S(1)} collective-permute-done((bf16[72,512]{1,0:T(8,128)(2,1)S(1)}, bf16[72,512]{1,0:T(8,128)(2,1)S(1)}, u32[]{:S(2)}, u32[]{:S(2)}) %collective-permute-start.4) | collective-permute-done | bytes 73760 | tf_op jit(solution)/shard_map/ppermute | solution.py:242
  17.2 4.0 %collective-permute-done.5.refs_6_ = bf16[72,512]{1,0:T(8,128)(2,1)S(1)} collective-permute-done((bf16[72,512]{1,0:T(8,128)(2,1)S(1)}, bf16[72,512]{1,0:T(8,128)(2,1)S(1)}, u32[]{:S(2)}, u32[]{:S(2)}) %collective-permute-start.5) | collective-permute-done | bytes 73760 | tf_op jit(solution)/shard_map/ppermute | solution.py:242
  21.2 1.0 %collective-permute-done.6.refs_7_ = bf16[72,512]{1,0:T(8,128)(2,1)S(1)} collective-permute-done((bf16[72,512]{1,0:T(8,128)(2,1)S(1)}, bf16[72,512]{1,0:T(8,128)(2,1)S(1)}, u32[]{:S(2)}, u32[]{:S(2)}) %collective-permute-start.6) | collective-permute-done | bytes 73760 | tf_op jit(solution)/shard_map/ppermute | solution.py:242
  22.1 1.8 %band_merges.1 = (bf16[144,512]{1,0:T(8,128)(2,1)S(1)}, bf16[144,512]{1,0:T(8,128)(2,1)S(1)}, bf16[144,512]{1,0:T(8,128)(2,1)S(1)}, bf16[144,512]{1,0:T(8,128)(2,1)S(1)}) custom-call(bf16[72,512]{1,0:T(8,128)(2,1)S(1)} %get-tuple-element.33.refs_0_, bf16[72,512]{1,0:T(8,128)(2,1)S(1)} %collective-permute-done.refs_1_, ...), custom_call_target="tpu_custom_call" | custom-call | flops 2147483648 | bytes 4194304 | tf_op jit(solution)/shard_map/band_merges/pallas_call | solution.py:299
  24.0 1.6 %collective-permute-start.7 = (bf16[144,512]{1,0:T(8,128)(2,1)S(1)}, bf16[144,512]{1,0:T(8,128)(2,1)S(1)}, u32[]{:S(2)}, u32[]{:S(2)}) collective-permute-start(bf16[144,512]{1,0:T(8,128)(2,1)S(1)} %get-tuple-element.52), channel_id=1, source_target_pairs={{0,8},{8,0},{16,24},{24,16},{1,9},{9,1},{17,25},{25,17},{2,10},{10... | collective-permute-start | bytes 442376 | tf_op jit(solution)/shard_map/ppermute | solution.py:242
  25.5 1.5 %collective-permute-start.8 = (bf16[144,512]{1,0:T(8,128)(2,1)S(1)}, bf16[144,512]{1,0:T(8,128)(2,1)S(1)}, u32[]{:S(2)}, u32[]{:S(2)}) collective-permute-start(bf16[144,512]{1,0:T(8,128)(2,1)S(1)} %get-tuple-element.53), channel_id=1, source_target_pairs={{0,16},{8,24},{16,0},{24,8},{1,17},{9,25},{17,1},{25,9},{2,18},{10... | collective-permute-start | bytes 442376 | tf_op jit(solution)/shard_map/ppermute | solution.py:242
  27.0 0.5 %collective-permute-start.9 = (bf16[144,512]{1,0:T(8,128)(2,1)S(1)}, bf16[144,512]{1,0:T(8,128)(2,1)S(1)}, u32[]{:S(2)}, u32[]{:S(2)}) collective-permute-start(bf16[144,512]{1,0:T(8,128)(2,1)S(1)} %get-tuple-element.54), channel_id=1, source_target_pairs={{0,24},{8,16},{16,8},{24,0},{1,25},{9,17},{17,9},{25,1},{2,26},{10... | collective-permute-start | bytes 442376 | tf_op jit(solution)/shard_map/ppermute | solution.py:242
  27.5 3.1 %collective-permute-done.7.along = bf16[144,512]{1,0:T(8,128)(2,1)S(1)} collective-permute-done((bf16[144,512]{1,0:T(8,128)(2,1)S(1)}, bf16[144,512]{1,0:T(8,128)(2,1)S(1)}, u32[]{:S(2)}, u32[]{:S(2)}) %collective-permute-start.7) | collective-permute-done | bytes 147488 | tf_op jit(solution)/shard_map/ppermute | solution.py:242
  30.6 3.7 %collective-permute-done.8.across = bf16[144,512]{1,0:T(8,128)(2,1)S(1)} collective-permute-done((bf16[144,512]{1,0:T(8,128)(2,1)S(1)}, bf16[144,512]{1,0:T(8,128)(2,1)S(1)}, u32[]{:S(2)}, u32[]{:S(2)}) %collective-permute-start.8) | collective-permute-done | bytes 147488 | tf_op jit(solution)/shard_map/ppermute | solution.py:242
  34.3 1.7 %grp_merges.1 = bf16[2,512,256]{2,1,0:T(8,128)(2,1)} custom-call(bf16[144,512]{1,0:T(8,128)(2,1)S(1)} %get-tuple-element.51.own, bf16[144,512]{1,0:T(8,128)(2,1)S(1)} %collective-permute-done.7.along, bf16[144,512]{1,0:T(8,128)(2,1)S(1)} %collective-permute-done.8.across, bf16[144,512]{1,0:T(8,128)(2,1)S(1)} %collective-permute-done.9.both, ...), custom_call_target="tpu_custom_call" | custom-call | flops 1073741824 | bytes 4194304 | tf_op jit(solution)/shard_map/grp_merges/pallas_call | solution.py:316
  (13 shorter events, 0.0 us)
Async XLA Ops:
  0.0 10.3 %copy-start = (bf16[8,64,512]{2,1,0:T(8,128)(2,1)S(1)}, bf16[8,64,512]{2,1,0:T(8,128)(2,1)}, u32[]{:S(2)}) copy-start(bf16[8,64,512]{2,1,0:T(8,128)(2,1)} %constant.13.clone.ranges) | copy-start | bytes 1572868
  0.0 10.3 %copy-start.3 = (f32[5]{0:T(128)S(1)}, f32[5]{0:T(128)}, u32[]{:S(2)}) copy-start(f32[5]{0:T(128)} %shifts.1) | copy-start | bytes 64
  0.0 10.3 %copy-start.2 = (f32[5,2,4,512]{3,2,1,0:T(4,128)S(1)}, f32[5,2,4,512]{3,2,1,0:T(4,128)}, u32[]{:S(2)}) copy-start(f32[5,2,4,512]{3,2,1,0:T(4,128)} %weights.1) | copy-start | bytes 245764
  0.0 10.3 %copy-start.1 = (s32[5,2,4,512]{3,2,1,0:T(4,128)S(1)}, s32[5,2,4,512]{3,2,1,0:T(4,128)}, u32[]{:S(2)}) copy-start(s32[5,2,4,512]{3,2,1,0:T(4,128)} %taps.1) | copy-start | bytes 245764
  0.1 1.1 %copy-start.4 = (bf16[2,32,4096]{2,1,0:T(8,128)(2,1)S(1)}, bf16[2,32,4096]{2,1,0:T(8,128)(2,1)}, u32[]{:S(2)}) copy-start(bf16[2,32,4096]{2,1,0:T(8,128)(2,1)} %raw.1) | copy-start | bytes 1572868
  1.2 1.3 %copy-start.5 = (bf16[576,1024]{1,0:T(8,128)(2,1)S(1)}, bf16[576,1024]{1,0:T(8,128)(2,1)}, u32[]{:S(2)}) copy-start(bf16[576,1024]{1,0:T(8,128)(2,1)} %constant.12.clone.table) | copy-start | bytes 3538948
  3.9 4.5 %collective-permute-start = (bf16[72,512]{1,0:T(8,128)(2,1)S(1)}, bf16[72,512]{1,0:T(8,128)(2,1)S(1)}, u32[]{:S(2)}, u32[]{:S(2)}) collective-permute-start(bf16[72,512]{1,0:T(8,128)(2,1)S(1)} %get-tuple-element.34), channel_id=1, source_target_pairs={{0,1},{1,0},{2,3},{3,2},{4,5},{5,4},{6,7},{7,6},{8,9},{9,8},{10,11... | collective-permute-start | bytes 221192 | tf_op jit(solution)/shard_map/ppermute | solution.py:242
  4.0 4.9 %collective-permute-start.1 = (bf16[72,512]{1,0:T(8,128)(2,1)S(1)}, bf16[72,512]{1,0:T(8,128)(2,1)S(1)}, u32[]{:S(2)}, u32[]{:S(2)}) collective-permute-start(bf16[72,512]{1,0:T(8,128)(2,1)S(1)} %get-tuple-element.35), channel_id=1, source_target_pairs={{0,2},{1,3},{2,0},{3,1},{4,6},{5,7},{6,4},{7,5},{8,10},{9,11},{10,... | collective-permute-start | bytes 221192 | tf_op jit(solution)/shard_map/ppermute | solution.py:242
  5.7 8.3 %collective-permute-start.2 = (bf16[72,512]{1,0:T(8,128)(2,1)S(1)}, bf16[72,512]{1,0:T(8,128)(2,1)S(1)}, u32[]{:S(2)}, u32[]{:S(2)}) collective-permute-start(bf16[72,512]{1,0:T(8,128)(2,1)S(1)} %get-tuple-element.36), channel_id=1, source_target_pairs={{0,3},{1,2},{2,1},{3,0},{4,7},{5,6},{6,5},{7,4},{8,11},{9,10},{10,... | collective-permute-start | bytes 221192 | tf_op jit(solution)/shard_map/ppermute | solution.py:242
  5.9 8.0 %collective-permute-start.3 = (bf16[72,512]{1,0:T(8,128)(2,1)S(1)}, bf16[72,512]{1,0:T(8,128)(2,1)S(1)}, u32[]{:S(2)}, u32[]{:S(2)}) collective-permute-start(bf16[72,512]{1,0:T(8,128)(2,1)S(1)} %get-tuple-element.37), channel_id=1, source_target_pairs={{0,4},{1,5},{2,6},{3,7},{4,0},{5,1},{6,2},{7,3},{8,12},{9,13},{10,... | collective-permute-start | bytes 221192 | tf_op jit(solution)/shard_map/ppermute | solution.py:242
  6.1 11.1 %collective-permute-start.4 = (bf16[72,512]{1,0:T(8,128)(2,1)S(1)}, bf16[72,512]{1,0:T(8,128)(2,1)S(1)}, u32[]{:S(2)}, u32[]{:S(2)}) collective-permute-start(bf16[72,512]{1,0:T(8,128)(2,1)S(1)} %get-tuple-element.38), channel_id=1, source_target_pairs={{0,5},{1,4},{2,7},{3,6},{4,1},{5,0},{6,3},{7,2},{8,13},{9,12},{10,... | collective-permute-start | bytes 221192 | tf_op jit(solution)/shard_map/ppermute | solution.py:242
  8.5 12.7 %collective-permute-start.5 = (bf16[72,512]{1,0:T(8,128)(2,1)S(1)}, bf16[72,512]{1,0:T(8,128)(2,1)S(1)}, u32[]{:S(2)}, u32[]{:S(2)}) collective-permute-start(bf16[72,512]{1,0:T(8,128)(2,1)S(1)} %get-tuple-element.39), channel_id=1, source_target_pairs={{0,6},{1,7},{2,4},{3,5},{4,2},{5,3},{6,0},{7,1},{8,14},{9,15},{10,... | collective-permute-start | bytes 221192 | tf_op jit(solution)/shard_map/ppermute | solution.py:242
  9.0 13.2 %collective-permute-start.6 = (bf16[72,512]{1,0:T(8,128)(2,1)S(1)}, bf16[72,512]{1,0:T(8,128)(2,1)S(1)}, u32[]{:S(2)}, u32[]{:S(2)}) collective-permute-start(bf16[72,512]{1,0:T(8,128)(2,1)S(1)} %get-tuple-element.40), channel_id=1, source_target_pairs={{0,7},{1,6},{2,5},{3,4},{4,3},{5,2},{6,1},{7,0},{8,15},{9,14},{10,... | collective-permute-start | bytes 221192 | tf_op jit(solution)/shard_map/ppermute | solution.py:242
  24.0 6.6 %collective-permute-start.7 = (bf16[144,512]{1,0:T(8,128)(2,1)S(1)}, bf16[144,512]{1,0:T(8,128)(2,1)S(1)}, u32[]{:S(2)}, u32[]{:S(2)}) collective-permute-start(bf16[144,512]{1,0:T(8,128)(2,1)S(1)} %get-tuple-element.52), channel_id=1, source_target_pairs={{0,8},{8,0},{16,24},{24,16},{1,9},{9,1},{17,25},{25,17},{2,10},{10... | collective-permute-start | bytes 442376 | tf_op jit(solution)/shard_map/ppermute | solution.py:242
  25.5 8.8 %collective-permute-start.8 = (bf16[144,512]{1,0:T(8,128)(2,1)S(1)}, bf16[144,512]{1,0:T(8,128)(2,1)S(1)}, u32[]{:S(2)}, u32[]{:S(2)}) collective-permute-start(bf16[144,512]{1,0:T(8,128)(2,1)S(1)} %get-tuple-element.53), channel_id=1, source_target_pairs={{0,16},{8,24},{16,0},{24,8},{1,17},{9,25},{17,1},{25,9},{2,18},{10... | collective-permute-start | bytes 442376 | tf_op jit(solution)/shard_map/ppermute | solution.py:242
  27.0 7.2 %collective-permute-start.9 = (bf16[144,512]{1,0:T(8,128)(2,1)S(1)}, bf16[144,512]{1,0:T(8,128)(2,1)S(1)}, u32[]{:S(2)}, u32[]{:S(2)}) collective-permute-start(bf16[144,512]{1,0:T(8,128)(2,1)S(1)} %get-tuple-element.54), channel_id=1, source_target_pairs={{0,24},{8,16},{16,8},{24,0},{1,25},{9,17},{17,9},{25,1},{2,26},{10... | collective-permute-start | bytes 442376 | tf_op jit(solution)/shard_map/ppermute | solution.py:242

commit v2 on v1

--- a/solution.py
+++ b/solution.py
@@ -30,6 +30,8 @@
 
 WIDE = up_to(rows_read(0, HALF - 1)[1] + 1, 16)
 WIDE_STEP = HALF - WIDE
+SENT = up_to(rows_read(0, HALF - 1)[1] + 1, 8)
+SENT_STEP = HALF - SENT
 
 
 def first_windows():
@@ -38,23 +40,27 @@
         low, high = rows_read(h2 * HALF, h2 * HALF + HALF - 1)
         for h1 in (0, 1):
             spans.append(rows_read(h1 * HALF + low, h1 * HALF + high))
-    rows = up_to(max(high - low + 1 for low, high in spans), 8)
-    return [min(low, HALF - rows) for low, high in spans], rows
+    rows = up_to(max(high - low + 1 + low % 2 for low, high in spans), 8)
+    return [min(low - low % 2, HALF - rows) for low, high in spans], rows
 
 
 FIRST_STARTS, FIRST = first_windows()
 FIRST_PAD = up_to(FIRST, 16)
+FIRST_SIDE = up_to(FIRST // 2, 8)
 
 
 def beam_rows(pulses):
-    pulse_ids = np.arange(pulses)
-    sectors = []
-    for sector in range(SUBS):
-        start = (sector & 1) * HALF + FIRST_STARTS[sector >> 1]
-        angle_ids = start + np.arange(FIRST)
-        phases = (angle_ids[:, None] * pulse_ids[None, :] % ANGLES) * (2.0 * math.pi / ANGLES)
-        sectors.append(np.concatenate([np.cos(phases), np.sin(phases)], axis=1))
-    return np.concatenate(sectors, axis=0).astype(ml_dtypes.bfloat16)
+    pulse_ids = np.arange(pulses // 2)
+    sides = []
+    for odd in (0, 1):
+        sectors = np.zeros((SUBS, FIRST_SIDE, pulses))
+        for sector in range(SUBS):
+            start = (sector & 1) * HALF + FIRST_STARTS[sector >> 1]
+            angle_ids = start + 2 * np.arange(FIRST // 2) + odd
+            phases = (angle_ids[:, None] * pulse_ids[None, :] % ANGLES) * (2.0 * math.pi / ANGLES)
+            sectors[sector, : FIRST // 2] = np.concatenate([np.cos(phases), np.sin(phases)], axis=1)
+        sides.append(sectors.reshape(SUBS * FIRST_SIDE, pulses))
+    return np.stack(sides).astype(ml_dtypes.bfloat16)
 
 
 def range_rows(freq_count, freq_local):
@@ -69,35 +75,51 @@
     return table.astype(ml_dtypes.bfloat16)
 
 
-def beam_kernel(pos, raw, table, *rest, pulses):
-    outs, (rhs, acc) = rest[:-2], rest[-2:]
+def beam_kernel(raw_far, table_far, *refs, pulses):
+    outs, (raw, table, rhs, acc, raw_sem, table_sem) = refs[:-6], refs[-6:]
     freqs = raw.shape[1]
-    band_pos = pos[0]
+    half = pulses // 2
+    band_pos = lax.axis_index("band")
     scale = 1.0 / math.sqrt(pulses)
+    raw_copy = pltpu.make_async_copy(raw_far, raw, raw_sem)
+    raw_copy.start()
+    table_copy = pltpu.make_async_copy(table_far, table, table_sem)
+    table_copy.start()
+    raw_copy.wait()
     for upper in range(len(outs) // SUBS):
-        block = band_pos // SUBS ^ upper
+        block = band_pos // SUBS ^ upper if len(outs) > SUBS else 0
         for t in range(SUBS):
             at = pl.multiple_of((block * SUBS + t) * pulses, pulses)
-            real = raw[0, :, pl.ds(at, pulses)]
-            imag = raw[1, :, pl.ds(at, pulses)]
             row = t * 2 * freqs
-            rhs[row : row + freqs, :pulses] = real
-            rhs[row : row + freqs, pulses:] = imag
-            rhs[row + freqs : row + 2 * freqs, :pulses] = imag
-            rhs[row + freqs : row + 2 * freqs, pulses:] = -real
-        acc[...] = lax.dot_general(
-            table[...], rhs[...], (((1,), (1,)), ((), ())), preferred_element_type=jnp.float32
-        )
+            first = raw[:, :, pl.ds(at, half)]
+            second = raw[:, :, pl.ds(at + half, half)]
+            for side, mixed in enumerate((first + second, first - second)):
+                rhs[side, row : row + freqs, :half] = mixed[0]
+                rhs[side, row : row + freqs, half:] = mixed[1]
+                rhs[side, row + freqs : row + 2 * freqs, :half] = mixed[1]
+                rhs[side, row + freqs : row + 2 * freqs, half:] = -mixed[0]
+        if upper == 0:
+            table_copy.wait()
+        for side in (0, 1):
+            acc[side] = lax.dot_general(
+                table[side],
+                rhs[side],
+                (((1,), (1,)), ((), ())),
+                preferred_element_type=jnp.float32,
+            )
         for low in range(SUBS):
             sector = (band_pos ^ low) & (SUBS - 1)
-            start = pl.multiple_of(sector * FIRST, 8)
-            outs[upper * SUBS + low][...] = (acc[pl.ds(start, FIRST), :] * scale).astype(
-                jnp.bfloat16
-            )
-
-
-def interp_t(taps, weights, start, rows):
-    row_ids = lax.broadcasted_iota(jnp.int32, (rows, ANGLES), 0) + start
+            rows = pl.ds(pl.multiple_of(sector * FIRST_SIDE, 8), FIRST // 2)
+            both = jnp.concatenate([acc[0, rows, :], acc[1, rows, :]], axis=0)
+            outs[upper * SUBS + low][...] = (both * scale).astype(jnp.bfloat16)
+
+
+def interp_t(taps, weights, start, rows, mixed=False):
+    row_ids = lax.broadcasted_iota(jnp.int32, (rows, ANGLES), 0)
+    if mixed:
+        side = FIRST // 2
+        row_ids = jnp.where(row_ids < side, 2 * row_ids, 2 * (row_ids - side) + 1)
+    row_ids += start
     total = jnp.zeros((rows, ANGLES), jnp.float32)
     for s in range(taps.shape[0]):
         total += jnp.where(row_ids == taps[s : s + 1, :], weights[s : s + 1, :], 0.0)
@@ -125,10 +147,10 @@
 
 
 def table_kernel(
-    pos, shifts, taps, weights, ranges,
+    shifts, taps, weights, ranges,
     range_out, m0, m1, m2, m3, m4, c0, s0, c1, s1, c2, s2, c3, s3, c4, s4, turned,
 ):
-    band_pos, grp_pos = pos[0], pos[1]
+    band_pos, grp_pos = lax.axis_index("band"), lax.axis_index("grp")
     h0, h1, h2 = band_pos & 1, band_pos >> 1 & 1, band_pos >> 2 & 1
     h3, h4 = grp_pos & 1, grp_pos >> 1 & 1
     count = ranges.shape[0]
@@ -144,7 +166,7 @@
     for combo in range(1, len(FIRST_STARTS)):
         first_start = jnp.where(h1 + 2 * h2 == combo, FIRST_STARTS[combo], first_start)
     wide1 = pl.multiple_of(h1 * HALF + h2 * WIDE_STEP, 16)
-    sum_rows = interp_t(taps[0, h0], weights[0, h0], first_start, FIRST_PAD)
+    sum_rows = interp_t(taps[0, h0], weights[0, h0], first_start, FIRST_PAD, True)
     turned[:, :FIRST_PAD] = sum_rows.T
     window = turned[pl.ds(wide1, WIDE), :FIRST_PAD].astype(jnp.bfloat16)
     m0[:WIDE, :FIRST_PAD] = window
@@ -160,13 +182,12 @@
     turned[...] = interp_t(taps[2, h2], weights[2, h2], 0, HALF).T
     for k in range(MATES):
         mate = grp_pos ^ k
-        at = pl.multiple_of((mate & 1) * HALF + (mate >> 1 & 1) * WIDE_STEP, 16)
-        m2[k * WIDE : (k + 1) * WIDE, :] = turned[pl.ds(at, WIDE), :].astype(jnp.bfloat16)
-        rows = pl.ds(k * WIDE, WIDE)
-        phase_rows(c2.at[rows], s2.at[rows], shifts[2], h2 * ANGLES + at, WIDE, 1.0)
+        at = pl.multiple_of((mate & 1) * HALF + (mate >> 1 & 1) * SENT_STEP, 8)
+        m2[k] = turned[pl.ds(at, SENT), :].astype(jnp.bfloat16)
+        phase_rows(c2.at[k], s2.at[k], shifts[2], h2 * ANGLES + at, SENT, 1.0)
 
     half4 = pl.multiple_of(h4 * HALF, HALF)
-    fill(m3, 3, h3, h4 * WIDE_STEP, WIDE, half4, HALF)
+    fill(m3, 3, h3, h4 * SENT_STEP, SENT, half4, HALF)
     sign3 = (1 - 2 * h3).astype(jnp.float32)
     phase_rows(c3, s3, shifts[3], h3 * ANGLES + half4, HALF, sign3)
     fill(m4, 4, h4, 0, HALF, 0, ANGLES)
@@ -174,6 +195,10 @@
     phase_rows(c4, s4, shifts[4], h4 * ANGLES, ANGLES, sign4)
 
 
+def send_order(count):
+    return [7, 6, 5, 3, 4, 2, 1, 0] if count == SUBS else list(range(count - 1, -1, -1))
+
+
 def dot(left, right):
     return jnp.dot(left, right, preferred_element_type=jnp.float32)
 
@@ -185,7 +210,8 @@
 
 
 def band_kernel(*refs, sources):
-    blocks = refs[:sources]
+    order = send_order(sources)
+    blocks = [refs[order.index(k)] for k in range(sources)]
     ranges, m0, m1, m2, c0, s0, c1, s1, c2, s2 = refs[sources : sources + 10]
     outs = refs[sources + 10 : sources + 10 + MATES]
     wide, sub0, sub1, sub2 = refs[sources + 10 + MATES :]
@@ -212,29 +238,48 @@
         rows = slice(p * HALF, (p + 1) * HALF)
         turn(sub2, rows, low + high, low - high, c1[...], s1[...])
     for k in range(MATES):
-        rows = slice(k * WIDE, (k + 1) * WIDE)
-        low = dot(m2[rows, :], sub2[:HALF, :])
-        high = dot(m2[rows, :], sub2[HALF:, :])
-        turn(outs[k], slice(None), low + high, low - high, c2[rows, :], s2[rows, :])
-
-
-def grp_kernel(own, along, across, both, m3, m4, c3, s3, c4, s4, out, sub4):
+        low = dot(m2[k], sub2[:HALF, :])
+        high = dot(m2[k], sub2[HALF:, :])
+        turn(outs[k], slice(None), low + high, low - high, c2[k], s2[k])
+
+
+def own_kernel(along, own, m3, m4, c3, s3, part, sub4):
+    low = dot(m3[...], own[...])
+    high = dot(m3[...], along[...])
+    turn(sub4, slice(None), low + high, low - high, c3[...], s3[...])
+    part[...] = dot(m4[...], sub4[...])
+
+
+def grp_kernel(across, both, part, m3, m4, c3, s3, c4, s4, out_far, sub4, out, sems):
     freqs = c3.shape[1]
-    for q, (mine, other) in enumerate(((own, along), (across, both))):
-        low = dot(m3[...], mine[...])
-        high = dot(m3[...], other[...])
-        turn(sub4, slice(q * HALF, (q + 1) * HALF), low + high, low - high, c3[...], s3[...])
-    low = dot(m4[...], sub4[:HALF, :])
-    high = dot(m4[...], sub4[HALF:, :])
-    total, diff = low + high, low - high
-    cosine, sine = c4[...], s4[...]
-    out[0] = (cosine * total[:, :freqs] - sine * diff[:, freqs:]).astype(out.dtype)
-    out[1] = (cosine * total[:, freqs:] + sine * diff[:, :freqs]).astype(out.dtype)
+    low = dot(m3[...], across[...])
+    high = dot(m3[...], both[...])
+    turn(sub4, slice(None), low + high, low - high, c3[...], s3[...])
+    pieces = sems.shape[0]
+    count = out.shape[1] // pieces
+    copies = []
+    for piece in range(pieces):
+        rows = slice(piece * count, (piece + 1) * count)
+        low = part[rows, :]
+        high = dot(m4[rows, :], sub4[...])
+        total, diff = low + high, low - high
+        cosine, sine = c4[rows, :], s4[rows, :]
+        out[0, rows, :] = (cosine * total[:, :freqs] - sine * diff[:, freqs:]).astype(out.dtype)
+        out[1, rows, :] = (cosine * total[:, freqs:] + sine * diff[:, :freqs]).astype(out.dtype)
+        copy = pltpu.make_async_copy(
+            out.at[:, rows, :], out_far.at[:, rows, :], sems.at[piece]
+        )
+        copy.start()
+        copies.append(copy)
+    for copy in copies:
+        copy.wait()
 
 
 VMEM = pl.BlockSpec(memory_space=pltpu.VMEM)
+FAR = pl.BlockSpec(memory_space=pltpu.HBM)
 SMEM = pl.BlockSpec(memory_space=pltpu.SMEM)
 PARAMS = pltpu.CompilerParams(vmem_limit_bytes=48 * 1024 * 1024)
+BEAM_PARAMS = pltpu.CompilerParams(vmem_limit_bytes=55687168)
 
 
 def swapped(block, axis, mask):
@@ -249,24 +294,28 @@
     pulses = raw.shape[2] // n_band
     bf16, f32 = jnp.bfloat16, jnp.float32
     shape = jax.ShapeDtypeStruct
-    pos = jnp.stack([lax.axis_index("band"), lax.axis_index("grp")]).astype(jnp.int32)
     lanes = SUBS * 2 * freqs
 
+    table = jnp.asarray(beam_rows(pulses))
     beams = pl.pallas_call(
         functools.partial(beam_kernel, pulses=pulses),
         out_shape=[shape((FIRST, lanes), bf16)] * n_band,
-        in_specs=[SMEM, VMEM, VMEM],
+        in_specs=[FAR, FAR],
         out_specs=[VMEM] * n_band,
         scratch_shapes=[
-            pltpu.VMEM((lanes, 2 * pulses), bf16),
-            pltpu.VMEM((SUBS * FIRST, lanes), f32),
+            pltpu.VMEM(raw.shape, bf16),
+            pltpu.VMEM(table.shape, bf16),
+            pltpu.VMEM((2, lanes, pulses), bf16),
+            pltpu.VMEM((2, SUBS * FIRST_SIDE, lanes), f32),
+            pltpu.SemaphoreType.DMA,
+            pltpu.SemaphoreType.DMA,
         ],
-        compiler_params=PARAMS,
+        compiler_params=BEAM_PARAMS,
         cost_estimate=pl.CostEstimate(
-            flops=2 * SUBS * FIRST * 2 * pulses * lanes, bytes_accessed=1 << 21, transcendentals=0
+            flops=2 * SUBS * FIRST * pulses * lanes, bytes_accessed=1 << 21, transcendentals=0
         ),
         name="beam",
-    )(pos, raw, jnp.asarray(beam_rows(pulses)))
+    )(raw, table)
 
     wide2 = 2 * freq_count
     tables = pl.pallas_call(
@@ -275,16 +324,16 @@
             shape((wide2, wide2), bf16),
             shape((2 * WIDE, 2 * FIRST_PAD), bf16),
             shape((HALF, WIDE), bf16),
-            shape((MATES * WIDE, HALF), bf16),
-            shape((HALF, WIDE), bf16),
+            shape((MATES, SENT, HALF), bf16),
+            shape((HALF, SENT), bf16),
             shape((ANGLES, HALF), bf16),
         ]
         + [
-            shape((rows, freq_count), f32)
-            for rows in (WIDE, HALF, MATES * WIDE, HALF, ANGLES)
+            shape(rows + (freq_count,), f32)
+            for rows in ((WIDE,), (HALF,), (MATES, SENT), (HALF,), (ANGLES,))
             for _ in range(2)
         ],
-        in_specs=[SMEM, SMEM, VMEM, VMEM, VMEM],
+        in_specs=[SMEM, VMEM, VMEM, VMEM],
         out_specs=[VMEM] * 16,
         scratch_shapes=[pltpu.VMEM((ANGLES, HALF), f32)],
         compiler_params=PARAMS,
@@ -292,13 +341,13 @@
             flops=1 << 24, bytes_accessed=1 << 23, transcendentals=1 << 18
         ),
         name="tables",
-    )(pos, shifts, taps, weights, jnp.asarray(range_rows(freq_count, freqs)))
+    )(shifts, taps, weights, jnp.asarray(range_rows(freq_count, freqs)))
     ranges, m0, m1, m2, m3, m4, c0, s0, c1, s1, c2, s2, c3, s3, c4, s4 = tables
 
-    blocks = [beams[0]] + [swapped(beams[k], "band", k) for k in range(1, n_band)]
+    blocks = [swapped(beams[k], "band", k) if k else beams[k] for k in send_order(n_band)]
     pieces = pl.pallas_call(
         functools.partial(band_kernel, sources=n_band),
-        out_shape=[shape((WIDE, wide2), bf16)] * MATES,
+        out_shape=[shape((SENT, wide2), bf16)] * MATES,
         in_specs=[VMEM] * (n_band + 10),
         out_specs=[VMEM] * MATES,
         scratch_shapes=[
@@ -312,17 +361,32 @@
         name="band_merges",
     )(*blocks, ranges, m0, m1, m2, c0, s0, c1, s1, c2, s2)
 
-    halves = [pieces[0]] + [swapped(pieces[k], "grp", k) for k in range(1, MATES)]
+    halves = [swapped(pieces[k], "grp", k) for k in range(1, MATES)] + [pieces[0]]
+    along, across, both, own = halves
+    part = pl.pallas_call(
+        own_kernel,
+        out_shape=shape((ANGLES, wide2), f32),
+        in_specs=[VMEM] * 6,
+        out_specs=VMEM,
+        scratch_shapes=[pltpu.VMEM((HALF, wide2), bf16)],
+        compiler_params=PARAMS,
+        cost_estimate=pl.CostEstimate(flops=1 << 29, bytes_accessed=1 << 21, transcendentals=0),
+        name="own_merge",
+    )(along, own, m3, m4, c3, s3)
     return pl.pallas_call(
         grp_kernel,
         out_shape=shape((2, ANGLES, freq_count), bf16),
-        in_specs=[VMEM] * 10,
-        out_specs=VMEM,
-        scratch_shapes=[pltpu.VMEM((2 * HALF, wide2), bf16)],
+        in_specs=[VMEM] * 9,
+        out_specs=FAR,
+        scratch_shapes=[
+            pltpu.VMEM((HALF, wide2), bf16),
+            pltpu.VMEM((2, ANGLES, freq_count), bf16),
+            pltpu.SemaphoreType.DMA((4,)),
+        ],
         compiler_params=PARAMS,
-        cost_estimate=pl.CostEstimate(flops=1 << 30, bytes_accessed=1 << 22, transcendentals=0),
+        cost_estimate=pl.CostEstimate(flops=1 << 29, bytes_accessed=1 << 21, transcendentals=0),
         name="grp_merges",
-    )(*halves, m3, m4, c3, s3, c4, s4)
+    )(across, both, part, m3, m4, c3, s3, c4, s4)
 
 
 def solution(mesh):

time: 36.1 us -> 33.4 us (0.925)
  the two profiles are of different devices: /device:TPU:16 before, /device:TPU:0 now
where the time goes in v2:
time: 33.4 us; the launch traced here: 33.2 us
  starting transfers between devices  13.4 us (40%)
  waiting for transfers between devices  10.4 us (31%)
  Pallas kernels  9.36 us (28%)
    ppermute x10, starting transfers between devices, swapped(): lax.ppermute(block, axis, [(low, low ^ mask) for low in range(count)])  13.4 us
    ppermute x10, waiting for transfers between devices, swapped(): lax.ppermute(block, axis, [(low, low ^ mask) for low in range(count)])  10.4 us
    pallas_call x1, Pallas kernels, on_device(): pl.pallas_call(table_kernel, out_shape=[shape((wide2, wide2), bf16), shap...  3.57 us
    pallas_call x1, Pallas kernels, on_device(): pl.pallas_call(functools.partial(beam_kernel, pulses=pulses), out_shape=[...  2.02 us
    pallas_call x1, Pallas kernels, on_device(): pl.pallas_call(functools.partial(band_kernel, sources=n_band), out_shape=...  1.84 us
    pallas_call x1, Pallas kernels, on_device(): pl.pallas_call(grp_kernel, out_shape=shape((2, ANGLES, freq_count), bf16)...  1.35 us
  transfers between devices with their start and end apart: 10, of which 5 were waited for; matrix products, arithmetic and copies ran while one was open for 0% of the time, Pallas kernels for 12%

profile of v2, /device:TPU:0, one launch (start us, length us, event | category | flops | bytes accessed | tf_op | source)
XLA Modules:
  0.0 33.2 jit_solution(16791721935512706048)
XLA Ops:
  0.0 2.0 %beam.1 = (bf16[72,512]{1,0:T(8,128)(2,1)S(1)}, bf16[72,512]{1,0:T(8,128)(2,1)S(1)}, bf16[72,512]{1,0:T(8,128)(2,1)S(1)}, bf16[72,512]{1,0:T(8,128)(2,1)S(1)}, b...) custom-call(bf16[2,32,4096]{2,1,0:T(8,128)(2,1)} %raw_far.1, ...), custom_call_target="tpu_custom_call" | custom-call | flops 301989888 | bytes 2097152 | tf_op jit(solution)/shard_map/beam/pallas_call | solution.py:300
  2.0 4.6 %collective-permute-start = (bf16[72,512]{1,0:T(8,128)(2,1)S(1)}, bf16[72,512]{1,0:T(8,128)(2,1)S(1)}, u32[]{:S(2)}, u32[]{:S(2)}) collective-permute-start(bf16[72,512]{1,0:T(8,128)(2,1)S(1)} %get-tuple-element.33), channel_id=1, source_target_pairs={{0,7},{1,6},{2,5},{3,4},{4,3},{5,2},{6,1},{7,0},{8,15},{9,14},{10,... | collective-permute-start | bytes 221192 | tf_op jit(solution)/shard_map/ppermute | solution.py:287
  6.6 0.6 %collective-permute-start.1 = (bf16[72,512]{1,0:T(8,128)(2,1)S(1)}, bf16[72,512]{1,0:T(8,128)(2,1)S(1)}, u32[]{:S(2)}, u32[]{:S(2)}) collective-permute-start(bf16[72,512]{1,0:T(8,128)(2,1)S(1)} %get-tuple-element.34), channel_id=1, source_target_pairs={{0,6},{1,7},{2,4},{3,5},{4,2},{5,3},{6,0},{7,1},{8,14},{9,15},{10,... | collective-permute-start | bytes 221192 | tf_op jit(solution)/shard_map/ppermute | solution.py:287
  7.2 0.4 %collective-permute-start.2 = (bf16[72,512]{1,0:T(8,128)(2,1)S(1)}, bf16[72,512]{1,0:T(8,128)(2,1)S(1)}, u32[]{:S(2)}, u32[]{:S(2)}) collective-permute-start(bf16[72,512]{1,0:T(8,128)(2,1)S(1)} %get-tuple-element.35), channel_id=1, source_target_pairs={{0,5},{1,4},{2,7},{3,6},{4,1},{5,0},{6,3},{7,2},{8,13},{9,12},{10,... | collective-permute-start | bytes 221192 | tf_op jit(solution)/shard_map/ppermute | solution.py:287
  7.6 3.1 %collective-permute-start.3 = (bf16[72,512]{1,0:T(8,128)(2,1)S(1)}, bf16[72,512]{1,0:T(8,128)(2,1)S(1)}, u32[]{:S(2)}, u32[]{:S(2)}) collective-permute-start(bf16[72,512]{1,0:T(8,128)(2,1)S(1)} %get-tuple-element.36), channel_id=1, source_target_pairs={{0,3},{1,2},{2,1},{3,0},{4,7},{5,6},{6,5},{7,4},{8,11},{9,10},{10,... | collective-permute-start | bytes 221192 | tf_op jit(solution)/shard_map/ppermute | solution.py:287
  10.7 0.2 collective-permute-start.4
  11.0 0.0 collective-permute-done.refs_0_
  11.0 0.9 %collective-permute-start.5 = (bf16[72,512]{1,0:T(8,128)(2,1)S(1)}, bf16[72,512]{1,0:T(8,128)(2,1)S(1)}, u32[]{:S(2)}, u32[]{:S(2)}) collective-permute-start(bf16[72,512]{1,0:T(8,128)(2,1)S(1)} %get-tuple-element.38), channel_id=1, source_target_pairs={{0,2},{1,3},{2,0},{3,1},{4,6},{5,7},{6,4},{7,5},{8,10},{9,11},{10,... | collective-permute-start | bytes 221192 | tf_op jit(solution)/shard_map/ppermute | solution.py:287
  11.9 1.7 %collective-permute-done.1.refs_1_ = bf16[72,512]{1,0:T(8,128)(2,1)S(1)} collective-permute-done((bf16[72,512]{1,0:T(8,128)(2,1)S(1)}, bf16[72,512]{1,0:T(8,128)(2,1)S(1)}, u32[]{:S(2)}, u32[]{:S(2)}) %collective-permute-start.1) | collective-permute-done | bytes 73760 | tf_op jit(solution)/shard_map/ppermute | solution.py:287
  13.6 0.0 collective-permute-start.6
  13.7 3.6 %tables.1 = (bf16[512,512]{1,0:T(8,128)(2,1)S(1)}, bf16[288,160]{1,0:T(8,128)(2,1)S(1)}, bf16[256,144]{1,0:T(8,128)(2,1)S(1)}, bf16[4,136,256]{2,1,0:T(8,128)(2,...) custom-call(f32[5]{0:T(128)S(1)} %copy-done.3, ...), custom_call_target="tpu_custom_call" | custom-call | flops 16777216 | bytes 8388608 | tf_op jit(solution)/shard_map/tables/pallas_call | solution.py:321
  17.2 1.2 %collective-permute-done.2.refs_2_ = bf16[72,512]{1,0:T(8,128)(2,1)S(1)} collective-permute-done((bf16[72,512]{1,0:T(8,128)(2,1)S(1)}, bf16[72,512]{1,0:T(8,128)(2,1)S(1)}, u32[]{:S(2)}, u32[]{:S(2)}) %collective-permute-start.2) | collective-permute-done | bytes 73760 | tf_op jit(solution)/shard_map/ppermute | solution.py:287
  18.5 0.0 collective-permute-done.3.refs_3_
  18.5 1.7 %collective-permute-done.4.refs_4_ = bf16[72,512]{1,0:T(8,128)(2,1)S(1)} collective-permute-done((bf16[72,512]{1,0:T(8,128)(2,1)S(1)}, bf16[72,512]{1,0:T(8,128)(2,1)S(1)}, u32[]{:S(2)}, u32[]{:S(2)}) %collective-permute-start.4) | collective-permute-done | bytes 73760 | tf_op jit(solution)/shard_map/ppermute | solution.py:287
  20.2 0.0 collective-permute-done.5.refs_5_
  20.2 0.0 collective-permute-done.6.refs_6_
  20.2 1.8 %band_merges.1 = (bf16[136,512]{1,0:T(8,128)(2,1)S(1)}, bf16[136,512]{1,0:T(8,128)(2,1)S(1)}, bf16[136,512]{1,0:T(8,128)(2,1)S(1)}, bf16[136,512]{1,0:T(8,128)(2,1)S(1)}) custom-call(bf16[72,512]{1,0:T(8,128)(2,1)S(1)} %collective-permute-done.refs_0_, bf16[72,512]{1,0:T(8,128)(2,1)S(1)} %collective-permute-done.1.refs_1_, ...), custom_call_target="tpu_custom_call" | custom-call | flops 2147483648 | bytes 4194304 | tf_op jit(solution)/shard_map/band_merges/pallas_call | solution.py:348
  22.0 1.6 %collective-permute-start.9 = (bf16[136,512]{1,0:T(8,128)(2,1)S(1)}, bf16[136,512]{1,0:T(8,128)(2,1)S(1)}, u32[]{:S(2)}, u32[]{:S(2)}) collective-permute-start(bf16[136,512]{1,0:T(8,128)(2,1)S(1)} %get-tuple-element.53), channel_id=1, source_target_pairs={{0,8},{8,0},{16,24},{24,16},{1,9},{9,1},{17,25},{25,17},{2,10},{10... | collective-permute-start | bytes 417800 | tf_op jit(solution)/shard_map/ppermute | solution.py:287
  23.6 1.5 %collective-permute-start.7 = (bf16[136,512]{1,0:T(8,128)(2,1)S(1)}, bf16[136,512]{1,0:T(8,128)(2,1)S(1)}, u32[]{:S(2)}, u32[]{:S(2)}) collective-permute-start(bf16[136,512]{1,0:T(8,128)(2,1)S(1)} %get-tuple-element.51), channel_id=1, source_target_pairs={{0,16},{8,24},{16,0},{24,8},{1,17},{9,25},{17,1},{25,9},{2,18},{10... | collective-permute-start | bytes 417800 | tf_op jit(solution)/shard_map/ppermute | solution.py:287
  25.1 0.5 %collective-permute-start.8 = (bf16[136,512]{1,0:T(8,128)(2,1)S(1)}, bf16[136,512]{1,0:T(8,128)(2,1)S(1)}, u32[]{:S(2)}, u32[]{:S(2)}) collective-permute-start(bf16[136,512]{1,0:T(8,128)(2,1)S(1)} %get-tuple-element.52), channel_id=1, source_target_pairs={{0,24},{8,16},{16,8},{24,0},{1,25},{9,17},{17,9},{25,1},{2,26},{10... | collective-permute-start | bytes 417800 | tf_op jit(solution)/shard_map/ppermute | solution.py:287
  25.6 2.6 %collective-permute-done.9.along = bf16[136,512]{1,0:T(8,128)(2,1)S(1)} collective-permute-done((bf16[136,512]{1,0:T(8,128)(2,1)S(1)}, bf16[136,512]{1,0:T(8,128)(2,1)S(1)}, u32[]{:S(2)}, u32[]{:S(2)}) %collective-permute-start.9) | collective-permute-done | bytes 139296 | tf_op jit(solution)/shard_map/ppermute | solution.py:287
  28.2 0.6 %own_merge.1.part = f32[512,512]{1,0:T(8,128)S(1)} custom-call(bf16[136,512]{1,0:T(8,128)(2,1)S(1)} %collective-permute-done.9.along, bf16[136,512]{1,0:T(8,128)(2,1)S(1)} %get-tuple-element.54.own, bf16[256,136]{1,0:T(8,128)(2,1)S(1)} %get-tuple-element.55.m3, bf16[512,256]{1,0:T(8,128)(2,1)S(1)} %get-tuple-element.56.m4, ...), custom_call_target="tpu_custom_call" | custom-call | flops 536870912 | bytes 2097152 | tf_op jit(solution)/shard_map/own_merge/pallas_call | solution.py:366
  28.8 3.1 %collective-permute-done.7.across = bf16[136,512]{1,0:T(8,128)(2,1)S(1)} collective-permute-done((bf16[136,512]{1,0:T(8,128)(2,1)S(1)}, bf16[136,512]{1,0:T(8,128)(2,1)S(1)}, u32[]{:S(2)}, u32[]{:S(2)}) %collective-permute-start.7) | collective-permute-done | bytes 139296 | tf_op jit(solution)/shard_map/ppermute | solution.py:287
  31.9 1.4 %grp_merges.1 = bf16[2,512,256]{2,1,0:T(8,128)(2,1)} custom-call(bf16[136,512]{1,0:T(8,128)(2,1)S(1)} %collective-permute-done.7.across, bf16[136,512]{1,0:T(8,128)(2,1)S(1)} %collective-permute-done.8.both, f32[512,512]{1,0:T(8,128)S(1)} %own_merge.1.part, bf16[256,136]{1,0:T(8,128)(2,1)S(1)} %get-tuple-element.55.m3, ...), custom_call_target="tpu_custom_call" | custom-call | flops 536870912 | bytes 2097152 | tf_op jit(solution)/shard_map/grp_merges/pallas_call | solution.py:376
  (9 shorter events, 0.0 us)
Async XLA Ops:
  0.0 13.6 %copy-start = (bf16[8,64,512]{2,1,0:T(8,128)(2,1)S(1)}, bf16[8,64,512]{2,1,0:T(8,128)(2,1)}, u32[]{:S(2)}) copy-start(bf16[8,64,512]{2,1,0:T(8,128)(2,1)} %constant.5.clone.ranges) | copy-start | bytes 1572868
  0.0 13.6 %copy-start.2 = (f32[5,2,4,512]{3,2,1,0:T(4,128)S(1)}, f32[5,2,4,512]{3,2,1,0:T(4,128)}, u32[]{:S(2)}) copy-start(f32[5,2,4,512]{3,2,1,0:T(4,128)} %weights.1) | copy-start | bytes 245764
  0.0 13.6 %copy-start.1 = (s32[5,2,4,512]{3,2,1,0:T(4,128)S(1)}, s32[5,2,4,512]{3,2,1,0:T(4,128)}, u32[]{:S(2)}) copy-start(s32[5,2,4,512]{3,2,1,0:T(4,128)} %taps.1) | copy-start | bytes 245764
  2.0 8.9 %collective-permute-start = (bf16[72,512]{1,0:T(8,128)(2,1)S(1)}, bf16[72,512]{1,0:T(8,128)(2,1)S(1)}, u32[]{:S(2)}, u32[]{:S(2)}) collective-permute-start(bf16[72,512]{1,0:T(8,128)(2,1)S(1)} %get-tuple-element.33), channel_id=1, source_target_pairs={{0,7},{1,6},{2,5},{3,4},{4,3},{5,2},{6,1},{7,0},{8,15},{9,14},{10,... | collective-permute-start | bytes 221192 | tf_op jit(solution)/shard_map/ppermute | solution.py:287
  6.6 7.0 %collective-permute-start.1 = (bf16[72,512]{1,0:T(8,128)(2,1)S(1)}, bf16[72,512]{1,0:T(8,128)(2,1)S(1)}, u32[]{:S(2)}, u32[]{:S(2)}) collective-permute-start(bf16[72,512]{1,0:T(8,128)(2,1)S(1)} %get-tuple-element.34), channel_id=1, source_target_pairs={{0,6},{1,7},{2,4},{3,5},{4,2},{5,3},{6,0},{7,1},{8,14},{9,15},{10,... | collective-permute-start | bytes 221192 | tf_op jit(solution)/shard_map/ppermute | solution.py:287
  7.2 11.3 %collective-permute-start.2 = (bf16[72,512]{1,0:T(8,128)(2,1)S(1)}, bf16[72,512]{1,0:T(8,128)(2,1)S(1)}, u32[]{:S(2)}, u32[]{:S(2)}) collective-permute-start(bf16[72,512]{1,0:T(8,128)(2,1)S(1)} %get-tuple-element.35), channel_id=1, source_target_pairs={{0,5},{1,4},{2,7},{3,6},{4,1},{5,0},{6,3},{7,2},{8,13},{9,12},{10,... | collective-permute-start | bytes 221192 | tf_op jit(solution)/shard_map/ppermute | solution.py:287
  7.6 10.8 %collective-permute-start.3 = (bf16[72,512]{1,0:T(8,128)(2,1)S(1)}, bf16[72,512]{1,0:T(8,128)(2,1)S(1)}, u32[]{:S(2)}, u32[]{:S(2)}) collective-permute-start(bf16[72,512]{1,0:T(8,128)(2,1)S(1)} %get-tuple-element.36), channel_id=1, source_target_pairs={{0,3},{1,2},{2,1},{3,0},{4,7},{5,6},{6,5},{7,4},{8,11},{9,10},{10,... | collective-permute-start | bytes 221192 | tf_op jit(solution)/shard_map/ppermute | solution.py:287
  10.7 9.5 %collective-permute-start.4 = (bf16[72,512]{1,0:T(8,128)(2,1)S(1)}, bf16[72,512]{1,0:T(8,128)(2,1)S(1)}, u32[]{:S(2)}, u32[]{:S(2)}) collective-permute-start(bf16[72,512]{1,0:T(8,128)(2,1)S(1)} %get-tuple-element.37), channel_id=1, source_target_pairs={{0,4},{1,5},{2,6},{3,7},{4,0},{5,1},{6,2},{7,3},{8,12},{9,13},{10,... | collective-permute-start | bytes 221192 | tf_op jit(solution)/shard_map/ppermute | solution.py:287
  11.0 2.7 %copy-start.3 = (f32[5]{0:T(128)S(1)}, f32[5]{0:T(128)}, u32[]{:S(2)}) copy-start(f32[5]{0:T(128)} %shifts.1) | copy-start | bytes 64
  11.0 9.2 %collective-permute-start.5 = (bf16[72,512]{1,0:T(8,128)(2,1)S(1)}, bf16[72,512]{1,0:T(8,128)(2,1)S(1)}, u32[]{:S(2)}, u32[]{:S(2)}) collective-permute-start(bf16[72,512]{1,0:T(8,128)(2,1)S(1)} %get-tuple-element.38), channel_id=1, source_target_pairs={{0,2},{1,3},{2,0},{3,1},{4,6},{5,7},{6,4},{7,5},{8,10},{9,11},{10,... | collective-permute-start | bytes 221192 | tf_op jit(solution)/shard_map/ppermute | solution.py:287
  13.6 6.6 %collective-permute-start.6 = (bf16[72,512]{1,0:T(8,128)(2,1)S(1)}, bf16[72,512]{1,0:T(8,128)(2,1)S(1)}, u32[]{:S(2)}, u32[]{:S(2)}) collective-permute-start(bf16[72,512]{1,0:T(8,128)(2,1)S(1)} %get-tuple-element.39), channel_id=1, source_target_pairs={{0,1},{1,0},{2,3},{3,2},{4,5},{5,4},{6,7},{7,6},{8,9},{9,8},{10,11... | collective-permute-start | bytes 221192 | tf_op jit(solution)/shard_map/ppermute | solution.py:287
  22.0 6.1 %collective-permute-start.9 = (bf16[136,512]{1,0:T(8,128)(2,1)S(1)}, bf16[136,512]{1,0:T(8,128)(2,1)S(1)}, u32[]{:S(2)}, u32[]{:S(2)}) collective-permute-start(bf16[136,512]{1,0:T(8,128)(2,1)S(1)} %get-tuple-element.53), channel_id=1, source_target_pairs={{0,8},{8,0},{16,24},{24,16},{1,9},{9,1},{17,25},{25,17},{2,10},{10... | collective-permute-start | bytes 417800 | tf_op jit(solution)/shard_map/ppermute | solution.py:287
  23.6 8.3 %collective-permute-start.7 = (bf16[136,512]{1,0:T(8,128)(2,1)S(1)}, bf16[136,512]{1,0:T(8,128)(2,1)S(1)}, u32[]{:S(2)}, u32[]{:S(2)}) collective-permute-start(bf16[136,512]{1,0:T(8,128)(2,1)S(1)} %get-tuple-element.51), channel_id=1, source_target_pairs={{0,16},{8,24},{16,0},{24,8},{1,17},{9,25},{17,1},{25,9},{2,18},{10... | collective-permute-start | bytes 417800 | tf_op jit(solution)/shard_map/ppermute | solution.py:287
  25.1 6.8 %collective-permute-start.8 = (bf16[136,512]{1,0:T(8,128)(2,1)S(1)}, bf16[136,512]{1,0:T(8,128)(2,1)S(1)}, u32[]{:S(2)}, u32[]{:S(2)}) collective-permute-start(bf16[136,512]{1,0:T(8,128)(2,1)S(1)} %get-tuple-element.52), channel_id=1, source_target_pairs={{0,24},{8,16},{16,8},{24,0},{1,25},{9,17},{17,9},{25,1},{2,26},{10... | collective-permute-start | bytes 417800 | tf_op jit(solution)/shard_map/ppermute | solution.py:287

commit v3 on v2

--- a/solution.py
+++ b/solution.py
@@ -40,13 +40,17 @@
         low, high = rows_read(h2 * HALF, h2 * HALF + HALF - 1)
         for h1 in (0, 1):
             spans.append(rows_read(h1 * HALF + low, h1 * HALF + high))
-    rows = up_to(max(high - low + 1 + low % 2 for low, high in spans), 8)
+    rows = up_to(max(high - low + 1 + low % 2 for low, high in spans), 2)
     return [min(low - low % 2, HALF - rows) for low, high in spans], rows
 
 
 FIRST_STARTS, FIRST = first_windows()
-FIRST_PAD = up_to(FIRST, 16)
 FIRST_SIDE = up_to(FIRST // 2, 8)
+MAIN_SIDE = FIRST // 32 * 16
+MAIN = 2 * MAIN_SIDE
+TAIL_SIDE = FIRST // 2 - MAIN_SIDE
+TAIL = 2 * TAIL_SIDE
+TAIL_PAD = up_to(TAIL, 8)
 
 
 def beam_rows(pulses):
@@ -109,16 +113,31 @@
             )
         for low in range(SUBS):
             sector = (band_pos ^ low) & (SUBS - 1)
-            rows = pl.ds(pl.multiple_of(sector * FIRST_SIDE, 8), FIRST // 2)
-            both = jnp.concatenate([acc[0, rows, :], acc[1, rows, :]], axis=0)
-            outs[upper * SUBS + low][...] = (both * scale).astype(jnp.bfloat16)
+            rows = pl.ds(pl.multiple_of(sector * FIRST_SIDE, 8), FIRST_SIDE)
+            even, odd = acc[0, rows, :] * scale, acc[1, rows, :] * scale
+            out = outs[upper * SUBS + low]
+            width = out.shape[1]
+            pieces = even.shape[1] // width
+            tails = []
+            for piece in range(pieces):
+                lanes = slice(piece * width, (piece + 1) * width)
+                at = piece * MAIN
+                out[at : at + MAIN_SIDE, :] = even[:MAIN_SIDE, lanes].astype(out.dtype)
+                out[at + MAIN_SIDE : at + MAIN, :] = odd[:MAIN_SIDE, lanes].astype(out.dtype)
+                for side in (even, odd):
+                    tails.append(side[MAIN_SIDE : MAIN_SIDE + TAIL_SIDE, lanes])
+            out[pieces * MAIN :, :] = jnp.concatenate(tails, axis=0).astype(out.dtype)
 
 
 def interp_t(taps, weights, start, rows, mixed=False):
     row_ids = lax.broadcasted_iota(jnp.int32, (rows, ANGLES), 0)
     if mixed:
-        side = FIRST // 2
-        row_ids = jnp.where(row_ids < side, 2 * row_ids, 2 * (row_ids - side) + 1)
+        ids = row_ids - MAIN
+        tail = jnp.where(ids < TAIL_SIDE, 2 * ids, 2 * (ids - TAIL_SIDE) + 1) + MAIN
+        ids = row_ids - MAIN_SIDE
+        main = jnp.where(ids < 0, 2 * row_ids, 2 * ids + 1)
+        row_ids = jnp.where(row_ids < MAIN, main, tail)
+        row_ids = jnp.where(row_ids < FIRST, row_ids, -ANGLES)
     row_ids += start
     total = jnp.zeros((rows, ANGLES), jnp.float32)
     for s in range(taps.shape[0]):
@@ -166,13 +185,15 @@
     for combo in range(1, len(FIRST_STARTS)):
         first_start = jnp.where(h1 + 2 * h2 == combo, FIRST_STARTS[combo], first_start)
     wide1 = pl.multiple_of(h1 * HALF + h2 * WIDE_STEP, 16)
-    sum_rows = interp_t(taps[0, h0], weights[0, h0], first_start, FIRST_PAD, True)
-    turned[:, :FIRST_PAD] = sum_rows.T
-    window = turned[pl.ds(wide1, WIDE), :FIRST_PAD].astype(jnp.bfloat16)
-    m0[:WIDE, :FIRST_PAD] = window
-    m0[:WIDE, FIRST_PAD:] = window
-    m0[WIDE:, :FIRST_PAD] = window
-    m0[WIDE:, FIRST_PAD:] = -window
+    rows = MAIN + TAIL_PAD
+    turned[:, :rows] = interp_t(taps[0, h0], weights[0, h0], first_start, rows, True).T
+    window = turned[pl.ds(wide1, WIDE), :rows].astype(jnp.bfloat16)
+    main, tail = window[:, :MAIN], window[:, MAIN:]
+    for at, sign in ((0, 1), (WIDE, -1)):
+        m0[at : at + WIDE, :MAIN] = main
+        m0[at : at + WIDE, MAIN : 2 * MAIN] = sign * main
+        m0[at : at + WIDE, 2 * MAIN : 2 * MAIN + TAIL_PAD] = tail
+        m0[at : at + WIDE, 2 * MAIN + TAIL_PAD :] = sign * tail
     phase_rows(c0, s0, shifts[0], h0 * ANGLES + wide1, WIDE, 1.0)
 
     half2 = pl.multiple_of(h2 * HALF, HALF)
@@ -183,7 +204,7 @@
     for k in range(MATES):
         mate = grp_pos ^ k
         at = pl.multiple_of((mate & 1) * HALF + (mate >> 1 & 1) * SENT_STEP, 8)
-        m2[k] = turned[pl.ds(at, SENT), :].astype(jnp.bfloat16)
+        m2[k * SENT : (k + 1) * SENT, :] = turned[pl.ds(at, SENT), :].astype(jnp.bfloat16)
         phase_rows(c2.at[k], s2.at[k], shifts[2], h2 * ANGLES + at, SENT, 1.0)
 
     half4 = pl.multiple_of(h4 * HALF, HALF)
@@ -196,7 +217,7 @@
 
 
 def send_order(count):
-    return [7, 6, 5, 3, 4, 2, 1, 0] if count == SUBS else list(range(count - 1, -1, -1))
+    return [6, 7, 5, 3, 4, 2, 1, 0] if count == SUBS else list(range(count - 1, -1, -1))
 
 
 def dot(left, right):
@@ -215,46 +236,53 @@
     ranges, m0, m1, m2, c0, s0, c1, s1, c2, s2 = refs[sources : sources + 10]
     outs = refs[sources + 10 : sources + 10 + MATES]
     wide, sub0, sub1, sub2 = refs[sources + 10 + MATES :]
-    depth = blocks[0].shape[1] // SUBS
+    depth = ranges.shape[0] // sources
     freqs = c0.shape[1]
     scale = 1.0 / math.sqrt(freqs)
+    width = blocks[0].shape[1]
+    pieces = blocks[0].shape[0] // FIRST
+    tails = SUBS * MAIN
+    wide[tails:, :] = jnp.zeros((SUBS * TAIL_PAD, wide.shape[1]), wide.dtype)
     for t in range(SUBS):
-        row = t * FIRST_PAD
-        if FIRST_PAD > FIRST:
-            wide[row + FIRST : row + FIRST_PAD, :] = jnp.zeros(
-                (FIRST_PAD - FIRST, wide.shape[1]), wide.dtype
-            )
+        piece, at = divmod(t * depth, width)
         for k in range(sources):
-            wide[row : row + FIRST, k * depth : (k + 1) * depth] = blocks[k][
-                :, t * depth : (t + 1) * depth
+            lanes = slice(k * depth, (k + 1) * depth)
+            block = blocks[k]
+            wide[t * MAIN : (t + 1) * MAIN, lanes] = block[
+                piece * MAIN : (piece + 1) * MAIN, at : at + depth
             ]
+            row = tails + t * TAIL_PAD
+            start = pieces * MAIN + piece * TAIL
+            wide[row : row + TAIL, lanes] = block[start : start + TAIL, at : at + depth]
     sub0[...] = (dot(wide[...], ranges[...]) * scale).astype(sub0.dtype)
     for p in range(SUBS // 2):
-        both = dot(m0[...], sub0[2 * p * FIRST_PAD : 2 * (p + 1) * FIRST_PAD, :])
+        main = sub0[2 * p * MAIN : 2 * (p + 1) * MAIN, :]
+        tail = sub0[tails + 2 * p * TAIL_PAD : tails + 2 * (p + 1) * TAIL_PAD, :]
+        both = dot(m0[...], jnp.concatenate([main, tail], axis=0))
         turn(sub1, slice(p * WIDE, (p + 1) * WIDE), both[:WIDE], both[WIDE:], c0[...], s0[...])
     for p in range(SUBS // 4):
-        low = dot(m1[...], sub1[2 * p * WIDE : (2 * p + 1) * WIDE, :])
-        high = dot(m1[...], sub1[(2 * p + 1) * WIDE : (2 * p + 2) * WIDE, :])
+        low = sub1[2 * p * WIDE : (2 * p + 1) * WIDE, :]
+        high = sub1[(2 * p + 1) * WIDE : (2 * p + 2) * WIDE, :]
         rows = slice(p * HALF, (p + 1) * HALF)
-        turn(sub2, rows, low + high, low - high, c1[...], s1[...])
+        turn(sub2, rows, dot(m1[...], low + high), dot(m1[...], low - high), c1[...], s1[...])
+    low, high = sub2[:HALF, :], sub2[HALF:, :]
+    total, diff = low + high, low - high
+    total, diff = dot(m2[...], total), dot(m2[...], diff)
     for k in range(MATES):
-        low = dot(m2[k], sub2[:HALF, :])
-        high = dot(m2[k], sub2[HALF:, :])
-        turn(outs[k], slice(None), low + high, low - high, c2[k], s2[k])
+        rows = slice(k * SENT, (k + 1) * SENT)
+        turn(outs[k], slice(None), total[rows], diff[rows], c2[k], s2[k])
 
 
 def own_kernel(along, own, m3, m4, c3, s3, part, sub4):
-    low = dot(m3[...], own[...])
-    high = dot(m3[...], along[...])
-    turn(sub4, slice(None), low + high, low - high, c3[...], s3[...])
+    low, high = own[...], along[...]
+    turn(sub4, slice(None), dot(m3[...], low + high), dot(m3[...], low - high), c3[...], s3[...])
     part[...] = dot(m4[...], sub4[...])
 
 
 def grp_kernel(across, both, part, m3, m4, c3, s3, c4, s4, out_far, sub4, out, sems):
     freqs = c3.shape[1]
-    low = dot(m3[...], across[...])
-    high = dot(m3[...], both[...])
-    turn(sub4, slice(None), low + high, low - high, c3[...], s3[...])
+    low, high = across[...], both[...]
+    turn(sub4, slice(None), dot(m3[...], low + high), dot(m3[...], low - high), c3[...], s3[...])
     pieces = sems.shape[0]
     count = out.shape[1] // pieces
     copies = []
@@ -295,11 +323,12 @@
     bf16, f32 = jnp.bfloat16, jnp.float32
     shape = jax.ShapeDtypeStruct
     lanes = SUBS * 2 * freqs
+    pieces = max(1, lanes // 128)
 
     table = jnp.asarray(beam_rows(pulses))
     beams = pl.pallas_call(
         functools.partial(beam_kernel, pulses=pulses),
-        out_shape=[shape((FIRST, lanes), bf16)] * n_band,
+        out_shape=[shape((FIRST * pieces, lanes // pieces), bf16)] * n_band,
         in_specs=[FAR, FAR],
         out_specs=[VMEM] * n_band,
         scratch_shapes=[
@@ -322,9 +351,9 @@
         table_kernel,
         out_shape=[
             shape((wide2, wide2), bf16),
-            shape((2 * WIDE, 2 * FIRST_PAD), bf16),
+            shape((2 * WIDE, 2 * (MAIN + TAIL_PAD)), bf16),
             shape((HALF, WIDE), bf16),
-            shape((MATES, SENT, HALF), bf16),
+            shape((MATES * SENT, HALF), bf16),
             shape((HALF, SENT), bf16),
             shape((ANGLES, HALF), bf16),
         ]
@@ -351,8 +380,8 @@
         in_specs=[VMEM] * (n_band + 10),
         out_specs=[VMEM] * MATES,
         scratch_shapes=[
-            pltpu.VMEM((SUBS * FIRST_PAD, wide2), bf16),
-            pltpu.VMEM((SUBS * FIRST_PAD, wide2), bf16),
+            pltpu.VMEM((SUBS * (MAIN + TAIL_PAD), wide2), bf16),
+            pltpu.VMEM((SUBS * (MAIN + TAIL_PAD), wide2), bf16),
             pltpu.VMEM((SUBS // 2 * WIDE, wide2), bf16),
             pltpu.VMEM((SUBS // 4 * HALF, wide2), bf16),
         ],

time: 33.4 us -> 32.3 us (0.967)
  waiting for transfers between devices: 10.4 us -> 7.31 us
  starting transfers between devices: 13.4 us -> 15.3 us
    ppermute x10, waiting for transfers between devices: 10.4 us -> 7.31 us  [swapped(): lax.ppermute(block, axis, [(low, low ^ mask) for low in range(count)])]
    ppermute x10, starting transfers between devices: 13.4 us -> 15.3 us  [swapped(): lax.ppermute(block, axis, [(low, low ^ mask) for low in range(count)])]
  transfers between devices with their start and end apart: 10 -> 10, of which waited for: 5 -> 3; matrix products, arithmetic and copies ran while one was open for 0% -> 0% of each run, Pallas kernels for 12% -> 13%
where the time goes in v3:
time: 32.3 us; the launch traced here: 32.2 us
  starting transfers between devices  15.3 us (47%)
  Pallas kernels  9.41 us (29%)
  waiting for transfers between devices  7.31 us (23%)
    ppermute x10, starting transfers between devices, swapped(): lax.ppermute(block, axis, [(low, low ^ mask) for low in range(count)])  15.3 us
    ppermute x10, waiting for transfers between devices, swapped(): lax.ppermute(block, axis, [(low, low ^ mask) for low in range(count)])  7.31 us
    pallas_call x1, Pallas kernels, on_device(): pl.pallas_call(table_kernel, out_shape=[shape((wide2, wide2), bf16), shap...  3.63 us
    pallas_call x1, Pallas kernels, on_device(): pl.pallas_call(functools.partial(beam_kernel, pulses=pulses), out_shape=[...  1.99 us
    pallas_call x1, Pallas kernels, on_device(): pl.pallas_call(functools.partial(band_kernel, sources=n_band), out_shape=...  1.9 us
    pallas_call x1, Pallas kernels, on_device(): pl.pallas_call(grp_kernel, out_shape=shape((2, ANGLES, freq_count), bf16)...  1.33 us
  transfers between devices with their start and end apart: 10, of which 3 were waited for; matrix products, arithmetic and copies ran while one was open for 0% of the time, Pallas kernels for 13%

profile of v3, /device:TPU:0, one launch (start us, length us, event | category | flops | bytes accessed | tf_op | source)
XLA Modules:
  0.0 32.2 jit_solution(9232975640223687188)
XLA Ops:
  0.0 2.0 %beam.1 = (bf16[280,128]{1,0:T(8,128)(2,1)S(1)}, bf16[280,128]{1,0:T(8,128)(2,1)S(1)}, bf16[280,128]{1,0:T(8,128)(2,1)S(1)}, bf16[280,128]{1,0:T(8,128)(2,1)S(1)...) custom-call(bf16[2,32,4096]{2,1,0:T(8,128)(2,1)} %raw_far.1, ...), custom_call_target="tpu_custom_call" | custom-call | flops 293601280 | bytes 2097152 | tf_op jit(solution)/shard_map/beam/pallas_call | solution.py:329
  2.0 5.1 %collective-permute-start = (bf16[280,128]{1,0:T(8,128)(2,1)S(1)}, bf16[280,128]{1,0:T(8,128)(2,1)S(1)}, u32[]{:S(2)}, u32[]{:S(2)}) collective-permute-start(bf16[280,128]{1,0:T(8,128)(2,1)S(1)} %get-tuple-element.33), channel_id=1, source_target_pairs={{0,6},{1,7},{2,4},{3,5},{4,2},{5,3},{6,0},{7,1},{8,14},{9,15},{10,... | collective-permute-start | bytes 215048 | tf_op jit(solution)/shard_map/ppermute | solution.py:315
  7.1 0.0 collective-permute-start.1
  7.1 0.7 %collective-permute-start.2 = (bf16[280,128]{1,0:T(8,128)(2,1)S(1)}, bf16[280,128]{1,0:T(8,128)(2,1)S(1)}, u32[]{:S(2)}, u32[]{:S(2)}) collective-permute-start(bf16[280,128]{1,0:T(8,128)(2,1)S(1)} %get-tuple-element.35), channel_id=1, source_target_pairs={{0,5},{1,4},{2,7},{3,6},{4,1},{5,0},{6,3},{7,2},{8,13},{9,12},{10,... | collective-permute-start | bytes 215048 | tf_op jit(solution)/shard_map/ppermute | solution.py:315
  7.8 2.5 %collective-permute-start.3 = (bf16[280,128]{1,0:T(8,128)(2,1)S(1)}, bf16[280,128]{1,0:T(8,128)(2,1)S(1)}, u32[]{:S(2)}, u32[]{:S(2)}) collective-permute-start(bf16[280,128]{1,0:T(8,128)(2,1)S(1)} %get-tuple-element.36), channel_id=1, source_target_pairs={{0,3},{1,2},{2,1},{3,0},{4,7},{5,6},{6,5},{7,4},{8,11},{9,10},{10,... | collective-permute-start | bytes 215048 | tf_op jit(solution)/shard_map/ppermute | solution.py:315
  10.4 0.8 %collective-permute-start.4 = (bf16[280,128]{1,0:T(8,128)(2,1)S(1)}, bf16[280,128]{1,0:T(8,128)(2,1)S(1)}, u32[]{:S(2)}, u32[]{:S(2)}) collective-permute-start(bf16[280,128]{1,0:T(8,128)(2,1)S(1)} %get-tuple-element.37), channel_id=1, source_target_pairs={{0,4},{1,5},{2,6},{3,7},{4,0},{5,1},{6,2},{7,3},{8,12},{9,13},{10,... | collective-permute-start | bytes 215048 | tf_op jit(solution)/shard_map/ppermute | solution.py:315
  11.2 0.0 collective-permute-done.refs_0_
  11.2 2.6 %collective-permute-start.5 = (bf16[280,128]{1,0:T(8,128)(2,1)S(1)}, bf16[280,128]{1,0:T(8,128)(2,1)S(1)}, u32[]{:S(2)}, u32[]{:S(2)}) collective-permute-start(bf16[280,128]{1,0:T(8,128)(2,1)S(1)} %get-tuple-element.38), channel_id=1, source_target_pairs={{0,2},{1,3},{2,0},{3,1},{4,6},{5,7},{6,4},{7,5},{8,10},{9,11},{10,... | collective-permute-start | bytes 215048 | tf_op jit(solution)/shard_map/ppermute | solution.py:315
  13.8 0.0 collective-permute-done.1.refs_1_
  13.8 0.0 collective-permute-start.6
  13.8 3.6 %tables.1 = (bf16[512,512]{1,0:T(8,128)(2,1)S(1)}, bf16[288,144]{1,0:T(8,128)(2,1)S(1)}, bf16[256,144]{1,0:T(8,128)(2,1)S(1)}, bf16[544,256]{1,0:T(8,128)(2,1)S(...) custom-call(f32[5]{0:T(128)S(1)} %copy-done.3, ...), custom_call_target="tpu_custom_call" | custom-call | flops 16777216 | bytes 8388608 | tf_op jit(solution)/shard_map/tables/pallas_call | solution.py:350
  17.5 0.0 collective-permute-done.2.refs_2_
  17.5 0.0 collective-permute-done.3.refs_3_
  17.5 1.8 %collective-permute-done.4.refs_4_ = bf16[280,128]{1,0:T(8,128)(2,1)S(1)} collective-permute-done((bf16[280,128]{1,0:T(8,128)(2,1)S(1)}, bf16[280,128]{1,0:T(8,128)(2,1)S(1)}, u32[]{:S(2)}, u32[]{:S(2)}) %collective-permute-start.4) | collective-permute-done | bytes 71712 | tf_op jit(solution)/shard_map/ppermute | solution.py:315
  19.3 0.0 collective-permute-done.5.refs_5_
  19.3 0.0 collective-permute-done.6.refs_6_
  19.3 1.9 %band_merges.1 = (bf16[136,512]{1,0:T(8,128)(2,1)S(1)}, bf16[136,512]{1,0:T(8,128)(2,1)S(1)}, bf16[136,512]{1,0:T(8,128)(2,1)S(1)}, bf16[136,512]{1,0:T(8,128)(2,1)S(1)}) custom-call(bf16[280,128]{1,0:T(8,128)(2,1)S(1)} %collective-permute-done.refs_0_, bf16[280,128]{1,0:T(8,128)(2,1)S(1)} %collective-permute-done.1.refs_1_, ...), custom_call_target="tpu_custom_call" | custom-call | flops 2147483648 | bytes 4194304 | tf_op jit(solution)/shard_map/band_merges/pallas_call | solution.py:377
  21.2 1.5 %collective-permute-start.9 = (bf16[136,512]{1,0:T(8,128)(2,1)S(1)}, bf16[136,512]{1,0:T(8,128)(2,1)S(1)}, u32[]{:S(2)}, u32[]{:S(2)}) collective-permute-start(bf16[136,512]{1,0:T(8,128)(2,1)S(1)} %get-tuple-element.53), channel_id=1, source_target_pairs={{0,8},{8,0},{16,24},{24,16},{1,9},{9,1},{17,25},{25,17},{2,10},{10... | collective-permute-start | bytes 417800 | tf_op jit(solution)/shard_map/ppermute | solution.py:315
  22.8 1.5 %collective-permute-start.7 = (bf16[136,512]{1,0:T(8,128)(2,1)S(1)}, bf16[136,512]{1,0:T(8,128)(2,1)S(1)}, u32[]{:S(2)}, u32[]{:S(2)}) collective-permute-start(bf16[136,512]{1,0:T(8,128)(2,1)S(1)} %get-tuple-element.51), channel_id=1, source_target_pairs={{0,16},{8,24},{16,0},{24,8},{1,17},{9,25},{17,1},{25,9},{2,18},{10... | collective-permute-start | bytes 417800 | tf_op jit(solution)/shard_map/ppermute | solution.py:315
  24.3 0.5 %collective-permute-start.8 = (bf16[136,512]{1,0:T(8,128)(2,1)S(1)}, bf16[136,512]{1,0:T(8,128)(2,1)S(1)}, u32[]{:S(2)}, u32[]{:S(2)}) collective-permute-start(bf16[136,512]{1,0:T(8,128)(2,1)S(1)} %get-tuple-element.52), channel_id=1, source_target_pairs={{0,24},{8,16},{16,8},{24,0},{1,25},{9,17},{17,9},{25,1},{2,26},{10... | collective-permute-start | bytes 417800 | tf_op jit(solution)/shard_map/ppermute | solution.py:315
  24.8 2.1 %collective-permute-done.9.along = bf16[136,512]{1,0:T(8,128)(2,1)S(1)} collective-permute-done((bf16[136,512]{1,0:T(8,128)(2,1)S(1)}, bf16[136,512]{1,0:T(8,128)(2,1)S(1)}, u32[]{:S(2)}, u32[]{:S(2)}) %collective-permute-start.9) | collective-permute-done | bytes 139296 | tf_op jit(solution)/shard_map/ppermute | solution.py:315
  26.9 0.6 %own_merge.1.part = f32[512,512]{1,0:T(8,128)S(1)} custom-call(bf16[136,512]{1,0:T(8,128)(2,1)S(1)} %collective-permute-done.9.along, bf16[136,512]{1,0:T(8,128)(2,1)S(1)} %get-tuple-element.54.own, bf16[256,136]{1,0:T(8,128)(2,1)S(1)} %get-tuple-element.55.m3, bf16[512,256]{1,0:T(8,128)(2,1)S(1)} %get-tuple-element.56.m4, ...), custom_call_target="tpu_custom_call" | custom-call | flops 536870912 | bytes 2097152 | tf_op jit(solution)/shard_map/own_merge/pallas_call | solution.py:395
  27.5 3.4 %collective-permute-done.7.across = bf16[136,512]{1,0:T(8,128)(2,1)S(1)} collective-permute-done((bf16[136,512]{1,0:T(8,128)(2,1)S(1)}, bf16[136,512]{1,0:T(8,128)(2,1)S(1)}, u32[]{:S(2)}, u32[]{:S(2)}) %collective-permute-start.7) | collective-permute-done | bytes 139296 | tf_op jit(solution)/shard_map/ppermute | solution.py:315
  30.8 1.3 %grp_merges.1 = bf16[2,512,256]{2,1,0:T(8,128)(2,1)} custom-call(bf16[136,512]{1,0:T(8,128)(2,1)S(1)} %collective-permute-done.7.across, bf16[136,512]{1,0:T(8,128)(2,1)S(1)} %collective-permute-done.8.both, f32[512,512]{1,0:T(8,128)S(1)} %own_merge.1.part, bf16[256,136]{1,0:T(8,128)(2,1)S(1)} %get-tuple-element.55.m3, ...), custom_call_target="tpu_custom_call" | custom-call | flops 536870912 | bytes 2097152 | tf_op jit(solution)/shard_map/grp_merges/pallas_call | solution.py:405
  (9 shorter events, 0.0 us)
Async XLA Ops:
  0.0 13.8 %copy-start = (bf16[8,64,512]{2,1,0:T(8,128)(2,1)S(1)}, bf16[8,64,512]{2,1,0:T(8,128)(2,1)}, u32[]{:S(2)}) copy-start(bf16[8,64,512]{2,1,0:T(8,128)(2,1)} %constant.5.clone.ranges) | copy-start | bytes 1572868
  0.0 13.8 %copy-start.2 = (f32[5,2,4,512]{3,2,1,0:T(4,128)S(1)}, f32[5,2,4,512]{3,2,1,0:T(4,128)}, u32[]{:S(2)}) copy-start(f32[5,2,4,512]{3,2,1,0:T(4,128)} %weights.1) | copy-start | bytes 245764
  0.0 13.8 %copy-start.1 = (s32[5,2,4,512]{3,2,1,0:T(4,128)S(1)}, s32[5,2,4,512]{3,2,1,0:T(4,128)}, u32[]{:S(2)}) copy-start(s32[5,2,4,512]{3,2,1,0:T(4,128)} %taps.1) | copy-start | bytes 245764
  2.0 9.2 %collective-permute-start = (bf16[280,128]{1,0:T(8,128)(2,1)S(1)}, bf16[280,128]{1,0:T(8,128)(2,1)S(1)}, u32[]{:S(2)}, u32[]{:S(2)}) collective-permute-start(bf16[280,128]{1,0:T(8,128)(2,1)S(1)} %get-tuple-element.33), channel_id=1, source_target_pairs={{0,6},{1,7},{2,4},{3,5},{4,2},{5,3},{6,0},{7,1},{8,14},{9,15},{10,... | collective-permute-start | bytes 215048 | tf_op jit(solution)/shard_map/ppermute | solution.py:315
  7.1 6.7 %collective-permute-start.1 = (bf16[280,128]{1,0:T(8,128)(2,1)S(1)}, bf16[280,128]{1,0:T(8,128)(2,1)S(1)}, u32[]{:S(2)}, u32[]{:S(2)}) collective-permute-start(bf16[280,128]{1,0:T(8,128)(2,1)S(1)} %get-tuple-element.34), channel_id=1, source_target_pairs={{0,7},{1,6},{2,5},{3,4},{4,3},{5,2},{6,1},{7,0},{8,15},{9,14},{10,... | collective-permute-start | bytes 215048 | tf_op jit(solution)/shard_map/ppermute | solution.py:315
  7.1 10.4 %collective-permute-start.2 = (bf16[280,128]{1,0:T(8,128)(2,1)S(1)}, bf16[280,128]{1,0:T(8,128)(2,1)S(1)}, u32[]{:S(2)}, u32[]{:S(2)}) collective-permute-start(bf16[280,128]{1,0:T(8,128)(2,1)S(1)} %get-tuple-element.35), channel_id=1, source_target_pairs={{0,5},{1,4},{2,7},{3,6},{4,1},{5,0},{6,3},{7,2},{8,13},{9,12},{10,... | collective-permute-start | bytes 215048 | tf_op jit(solution)/shard_map/ppermute | solution.py:315
  7.8 9.6 %collective-permute-start.3 = (bf16[280,128]{1,0:T(8,128)(2,1)S(1)}, bf16[280,128]{1,0:T(8,128)(2,1)S(1)}, u32[]{:S(2)}, u32[]{:S(2)}) collective-permute-start(bf16[280,128]{1,0:T(8,128)(2,1)S(1)} %get-tuple-element.36), channel_id=1, source_target_pairs={{0,3},{1,2},{2,1},{3,0},{4,7},{5,6},{6,5},{7,4},{8,11},{9,10},{10,... | collective-permute-start | bytes 215048 | tf_op jit(solution)/shard_map/ppermute | solution.py:315
  10.4 8.9 %collective-permute-start.4 = (bf16[280,128]{1,0:T(8,128)(2,1)S(1)}, bf16[280,128]{1,0:T(8,128)(2,1)S(1)}, u32[]{:S(2)}, u32[]{:S(2)}) collective-permute-start(bf16[280,128]{1,0:T(8,128)(2,1)S(1)} %get-tuple-element.37), channel_id=1, source_target_pairs={{0,4},{1,5},{2,6},{3,7},{4,0},{5,1},{6,2},{7,3},{8,12},{9,13},{10,... | collective-permute-start | bytes 215048 | tf_op jit(solution)/shard_map/ppermute | solution.py:315
  11.2 2.6 %copy-start.3 = (f32[5]{0:T(128)S(1)}, f32[5]{0:T(128)}, u32[]{:S(2)}) copy-start(f32[5]{0:T(128)} %shifts.1) | copy-start | bytes 64
  11.2 8.1 %collective-permute-start.5 = (bf16[280,128]{1,0:T(8,128)(2,1)S(1)}, bf16[280,128]{1,0:T(8,128)(2,1)S(1)}, u32[]{:S(2)}, u32[]{:S(2)}) collective-permute-start(bf16[280,128]{1,0:T(8,128)(2,1)S(1)} %get-tuple-element.38), channel_id=1, source_target_pairs={{0,2},{1,3},{2,0},{3,1},{4,6},{5,7},{6,4},{7,5},{8,10},{9,11},{10,... | collective-permute-start | bytes 215048 | tf_op jit(solution)/shard_map/ppermute | solution.py:315
  13.8 5.5 %collective-permute-start.6 = (bf16[280,128]{1,0:T(8,128)(2,1)S(1)}, bf16[280,128]{1,0:T(8,128)(2,1)S(1)}, u32[]{:S(2)}, u32[]{:S(2)}) collective-permute-start(bf16[280,128]{1,0:T(8,128)(2,1)S(1)} %get-tuple-element.39), channel_id=1, source_target_pairs={{0,1},{1,0},{2,3},{3,2},{4,5},{5,4},{6,7},{7,6},{8,9},{9,8},{10,11... | collective-permute-start | bytes 215048 | tf_op jit(solution)/shard_map/ppermute | solution.py:315
  21.2 5.6 %collective-permute-start.9 = (bf16[136,512]{1,0:T(8,128)(2,1)S(1)}, bf16[136,512]{1,0:T(8,128)(2,1)S(1)}, u32[]{:S(2)}, u32[]{:S(2)}) collective-permute-start(bf16[136,512]{1,0:T(8,128)(2,1)S(1)} %get-tuple-element.53), channel_id=1, source_target_pairs={{0,8},{8,0},{16,24},{24,16},{1,9},{9,1},{17,25},{25,17},{2,10},{10... | collective-permute-start | bytes 417800 | tf_op jit(solution)/shard_map/ppermute | solution.py:315
  22.8 8.0 %collective-permute-start.7 = (bf16[136,512]{1,0:T(8,128)(2,1)S(1)}, bf16[136,512]{1,0:T(8,128)(2,1)S(1)}, u32[]{:S(2)}, u32[]{:S(2)}) collective-permute-start(bf16[136,512]{1,0:T(8,128)(2,1)S(1)} %get-tuple-element.51), channel_id=1, source_target_pairs={{0,16},{8,24},{16,0},{24,8},{1,17},{9,25},{17,1},{25,9},{2,18},{10... | collective-permute-start | bytes 417800 | tf_op jit(solution)/shard_map/ppermute | solution.py:315
  24.3 6.5 %collective-permute-start.8 = (bf16[136,512]{1,0:T(8,128)(2,1)S(1)}, bf16[136,512]{1,0:T(8,128)(2,1)S(1)}, u32[]{:S(2)}, u32[]{:S(2)}) collective-permute-start(bf16[136,512]{1,0:T(8,128)(2,1)S(1)} %get-tuple-element.52), channel_id=1, source_target_pairs={{0,24},{8,16},{16,8},{24,0},{1,25},{9,17},{17,9},{25,1},{2,26},{10... | collective-permute-start | bytes 417800 | tf_op jit(solution)/shard_map/ppermute | solution.py:315

commit v4 on v3

--- a/solution.py
+++ b/solution.py
@@ -30,8 +30,11 @@
 
 WIDE = up_to(rows_read(0, HALF - 1)[1] + 1, 16)
 WIDE_STEP = HALF - WIDE
-SENT = up_to(rows_read(0, HALF - 1)[1] + 1, 8)
+SENT = up_to(rows_read(0, HALF - 1)[1] + 1, 4)
 SENT_STEP = HALF - SENT
+BULK = SENT // 16 * 16
+REST = SENT - BULK
+SENT_PAD = BULK + 2 * REST
 
 
 def first_windows():
@@ -45,26 +48,27 @@
 
 
 FIRST_STARTS, FIRST = first_windows()
-FIRST_SIDE = up_to(FIRST // 2, 8)
-MAIN_SIDE = FIRST // 32 * 16
-MAIN = 2 * MAIN_SIDE
-TAIL_SIDE = FIRST // 2 - MAIN_SIDE
-TAIL = 2 * TAIL_SIDE
+CLASSES = 4
+CLASS_MAIN = FIRST // (16 * CLASSES) * 16
+MAIN = CLASSES * CLASS_MAIN
+CLASS_ROWS = [len(range(u, FIRST, CLASSES)) for u in range(CLASSES)]
+CLASS_PAD = up_to(max(CLASS_ROWS), 8)
+TAIL_IDS = [CLASSES * m + u for u in range(CLASSES) for m in range(CLASS_MAIN, CLASS_ROWS[u])]
+TAIL = len(TAIL_IDS)
 TAIL_PAD = up_to(TAIL, 8)
 
 
 def beam_rows(pulses):
-    pulse_ids = np.arange(pulses // 2)
-    sides = []
-    for odd in (0, 1):
-        sectors = np.zeros((SUBS, FIRST_SIDE, pulses))
-        for sector in range(SUBS):
-            start = (sector & 1) * HALF + FIRST_STARTS[sector >> 1]
-            angle_ids = start + 2 * np.arange(FIRST // 2) + odd
+    pulse_ids = np.arange(pulses // CLASSES)
+    table = np.zeros((CLASSES, SUBS, CLASS_PAD, 2 * len(pulse_ids)))
+    for sector in range(SUBS):
+        start = (sector & 1) * HALF + FIRST_STARTS[sector >> 1]
+        for u in range(CLASSES):
+            angle_ids = start + u + CLASSES * np.arange(CLASS_ROWS[u])
             phases = (angle_ids[:, None] * pulse_ids[None, :] % ANGLES) * (2.0 * math.pi / ANGLES)
-            sectors[sector, : FIRST // 2] = np.concatenate([np.cos(phases), np.sin(phases)], axis=1)
-        sides.append(sectors.reshape(SUBS * FIRST_SIDE, pulses))
-    return np.stack(sides).astype(ml_dtypes.bfloat16)
+            rows = np.concatenate([np.cos(phases), np.sin(phases)], axis=1)
+            table[(start + u) % CLASSES, sector, : len(rows)] = rows
+    return table.reshape(CLASSES, SUBS * CLASS_PAD, -1).astype(ml_dtypes.bfloat16)
 
 
 def range_rows(freq_count, freq_local):
@@ -82,7 +86,7 @@
 def beam_kernel(raw_far, table_far, *refs, pulses):
     outs, (raw, table, rhs, acc, raw_sem, table_sem) = refs[:-6], refs[-6:]
     freqs = raw.shape[1]
-    half = pulses // 2
+    quarter = pulses // CLASSES
     band_pos = lax.axis_index("band")
     scale = 1.0 / math.sqrt(pulses)
     raw_copy = pltpu.make_async_copy(raw_far, raw, raw_sem)
@@ -95,49 +99,63 @@
         for t in range(SUBS):
             at = pl.multiple_of((block * SUBS + t) * pulses, pulses)
             row = t * 2 * freqs
-            first = raw[:, :, pl.ds(at, half)]
-            second = raw[:, :, pl.ds(at + half, half)]
-            for side, mixed in enumerate((first + second, first - second)):
-                rhs[side, row : row + freqs, :half] = mixed[0]
-                rhs[side, row : row + freqs, half:] = mixed[1]
-                rhs[side, row + freqs : row + 2 * freqs, :half] = mixed[1]
-                rhs[side, row + freqs : row + 2 * freqs, half:] = -mixed[0]
+            x0, x1, x2, x3 = (
+                raw[:, :, pl.ds(at + j * quarter, quarter)].astype(jnp.float32)
+                for j in range(CLASSES)
+            )
+            even, odd, even_diff, odd_diff = x0 + x2, x1 + x3, x0 - x2, x1 - x3
+            for u, (real, imag) in enumerate(
+                (
+                    (even[0] + odd[0], even[1] + odd[1]),
+                    (even_diff[0] + odd_diff[1], even_diff[1] - odd_diff[0]),
+                    (even[0] - odd[0], even[1] - odd[1]),
+                    (even_diff[0] - odd_diff[1], even_diff[1] + odd_diff[0]),
+                )
+            ):
+                real, imag = real.astype(rhs.dtype), imag.astype(rhs.dtype)
+                rhs[u, row : row + freqs, :quarter] = real
+                rhs[u, row : row + freqs, quarter:] = imag
+                rhs[u, row + freqs : row + 2 * freqs, :quarter] = imag
+                rhs[u, row + freqs : row + 2 * freqs, quarter:] = -real
         if upper == 0:
             table_copy.wait()
-        for side in (0, 1):
-            acc[side] = lax.dot_general(
-                table[side],
-                rhs[side],
+        for u in range(CLASSES):
+            acc[u] = lax.dot_general(
+                table[u],
+                rhs[u],
                 (((1,), (1,)), ((), ())),
                 preferred_element_type=jnp.float32,
             )
         for low in range(SUBS):
             sector = (band_pos ^ low) & (SUBS - 1)
-            rows = pl.ds(pl.multiple_of(sector * FIRST_SIDE, 8), FIRST_SIDE)
-            even, odd = acc[0, rows, :] * scale, acc[1, rows, :] * scale
+            rows = pl.ds(pl.multiple_of(sector * CLASS_PAD, 8), CLASS_PAD)
+            shift = FIRST_STARTS[0] % CLASSES
+            for combo in range(1, len(FIRST_STARTS)):
+                shift = jnp.where(sector >> 1 == combo, FIRST_STARTS[combo] % CLASSES, shift)
+            classes = [
+                acc[(shift + u) & (CLASSES - 1), rows, :] * scale for u in range(CLASSES)
+            ]
             out = outs[upper * SUBS + low]
             width = out.shape[1]
-            pieces = even.shape[1] // width
+            pieces = acc.shape[2] // width
             tails = []
             for piece in range(pieces):
                 lanes = slice(piece * width, (piece + 1) * width)
-                at = piece * MAIN
-                out[at : at + MAIN_SIDE, :] = even[:MAIN_SIDE, lanes].astype(out.dtype)
-                out[at + MAIN_SIDE : at + MAIN, :] = odd[:MAIN_SIDE, lanes].astype(out.dtype)
-                for side in (even, odd):
-                    tails.append(side[MAIN_SIDE : MAIN_SIDE + TAIL_SIDE, lanes])
+                for u, values in enumerate(classes):
+                    at = piece * MAIN + u * CLASS_MAIN
+                    out[at : at + CLASS_MAIN, :] = values[:CLASS_MAIN, lanes].astype(out.dtype)
+                    tails.append(values[CLASS_MAIN : CLASS_ROWS[u], lanes])
             out[pieces * MAIN :, :] = jnp.concatenate(tails, axis=0).astype(out.dtype)
 
 
 def interp_t(taps, weights, start, rows, mixed=False):
     row_ids = lax.broadcasted_iota(jnp.int32, (rows, ANGLES), 0)
     if mixed:
-        ids = row_ids - MAIN
-        tail = jnp.where(ids < TAIL_SIDE, 2 * ids, 2 * (ids - TAIL_SIDE) + 1) + MAIN
-        ids = row_ids - MAIN_SIDE
-        main = jnp.where(ids < 0, 2 * row_ids, 2 * ids + 1)
-        row_ids = jnp.where(row_ids < MAIN, main, tail)
-        row_ids = jnp.where(row_ids < FIRST, row_ids, -ANGLES)
+        ids = row_ids % CLASS_MAIN * CLASSES + row_ids // CLASS_MAIN
+        for place in range(TAIL_PAD):
+            value = TAIL_IDS[place] if place < TAIL else -ANGLES
+            ids = jnp.where(row_ids == MAIN + place, value, ids)
+        row_ids = ids
     row_ids += start
     total = jnp.zeros((rows, ANGLES), jnp.float32)
     for s in range(taps.shape[0]):
@@ -152,17 +170,26 @@
         * (2.0 * math.pi / freqs)
         * shift
     )
-    groups = count // 8
-    coarse_ids = lax.broadcasted_iota(jnp.int32, (groups, 1), 0) * 8 + first
-    coarse = ((coarse_ids.astype(jnp.float32) + 0.5) / (2.0 * ANGLES) - 0.5) * ranges
-    fine_ids = lax.broadcasted_iota(jnp.int32, (8, 1), 0)
-    fine = (fine_ids.astype(jnp.float32) / (2.0 * ANGLES)) * ranges
-    coarse_cos, coarse_sin = jnp.cos(coarse) * ROOT_HALF, jnp.sin(coarse) * ROOT_HALF
-    fine_cos, fine_sin = jnp.cos(fine), jnp.sin(fine)
-    for group in range(groups):
-        c, s = coarse_cos[group : group + 1], coarse_sin[group : group + 1]
-        cos_ref[group * 8 : group * 8 + 8, :] = c * fine_cos - s * fine_sin
-        sin_ref[group * 8 : group * 8 + 8, :] = sign * (s * fine_cos + c * fine_sin)
+    def turns(start, step, count):
+        ids = lax.broadcasted_iota(jnp.int32, (count, 1), 0) * step + start
+        angle = ids.astype(jnp.float32) / (2.0 * ANGLES) * ranges
+        return jnp.cos(angle), jnp.sin(angle)
+
+    def times(left, right):
+        return left[0] * right[0] - left[1] * right[1], left[0] * right[1] + left[1] * right[0]
+
+    offset = (0.5 / (2.0 * ANGLES) - 0.5) * ranges
+    offset = (jnp.cos(offset) * ROOT_HALF, jnp.sin(offset) * ROOT_HALF)
+    coarse = times(turns(first, 64, 8), offset)
+    middle, fine = turns(0, 8, 8), turns(0, 1, 8)
+    for group in range(count // 8):
+        if group % 8 == 0:
+            a = group // 8
+            row = times((coarse[0][a : a + 1], coarse[1][a : a + 1]), middle)
+        b = group % 8
+        cosine, sine = times((row[0][b : b + 1], row[1][b : b + 1]), fine)
+        cos_ref[group * 8 : group * 8 + 8, :] = cosine
+        sin_ref[group * 8 : group * 8 + 8, :] = sign * sine
 
 
 def table_kernel(
@@ -178,7 +205,7 @@
         range_out[k * depth : (k + 1) * depth, :] = ranges[band_pos ^ k]
 
     def fill(out, level, half, start, rows, first, count, row=0):
-        turned[:, :rows] = interp_t(taps[level, half], weights[level, half], start, rows).T
+        turned[:ANGLES, :rows] = interp_t(taps[level, half], weights[level, half], start, rows).T
         out[row : row + count, :rows] = turned[pl.ds(first, count), :rows].astype(jnp.bfloat16)
 
     first_start = FIRST_STARTS[0]
@@ -186,7 +213,7 @@
         first_start = jnp.where(h1 + 2 * h2 == combo, FIRST_STARTS[combo], first_start)
     wide1 = pl.multiple_of(h1 * HALF + h2 * WIDE_STEP, 16)
     rows = MAIN + TAIL_PAD
-    turned[:, :rows] = interp_t(taps[0, h0], weights[0, h0], first_start, rows, True).T
+    turned[:ANGLES, :rows] = interp_t(taps[0, h0], weights[0, h0], first_start, rows, True).T
     window = turned[pl.ds(wide1, WIDE), :rows].astype(jnp.bfloat16)
     main, tail = window[:, :MAIN], window[:, MAIN:]
     for at, sign in ((0, 1), (WIDE, -1)):
@@ -200,15 +227,27 @@
     fill(m1, 1, h1, h2 * WIDE_STEP, WIDE, half2, HALF)
     phase_rows(c1, s1, shifts[1], h1 * ANGLES + half2, HALF, 1.0)
 
-    turned[...] = interp_t(taps[2, h2], weights[2, h2], 0, HALF).T
+    turned[:ANGLES, :] = interp_t(taps[2, h2], weights[2, h2], 0, HALF).T
+    turned[ANGLES:, :] = jnp.zeros((turned.shape[0] - ANGLES, HALF), jnp.float32)
     for k in range(MATES):
         mate = grp_pos ^ k
-        at = pl.multiple_of((mate & 1) * HALF + (mate >> 1 & 1) * SENT_STEP, 8)
-        m2[k * SENT : (k + 1) * SENT, :] = turned[pl.ds(at, SENT), :].astype(jnp.bfloat16)
-        phase_rows(c2.at[k], s2.at[k], shifts[2], h2 * ANGLES + at, SENT, 1.0)
+        half, side = mate & 1, mate >> 1 & 1
+        rows = turned[pl.ds(pl.multiple_of(half * HALF, HALF), SENT_STEP + SENT_PAD), :]
+        window = jnp.where(side == 1, rows[SENT_STEP:], rows[:SENT_PAD])
+        m2[k * SENT_PAD : (k + 1) * SENT_PAD, :] = window.astype(jnp.bfloat16)
+        first = h2 * ANGLES + half * HALF + side * SENT_STEP
+        phase_rows(c2.at[k], s2.at[k], shifts[2], first, SENT_PAD, 1.0)
 
     half4 = pl.multiple_of(h4 * HALF, HALF)
-    fill(m3, 3, h3, h4 * SENT_STEP, SENT, half4, HALF)
+    turned[:ANGLES, :SENT_PAD] = interp_t(taps[3, h3], weights[3, h3], h4 * SENT_STEP, SENT_PAD).T
+    window = turned[pl.ds(half4, HALF), :SENT_PAD].astype(jnp.bfloat16)
+    nothing = jnp.zeros((HALF, REST), jnp.bfloat16)
+    for part in (0, 1):
+        m3[part, :, :BULK] = window[:, :BULK]
+        tail = BULK + part * REST
+        m3[part, :, tail : tail + REST] = window[:, BULK:SENT]
+        tail = BULK + (1 - part) * REST
+        m3[part, :, tail : tail + REST] = nothing
     sign3 = (1 - 2 * h3).astype(jnp.float32)
     phase_rows(c3, s3, shifts[3], h3 * ANGLES + half4, HALF, sign3)
     fill(m4, 4, h4, 0, HALF, 0, ANGLES)
@@ -224,10 +263,31 @@
     return jnp.dot(left, right, preferred_element_type=jnp.float32)
 
 
+def turned_pair(total, diff, cosine, sine):
+    freqs = cosine.shape[1]
+    real = cosine * total[:, :freqs] - sine * diff[:, freqs:]
+    imag = cosine * total[:, freqs:] + sine * diff[:, :freqs]
+    return real, imag
+
+
 def turn(out, rows, total, diff, cosine, sine):
     freqs = cosine.shape[1]
-    out[rows, :freqs] = (cosine * total[:, :freqs] - sine * diff[:, freqs:]).astype(out.dtype)
-    out[rows, freqs:] = (cosine * total[:, freqs:] + sine * diff[:, :freqs]).astype(out.dtype)
+    real, imag = turned_pair(total, diff, cosine, sine)
+    out[rows, :freqs] = real.astype(out.dtype)
+    out[rows, freqs:] = imag.astype(out.dtype)
+
+
+def merge_sent(out, low, high, m3, cosine, sine):
+    freqs = cosine.shape[1]
+    sides = []
+    for mixed in (low + high, low - high):
+        tail = mixed[2 * BULK :]
+        for part in (0, 1):
+            rows = jnp.concatenate([mixed[part * BULK : (part + 1) * BULK], tail], axis=0)
+            sides.append(dot(m3[part], rows))
+    total_real, total_imag, diff_real, diff_imag = sides
+    out[:, :freqs] = (cosine * total_real - sine * diff_imag).astype(out.dtype)
+    out[:, freqs:] = (cosine * total_imag + sine * diff_real).astype(out.dtype)
 
 
 def band_kernel(*refs, sources):
@@ -269,20 +329,22 @@
     total, diff = low + high, low - high
     total, diff = dot(m2[...], total), dot(m2[...], diff)
     for k in range(MATES):
-        rows = slice(k * SENT, (k + 1) * SENT)
-        turn(outs[k], slice(None), total[rows], diff[rows], c2[k], s2[k])
+        rows = slice(k * SENT_PAD, (k + 1) * SENT_PAD)
+        real, imag = turned_pair(total[rows], diff[rows], c2[k], s2[k])
+        for part, rows in enumerate((real.astype(sub2.dtype), imag.astype(sub2.dtype))):
+            outs[k][part * BULK : (part + 1) * BULK, :] = rows[:BULK]
+            tail = 2 * BULK + part * REST
+            outs[k][tail : tail + REST, :] = rows[BULK:SENT]
 
 
 def own_kernel(along, own, m3, m4, c3, s3, part, sub4):
-    low, high = own[...], along[...]
-    turn(sub4, slice(None), dot(m3[...], low + high), dot(m3[...], low - high), c3[...], s3[...])
+    merge_sent(sub4, own[...], along[...], m3, c3[...], s3[...])
     part[...] = dot(m4[...], sub4[...])
 
 
 def grp_kernel(across, both, part, m3, m4, c3, s3, c4, s4, out_far, sub4, out, sems):
     freqs = c3.shape[1]
-    low, high = across[...], both[...]
-    turn(sub4, slice(None), dot(m3[...], low + high), dot(m3[...], low - high), c3[...], s3[...])
+    merge_sent(sub4, across[...], both[...], m3, c3[...], s3[...])
     pieces = sems.shape[0]
     count = out.shape[1] // pieces
     copies = []
@@ -334,14 +396,14 @@
         scratch_shapes=[
             pltpu.VMEM(raw.shape, bf16),
             pltpu.VMEM(table.shape, bf16),
-            pltpu.VMEM((2, lanes, pulses), bf16),
-            pltpu.VMEM((2, SUBS * FIRST_SIDE, lanes), f32),
+            pltpu.VMEM((CLASSES, lanes, 2 * pulses // CLASSES), bf16),
+            pltpu.VMEM((CLASSES, SUBS * CLASS_PAD, lanes), f32),
             pltpu.SemaphoreType.DMA,
             pltpu.SemaphoreType.DMA,
         ],
         compiler_params=BEAM_PARAMS,
         cost_estimate=pl.CostEstimate(
-            flops=2 * SUBS * FIRST * pulses * lanes, bytes_accessed=1 << 21, transcendentals=0
+            flops=SUBS * FIRST * pulses * lanes, bytes_accessed=1 << 21, transcendentals=0
         ),
         name="beam",
     )(raw, table)
@@ -353,18 +415,18 @@
             shape((wide2, wide2), bf16),
             shape((2 * WIDE, 2 * (MAIN + TAIL_PAD)), bf16),
             shape((HALF, WIDE), bf16),
-            shape((MATES * SENT, HALF), bf16),
-            shape((HALF, SENT), bf16),
+            shape((MATES * SENT_PAD, HALF), bf16),
+            shape((2, HALF, SENT_PAD), bf16),
             shape((ANGLES, HALF), bf16),
         ]
         + [
             shape(rows + (freq_count,), f32)
-            for rows in ((WIDE,), (HALF,), (MATES, SENT), (HALF,), (ANGLES,))
+            for rows in ((WIDE,), (HALF,), (MATES, SENT_PAD), (HALF,), (ANGLES,))
             for _ in range(2)
         ],
         in_specs=[SMEM, VMEM, VMEM, VMEM],
         out_specs=[VMEM] * 16,
-        scratch_shapes=[pltpu.VMEM((ANGLES, HALF), f32)],
+        scratch_shapes=[pltpu.VMEM((ANGLES + 2 * REST, HALF), f32)],
         compiler_params=PARAMS,
         cost_estimate=pl.CostEstimate(
             flops=1 << 24, bytes_accessed=1 << 23, transcendentals=1 << 18
@@ -376,7 +438,7 @@
     blocks = [swapped(beams[k], "band", k) if k else beams[k] for k in send_order(n_band)]
     pieces = pl.pallas_call(
         functools.partial(band_kernel, sources=n_band),
-        out_shape=[shape((SENT, wide2), bf16)] * MATES,
+        out_shape=[shape((2 * SENT, freq_count), bf16)] * MATES,
         in_specs=[VMEM] * (n_band + 10),
         out_specs=[VMEM] * MATES,
         scratch_shapes=[

time: 32.3 us -> 32.2 us (level)
  no operation moved by 1% of the time
where the time goes in v4:
time: 32.2 us; the launch traced here: 32 us
  starting transfers between devices  15.4 us (48%)
  Pallas kernels  9.25 us (29%)
  waiting for transfers between devices  7.32 us (23%)
    ppermute x10, starting transfers between devices, swapped(): lax.ppermute(block, axis, [(low, low ^ mask) for low in range(count)])  15.4 us
    ppermute x10, waiting for transfers between devices, swapped(): lax.ppermute(block, axis, [(low, low ^ mask) for low in range(count)])  7.32 us
    pallas_call x1, Pallas kernels, on_device(): pl.pallas_call(table_kernel, out_shape=[shape((wide2, wide2), bf16), shap...  3.48 us
    pallas_call x1, Pallas kernels, on_device(): pl.pallas_call(functools.partial(beam_kernel, pulses=pulses), out_shape=[...  1.95 us
    pallas_call x1, Pallas kernels, on_device(): pl.pallas_call(functools.partial(band_kernel, sources=n_band), out_shape=...  1.89 us
    pallas_call x1, Pallas kernels, on_device(): pl.pallas_call(grp_kernel, out_shape=shape((2, ANGLES, freq_count), bf16)...  1.36 us
  transfers between devices with their start and end apart: 10, of which 3 were waited for; matrix products, arithmetic and copies ran while one was open for 0% of the time, Pallas kernels for 13%

profile of v4, /device:TPU:0, one launch (start us, length us, event | category | flops | bytes accessed | tf_op | source)
XLA Modules:
  0.0 32.0 jit_solution(1803342773867278293)
XLA Ops:
  0.0 2.0 %beam.1 = (bf16[280,128]{1,0:T(8,128)(2,1)S(1)}, bf16[280,128]{1,0:T(8,128)(2,1)S(1)}, bf16[280,128]{1,0:T(8,128)(2,1)S(1)}, bf16[280,128]{1,0:T(8,128)(2,1)S(1)...) custom-call(bf16[2,32,4096]{2,1,0:T(8,128)(2,1)} %raw_far.1, ...), custom_call_target="tpu_custom_call" | custom-call | flops 146800640 | bytes 2097152 | tf_op jit(solution)/shard_map/beam/pallas_call | solution.py:391
  2.0 5.1 %collective-permute-start = (bf16[280,128]{1,0:T(8,128)(2,1)S(1)}, bf16[280,128]{1,0:T(8,128)(2,1)S(1)}, u32[]{:S(2)}, u32[]{:S(2)}) collective-permute-start(bf16[280,128]{1,0:T(8,128)(2,1)S(1)} %get-tuple-element.33), channel_id=1, source_target_pairs={{0,6},{1,7},{2,4},{3,5},{4,2},{5,3},{6,0},{7,1},{8,14},{9,15},{10,... | collective-permute-start | bytes 215048 | tf_op jit(solution)/shard_map/ppermute | solution.py:377
  7.1 0.0 collective-permute-start.1
  7.1 0.7 %collective-permute-start.2 = (bf16[280,128]{1,0:T(8,128)(2,1)S(1)}, bf16[280,128]{1,0:T(8,128)(2,1)S(1)}, u32[]{:S(2)}, u32[]{:S(2)}) collective-permute-start(bf16[280,128]{1,0:T(8,128)(2,1)S(1)} %get-tuple-element.35), channel_id=1, source_target_pairs={{0,5},{1,4},{2,7},{3,6},{4,1},{5,0},{6,3},{7,2},{8,13},{9,12},{10,... | collective-permute-start | bytes 215048 | tf_op jit(solution)/shard_map/ppermute | solution.py:377
  7.8 2.5 %collective-permute-start.3 = (bf16[280,128]{1,0:T(8,128)(2,1)S(1)}, bf16[280,128]{1,0:T(8,128)(2,1)S(1)}, u32[]{:S(2)}, u32[]{:S(2)}) collective-permute-start(bf16[280,128]{1,0:T(8,128)(2,1)S(1)} %get-tuple-element.36), channel_id=1, source_target_pairs={{0,3},{1,2},{2,1},{3,0},{4,7},{5,6},{6,5},{7,4},{8,11},{9,10},{10,... | collective-permute-start | bytes 215048 | tf_op jit(solution)/shard_map/ppermute | solution.py:377
  10.4 0.8 %collective-permute-start.4 = (bf16[280,128]{1,0:T(8,128)(2,1)S(1)}, bf16[280,128]{1,0:T(8,128)(2,1)S(1)}, u32[]{:S(2)}, u32[]{:S(2)}) collective-permute-start(bf16[280,128]{1,0:T(8,128)(2,1)S(1)} %get-tuple-element.37), channel_id=1, source_target_pairs={{0,4},{1,5},{2,6},{3,7},{4,0},{5,1},{6,2},{7,3},{8,12},{9,13},{10,... | collective-permute-start | bytes 215048 | tf_op jit(solution)/shard_map/ppermute | solution.py:377
  11.2 0.0 collective-permute-done.refs_0_
  11.2 2.6 %collective-permute-start.5 = (bf16[280,128]{1,0:T(8,128)(2,1)S(1)}, bf16[280,128]{1,0:T(8,128)(2,1)S(1)}, u32[]{:S(2)}, u32[]{:S(2)}) collective-permute-start(bf16[280,128]{1,0:T(8,128)(2,1)S(1)} %get-tuple-element.38), channel_id=1, source_target_pairs={{0,2},{1,3},{2,0},{3,1},{4,6},{5,7},{6,4},{7,5},{8,10},{9,11},{10,... | collective-permute-start | bytes 215048 | tf_op jit(solution)/shard_map/ppermute | solution.py:377
  13.8 0.0 collective-permute-done.1.refs_1_
  13.8 0.0 collective-permute-start.6
  13.8 3.5 %tables.1 = (bf16[512,512]{1,0:T(8,128)(2,1)S(1)}, bf16[288,144]{1,0:T(8,128)(2,1)S(1)}, bf16[256,144]{1,0:T(8,128)(2,1)S(1)}, bf16[544,256]{1,0:T(8,128)(2,1)S(...) custom-call(f32[5]{0:T(128)S(1)} %copy-done.3, ...), custom_call_target="tpu_custom_call" | custom-call | flops 16777216 | bytes 8388608 | tf_op jit(solution)/shard_map/tables/pallas_call | solution.py:412
  17.3 0.0 collective-permute-done.2.refs_2_
  17.3 0.0 collective-permute-done.3.refs_3_
  17.3 2.0 %collective-permute-done.4.refs_4_ = bf16[280,128]{1,0:T(8,128)(2,1)S(1)} collective-permute-done((bf16[280,128]{1,0:T(8,128)(2,1)S(1)}, bf16[280,128]{1,0:T(8,128)(2,1)S(1)}, u32[]{:S(2)}, u32[]{:S(2)}) %collective-permute-start.4) | collective-permute-done | bytes 71712 | tf_op jit(solution)/shard_map/ppermute | solution.py:377
  19.3 0.0 collective-permute-done.5.refs_5_
  19.3 1.9 %band_merges.1 = (bf16[264,256]{1,0:T(8,128)(2,1)S(1)}, bf16[264,256]{1,0:T(8,128)(2,1)S(1)}, bf16[264,256]{1,0:T(8,128)(2,1)S(1)}, bf16[264,256]{1,0:T(8,128)(2,1)S(1)}) custom-call(bf16[280,128]{1,0:T(8,128)(2,1)S(1)} %collective-permute-done.refs_0_, bf16[280,128]{1,0:T(8,128)(2,1)S(1)} %collective-permute-done.1.refs_1_, ...), custom_call_target="tpu_custom_call" | custom-call | flops 2147483648 | bytes 4194304 | tf_op jit(solution)/shard_map/band_merges/pallas_call | solution.py:439
  21.2 1.6 %collective-permute-start.9 = (bf16[264,256]{1,0:T(8,128)(2,1)S(1)}, bf16[264,256]{1,0:T(8,128)(2,1)S(1)}, u32[]{:S(2)}, u32[]{:S(2)}) collective-permute-start(bf16[264,256]{1,0:T(8,128)(2,1)S(1)} %get-tuple-element.53), channel_id=1, source_target_pairs={{0,8},{8,0},{16,24},{24,16},{1,9},{9,1},{17,25},{25,17},{2,10},{10... | collective-permute-start | bytes 405512 | tf_op jit(solution)/shard_map/ppermute | solution.py:377
  22.8 1.5 %collective-permute-start.7 = (bf16[264,256]{1,0:T(8,128)(2,1)S(1)}, bf16[264,256]{1,0:T(8,128)(2,1)S(1)}, u32[]{:S(2)}, u32[]{:S(2)}) collective-permute-start(bf16[264,256]{1,0:T(8,128)(2,1)S(1)} %get-tuple-element.51), channel_id=1, source_target_pairs={{0,16},{8,24},{16,0},{24,8},{1,17},{9,25},{17,1},{25,9},{2,18},{10... | collective-permute-start | bytes 405512 | tf_op jit(solution)/shard_map/ppermute | solution.py:377
  24.3 0.5 %collective-permute-start.8 = (bf16[264,256]{1,0:T(8,128)(2,1)S(1)}, bf16[264,256]{1,0:T(8,128)(2,1)S(1)}, u32[]{:S(2)}, u32[]{:S(2)}) collective-permute-start(bf16[264,256]{1,0:T(8,128)(2,1)S(1)} %get-tuple-element.52), channel_id=1, source_target_pairs={{0,24},{8,16},{16,8},{24,0},{1,25},{9,17},{17,9},{25,1},{2,26},{10... | collective-permute-start | bytes 405512 | tf_op jit(solution)/shard_map/ppermute | solution.py:377
  24.8 2.0 %collective-permute-done.9.along = bf16[264,256]{1,0:T(8,128)(2,1)S(1)} collective-permute-done((bf16[264,256]{1,0:T(8,128)(2,1)S(1)}, bf16[264,256]{1,0:T(8,128)(2,1)S(1)}, u32[]{:S(2)}, u32[]{:S(2)}) %collective-permute-start.9) | collective-permute-done | bytes 135200 | tf_op jit(solution)/shard_map/ppermute | solution.py:377
  26.8 0.6 %own_merge.1.part = f32[512,512]{1,0:T(8,128)S(1)} custom-call(bf16[264,256]{1,0:T(8,128)(2,1)S(1)} %collective-permute-done.9.along, bf16[264,256]{1,0:T(8,128)(2,1)S(1)} %get-tuple-element.54.own, bf16[2,256,136]{2,1,0:T(8,128)(2,1)S(1)} %get-tuple-element.55.m3, bf16[512,256]{1,0:T(8,128)(2,1)S(1)} %get-tuple-element.56.m4, ...), custom_call_target="tpu_custom_call" | custom-call | flops 536870912 | bytes 2097152 | tf_op jit(solution)/shard_map/own_merge/pallas_call | solution.py:457
  27.3 3.3 %collective-permute-done.7.across = bf16[264,256]{1,0:T(8,128)(2,1)S(1)} collective-permute-done((bf16[264,256]{1,0:T(8,128)(2,1)S(1)}, bf16[264,256]{1,0:T(8,128)(2,1)S(1)}, u32[]{:S(2)}, u32[]{:S(2)}) %collective-permute-start.7) | collective-permute-done | bytes 135200 | tf_op jit(solution)/shard_map/ppermute | solution.py:377
  30.7 0.0 collective-permute-done.8.both
  30.7 1.4 %grp_merges.1 = bf16[2,512,256]{2,1,0:T(8,128)(2,1)} custom-call(bf16[264,256]{1,0:T(8,128)(2,1)S(1)} %collective-permute-done.7.across, bf16[264,256]{1,0:T(8,128)(2,1)S(1)} %collective-permute-done.8.both, f32[512,512]{1,0:T(8,128)S(1)} %own_merge.1.part, bf16[2,256,136]{2,1,0:T(8,128)(2,1)S(1)} %get-tuple-element.55.m3, ...), custom_call_target="tpu_custom_call" | custom-call | flops 536870912 | bytes 2097152 | tf_op jit(solution)/shard_map/grp_merges/pallas_call | solution.py:467
  (9 shorter events, 0.0 us)
Async XLA Ops:
  0.0 13.8 %copy-start = (bf16[8,64,512]{2,1,0:T(8,128)(2,1)S(1)}, bf16[8,64,512]{2,1,0:T(8,128)(2,1)}, u32[]{:S(2)}) copy-start(bf16[8,64,512]{2,1,0:T(8,128)(2,1)} %constant.5.clone.ranges) | copy-start | bytes 1572868
  0.0 13.8 %copy-start.2 = (f32[5,2,4,512]{3,2,1,0:T(4,128)S(1)}, f32[5,2,4,512]{3,2,1,0:T(4,128)}, u32[]{:S(2)}) copy-start(f32[5,2,4,512]{3,2,1,0:T(4,128)} %weights.1) | copy-start | bytes 245764
  0.0 13.8 %copy-start.1 = (s32[5,2,4,512]{3,2,1,0:T(4,128)S(1)}, s32[5,2,4,512]{3,2,1,0:T(4,128)}, u32[]{:S(2)}) copy-start(s32[5,2,4,512]{3,2,1,0:T(4,128)} %taps.1) | copy-start | bytes 245764
  2.0 9.2 %collective-permute-start = (bf16[280,128]{1,0:T(8,128)(2,1)S(1)}, bf16[280,128]{1,0:T(8,128)(2,1)S(1)}, u32[]{:S(2)}, u32[]{:S(2)}) collective-permute-start(bf16[280,128]{1,0:T(8,128)(2,1)S(1)} %get-tuple-element.33), channel_id=1, source_target_pairs={{0,6},{1,7},{2,4},{3,5},{4,2},{5,3},{6,0},{7,1},{8,14},{9,15},{10,... | collective-permute-start | bytes 215048 | tf_op jit(solution)/shard_map/ppermute | solution.py:377
  7.1 6.7 %collective-permute-start.1 = (bf16[280,128]{1,0:T(8,128)(2,1)S(1)}, bf16[280,128]{1,0:T(8,128)(2,1)S(1)}, u32[]{:S(2)}, u32[]{:S(2)}) collective-permute-start(bf16[280,128]{1,0:T(8,128)(2,1)S(1)} %get-tuple-element.34), channel_id=1, source_target_pairs={{0,7},{1,6},{2,5},{3,4},{4,3},{5,2},{6,1},{7,0},{8,15},{9,14},{10,... | collective-permute-start | bytes 215048 | tf_op jit(solution)/shard_map/ppermute | solution.py:377
  7.1 10.2 %collective-permute-start.2 = (bf16[280,128]{1,0:T(8,128)(2,1)S(1)}, bf16[280,128]{1,0:T(8,128)(2,1)S(1)}, u32[]{:S(2)}, u32[]{:S(2)}) collective-permute-start(bf16[280,128]{1,0:T(8,128)(2,1)S(1)} %get-tuple-element.35), channel_id=1, source_target_pairs={{0,5},{1,4},{2,7},{3,6},{4,1},{5,0},{6,3},{7,2},{8,13},{9,12},{10,... | collective-permute-start | bytes 215048 | tf_op jit(solution)/shard_map/ppermute | solution.py:377
  7.8 9.5 %collective-permute-start.3 = (bf16[280,128]{1,0:T(8,128)(2,1)S(1)}, bf16[280,128]{1,0:T(8,128)(2,1)S(1)}, u32[]{:S(2)}, u32[]{:S(2)}) collective-permute-start(bf16[280,128]{1,0:T(8,128)(2,1)S(1)} %get-tuple-element.36), channel_id=1, source_target_pairs={{0,3},{1,2},{2,1},{3,0},{4,7},{5,6},{6,5},{7,4},{8,11},{9,10},{10,... | collective-permute-start | bytes 215048 | tf_op jit(solution)/shard_map/ppermute | solution.py:377
  10.4 8.9 %collective-permute-start.4 = (bf16[280,128]{1,0:T(8,128)(2,1)S(1)}, bf16[280,128]{1,0:T(8,128)(2,1)S(1)}, u32[]{:S(2)}, u32[]{:S(2)}) collective-permute-start(bf16[280,128]{1,0:T(8,128)(2,1)S(1)} %get-tuple-element.37), channel_id=1, source_target_pairs={{0,4},{1,5},{2,6},{3,7},{4,0},{5,1},{6,2},{7,3},{8,12},{9,13},{10,... | collective-permute-start | bytes 215048 | tf_op jit(solution)/shard_map/ppermute | solution.py:377
  11.2 2.6 %copy-start.3 = (f32[5]{0:T(128)S(1)}, f32[5]{0:T(128)}, u32[]{:S(2)}) copy-start(f32[5]{0:T(128)} %shifts.1) | copy-start | bytes 64
  11.2 8.1 %collective-permute-start.5 = (bf16[280,128]{1,0:T(8,128)(2,1)S(1)}, bf16[280,128]{1,0:T(8,128)(2,1)S(1)}, u32[]{:S(2)}, u32[]{:S(2)}) collective-permute-start(bf16[280,128]{1,0:T(8,128)(2,1)S(1)} %get-tuple-element.38), channel_id=1, source_target_pairs={{0,2},{1,3},{2,0},{3,1},{4,6},{5,7},{6,4},{7,5},{8,10},{9,11},{10,... | collective-permute-start | bytes 215048 | tf_op jit(solution)/shard_map/ppermute | solution.py:377
  13.8 5.5 %collective-permute-start.6 = (bf16[280,128]{1,0:T(8,128)(2,1)S(1)}, bf16[280,128]{1,0:T(8,128)(2,1)S(1)}, u32[]{:S(2)}, u32[]{:S(2)}) collective-permute-start(bf16[280,128]{1,0:T(8,128)(2,1)S(1)} %get-tuple-element.39), channel_id=1, source_target_pairs={{0,1},{1,0},{2,3},{3,2},{4,5},{5,4},{6,7},{7,6},{8,9},{9,8},{10,11... | collective-permute-start | bytes 215048 | tf_op jit(solution)/shard_map/ppermute | solution.py:377
  21.2 5.6 %collective-permute-start.9 = (bf16[264,256]{1,0:T(8,128)(2,1)S(1)}, bf16[264,256]{1,0:T(8,128)(2,1)S(1)}, u32[]{:S(2)}, u32[]{:S(2)}) collective-permute-start(bf16[264,256]{1,0:T(8,128)(2,1)S(1)} %get-tuple-element.53), channel_id=1, source_target_pairs={{0,8},{8,0},{16,24},{24,16},{1,9},{9,1},{17,25},{25,17},{2,10},{10... | collective-permute-start | bytes 405512 | tf_op jit(solution)/shard_map/ppermute | solution.py:377
  22.8 7.9 %collective-permute-start.7 = (bf16[264,256]{1,0:T(8,128)(2,1)S(1)}, bf16[264,256]{1,0:T(8,128)(2,1)S(1)}, u32[]{:S(2)}, u32[]{:S(2)}) collective-permute-start(bf16[264,256]{1,0:T(8,128)(2,1)S(1)} %get-tuple-element.51), channel_id=1, source_target_pairs={{0,16},{8,24},{16,0},{24,8},{1,17},{9,25},{17,1},{25,9},{2,18},{10... | collective-permute-start | bytes 405512 | tf_op jit(solution)/shard_map/ppermute | solution.py:377
  24.3 6.4 %collective-permute-start.8 = (bf16[264,256]{1,0:T(8,128)(2,1)S(1)}, bf16[264,256]{1,0:T(8,128)(2,1)S(1)}, u32[]{:S(2)}, u32[]{:S(2)}) collective-permute-start(bf16[264,256]{1,0:T(8,128)(2,1)S(1)} %get-tuple-element.52), channel_id=1, source_target_pairs={{0,24},{8,16},{16,8},{24,0},{1,25},{9,17},{17,9},{25,1},{2,26},{10... | collective-permute-start | bytes 405512 | tf_op jit(solution)/shard_map/ppermute | solution.py:377

commit v5 on v4

--- a/solution.py
+++ b/solution.py
@@ -30,7 +30,7 @@
 
 WIDE = up_to(rows_read(0, HALF - 1)[1] + 1, 16)
 WIDE_STEP = HALF - WIDE
-SENT = up_to(rows_read(0, HALF - 1)[1] + 1, 4)
+SENT = up_to(rows_read(0, HALF - 1)[1] + 1, 8)
 SENT_STEP = HALF - SENT
 BULK = SENT // 16 * 16
 REST = SENT - BULK
@@ -43,7 +43,7 @@
         low, high = rows_read(h2 * HALF, h2 * HALF + HALF - 1)
         for h1 in (0, 1):
             spans.append(rows_read(h1 * HALF + low, h1 * HALF + high))
-    rows = up_to(max(high - low + 1 + low % 2 for low, high in spans), 2)
+    rows = up_to(max(high - low + 1 + low % 2 for low, high in spans), 8)
     return [min(low - low % 2, HALF - rows) for low, high in spans], rows
 
 
@@ -55,7 +55,7 @@
 CLASS_PAD = up_to(max(CLASS_ROWS), 8)
 TAIL_IDS = [CLASSES * m + u for u in range(CLASSES) for m in range(CLASS_MAIN, CLASS_ROWS[u])]
 TAIL = len(TAIL_IDS)
-TAIL_PAD = up_to(TAIL, 8)
+TAIL_PAD = up_to(TAIL, 16)
 
 
 def beam_rows(pulses):
@@ -302,18 +302,18 @@
     width = blocks[0].shape[1]
     pieces = blocks[0].shape[0] // FIRST
     tails = SUBS * MAIN
-    wide[tails:, :] = jnp.zeros((SUBS * TAIL_PAD, wide.shape[1]), wide.dtype)
-    for t in range(SUBS):
-        piece, at = divmod(t * depth, width)
-        for k in range(sources):
-            lanes = slice(k * depth, (k + 1) * depth)
-            block = blocks[k]
-            wide[t * MAIN : (t + 1) * MAIN, lanes] = block[
+    blank = jnp.zeros((TAIL_PAD - TAIL, depth), wide.dtype)
+    for k in range(sources):
+        lanes = slice(k * depth, (k + 1) * depth)
+        ends = blocks[k][pieces * MAIN :, :]
+        for t in range(SUBS):
+            piece, at = divmod(t * depth, width)
+            wide[t * MAIN : (t + 1) * MAIN, lanes] = blocks[k][
                 piece * MAIN : (piece + 1) * MAIN, at : at + depth
             ]
+            end = ends[piece * TAIL : (piece + 1) * TAIL, at : at + depth]
             row = tails + t * TAIL_PAD
-            start = pieces * MAIN + piece * TAIL
-            wide[row : row + TAIL, lanes] = block[start : start + TAIL, at : at + depth]
+            wide[row : row + TAIL_PAD, lanes] = jnp.concatenate([end, blank], axis=0)
     sub0[...] = (dot(wide[...], ranges[...]) * scale).astype(sub0.dtype)
     for p in range(SUBS // 2):
         main = sub0[2 * p * MAIN : 2 * (p + 1) * MAIN, :]
@@ -331,10 +331,10 @@
     for k in range(MATES):
         rows = slice(k * SENT_PAD, (k + 1) * SENT_PAD)
         real, imag = turned_pair(total[rows], diff[rows], c2[k], s2[k])
-        for part, rows in enumerate((real.astype(sub2.dtype), imag.astype(sub2.dtype))):
-            outs[k][part * BULK : (part + 1) * BULK, :] = rows[:BULK]
-            tail = 2 * BULK + part * REST
-            outs[k][tail : tail + REST, :] = rows[BULK:SENT]
+        outs[k][:BULK, :] = real[:BULK].astype(sub2.dtype)
+        outs[k][BULK : 2 * BULK, :] = imag[:BULK].astype(sub2.dtype)
+        ends = jnp.concatenate([real[BULK:SENT], imag[BULK:SENT]], axis=0)
+        outs[k][2 * BULK :, :] = ends.astype(sub2.dtype)
 
 
 def own_kernel(along, own, m3, m4, c3, s3, part, sub4):

time: 32.2 us -> 32.7 us (1.016)
  waiting for transfers between devices: 7.32 us -> 7.65 us
    ppermute x10, waiting for transfers between devices: 7.32 us -> 7.65 us  [swapped(): lax.ppermute(block, axis, [(low, low ^ mask) for low in range(count)])]
  transfers between devices with their start and end apart: 10 -> 10, of which waited for: 3 -> 3; matrix products, arithmetic and copies ran while one was open for 0% -> 0% of each run, Pallas kernels for 13% -> 12%
where the time goes in v5:
time: 32.7 us; the launch traced here: 32.5 us
  starting transfers between devices  15.5 us (47%)
  Pallas kernels  9.23 us (28%)
  waiting for transfers between devices  7.65 us (23%)
    ppermute x10, starting transfers between devices, swapped(): lax.ppermute(block, axis, [(low, low ^ mask) for low in range(count)])  15.5 us
    ppermute x10, waiting for transfers between devices, swapped(): lax.ppermute(block, axis, [(low, low ^ mask) for low in range(count)])  7.65 us
    pallas_call x1, Pallas kernels, on_device(): pl.pallas_call(table_kernel, out_shape=[shape((wide2, wide2), bf16), shap...  3.43 us
    pallas_call x1, Pallas kernels, on_device(): pl.pallas_call(functools.partial(beam_kernel, pulses=pulses), out_shape=[...  1.95 us
    pallas_call x1, Pallas kernels, on_device(): pl.pallas_call(functools.partial(band_kernel, sources=n_band), out_shape=...  1.93 us
    pallas_call x1, Pallas kernels, on_device(): pl.pallas_call(grp_kernel, out_shape=shape((2, ANGLES, freq_count), bf16)...  1.36 us
  transfers between devices with their start and end apart: 10, of which 3 were waited for; matrix products, arithmetic and copies ran while one was open for 0% of the time, Pallas kernels for 12%

profile of v5, /device:TPU:0, one launch (start us, length us, event | category | flops | bytes accessed | tf_op | source)
XLA Modules:
  0.0 32.5 jit_solution(13622912921271164289)
XLA Ops:
  0.0 1.9 %beam.1 = (bf16[288,128]{1,0:T(8,128)(2,1)S(1)}, bf16[288,128]{1,0:T(8,128)(2,1)S(1)}, bf16[288,128]{1,0:T(8,128)(2,1)S(1)}, bf16[288,128]{1,0:T(8,128)(2,1)S(1)...) custom-call(bf16[2,32,4096]{2,1,0:T(8,128)(2,1)} %raw_far.1, ...), custom_call_target="tpu_custom_call" | custom-call | flops 150994944 | bytes 2097152 | tf_op jit(solution)/shard_map/beam/pallas_call | solution.py:391
  2.0 5.1 %collective-permute-start = (bf16[288,128]{1,0:T(8,128)(2,1)S(1)}, bf16[288,128]{1,0:T(8,128)(2,1)S(1)}, u32[]{:S(2)}, u32[]{:S(2)}) collective-permute-start(bf16[288,128]{1,0:T(8,128)(2,1)S(1)} %get-tuple-element.33), channel_id=1, source_target_pairs={{0,6},{1,7},{2,4},{3,5},{4,2},{5,3},{6,0},{7,1},{8,14},{9,15},{10,... | collective-permute-start | bytes 221192 | tf_op jit(solution)/shard_map/ppermute | solution.py:377
  7.1 0.0 collective-permute-start.1
  7.1 0.7 %collective-permute-start.2 = (bf16[288,128]{1,0:T(8,128)(2,1)S(1)}, bf16[288,128]{1,0:T(8,128)(2,1)S(1)}, u32[]{:S(2)}, u32[]{:S(2)}) collective-permute-start(bf16[288,128]{1,0:T(8,128)(2,1)S(1)} %get-tuple-element.35), channel_id=1, source_target_pairs={{0,5},{1,4},{2,7},{3,6},{4,1},{5,0},{6,3},{7,2},{8,13},{9,12},{10,... | collective-permute-start | bytes 221192 | tf_op jit(solution)/shard_map/ppermute | solution.py:377
  7.8 2.5 %collective-permute-start.3 = (bf16[288,128]{1,0:T(8,128)(2,1)S(1)}, bf16[288,128]{1,0:T(8,128)(2,1)S(1)}, u32[]{:S(2)}, u32[]{:S(2)}) collective-permute-start(bf16[288,128]{1,0:T(8,128)(2,1)S(1)} %get-tuple-element.36), channel_id=1, source_target_pairs={{0,3},{1,2},{2,1},{3,0},{4,7},{5,6},{6,5},{7,4},{8,11},{9,10},{10,... | collective-permute-start | bytes 221192 | tf_op jit(solution)/shard_map/ppermute | solution.py:377
  10.4 0.8 %collective-permute-start.4 = (bf16[288,128]{1,0:T(8,128)(2,1)S(1)}, bf16[288,128]{1,0:T(8,128)(2,1)S(1)}, u32[]{:S(2)}, u32[]{:S(2)}) collective-permute-start(bf16[288,128]{1,0:T(8,128)(2,1)S(1)} %get-tuple-element.37), channel_id=1, source_target_pairs={{0,4},{1,5},{2,6},{3,7},{4,0},{5,1},{6,2},{7,3},{8,12},{9,13},{10,... | collective-permute-start | bytes 221192 | tf_op jit(solution)/shard_map/ppermute | solution.py:377
  11.2 0.0 collective-permute-done.refs_0_
  11.2 2.8 %collective-permute-start.5 = (bf16[288,128]{1,0:T(8,128)(2,1)S(1)}, bf16[288,128]{1,0:T(8,128)(2,1)S(1)}, u32[]{:S(2)}, u32[]{:S(2)}) collective-permute-start(bf16[288,128]{1,0:T(8,128)(2,1)S(1)} %get-tuple-element.38), channel_id=1, source_target_pairs={{0,2},{1,3},{2,0},{3,1},{4,6},{5,7},{6,4},{7,5},{8,10},{9,11},{10,... | collective-permute-start | bytes 221192 | tf_op jit(solution)/shard_map/ppermute | solution.py:377
  14.0 0.0 collective-permute-done.1.refs_1_
  14.0 0.0 collective-permute-start.6
  14.0 3.4 %tables.1 = (bf16[512,512]{1,0:T(8,128)(2,1)S(1)}, bf16[288,160]{1,0:T(8,128)(2,1)S(1)}, bf16[256,144]{1,0:T(8,128)(2,1)S(1)}, bf16[576,256]{1,0:T(8,128)(2,1)S(...) custom-call(f32[5]{0:T(128)S(1)} %copy-done.3, ...), custom_call_target="tpu_custom_call" | custom-call | flops 16777216 | bytes 8388608 | tf_op jit(solution)/shard_map/tables/pallas_call | solution.py:412
  17.4 0.0 collective-permute-done.2.refs_2_
  17.4 2.2 %collective-permute-done.4.refs_4_ = bf16[288,128]{1,0:T(8,128)(2,1)S(1)} collective-permute-done((bf16[288,128]{1,0:T(8,128)(2,1)S(1)}, bf16[288,128]{1,0:T(8,128)(2,1)S(1)}, u32[]{:S(2)}, u32[]{:S(2)}) %collective-permute-start.4) | collective-permute-done | bytes 73760 | tf_op jit(solution)/shard_map/ppermute | solution.py:377
  19.6 0.0 collective-permute-done.5.refs_5_
  19.6 0.0 collective-permute-done.6.refs_6_
  19.6 1.9 %band_merges.1 = (bf16[272,256]{1,0:T(8,128)(2,1)S(1)}, bf16[272,256]{1,0:T(8,128)(2,1)S(1)}, bf16[272,256]{1,0:T(8,128)(2,1)S(1)}, bf16[272,256]{1,0:T(8,128)(2,1)S(1)}) custom-call(bf16[288,128]{1,0:T(8,128)(2,1)S(1)} %collective-permute-done.refs_0_, bf16[288,128]{1,0:T(8,128)(2,1)S(1)} %collective-permute-done.1.refs_1_, ...), custom_call_target="tpu_custom_call" | custom-call | flops 2147483648 | bytes 4194304 | tf_op jit(solution)/shard_map/band_merges/pallas_call | solution.py:439
  21.6 1.6 %collective-permute-start.9 = (bf16[272,256]{1,0:T(8,128)(2,1)S(1)}, bf16[272,256]{1,0:T(8,128)(2,1)S(1)}, u32[]{:S(2)}, u32[]{:S(2)}) collective-permute-start(bf16[272,256]{1,0:T(8,128)(2,1)S(1)} %get-tuple-element.53), channel_id=1, source_target_pairs={{0,8},{8,0},{16,24},{24,16},{1,9},{9,1},{17,25},{25,17},{2,10},{10... | collective-permute-start | bytes 417800 | tf_op jit(solution)/shard_map/ppermute | solution.py:377
  23.1 1.5 %collective-permute-start.7 = (bf16[272,256]{1,0:T(8,128)(2,1)S(1)}, bf16[272,256]{1,0:T(8,128)(2,1)S(1)}, u32[]{:S(2)}, u32[]{:S(2)}) collective-permute-start(bf16[272,256]{1,0:T(8,128)(2,1)S(1)} %get-tuple-element.51), channel_id=1, source_target_pairs={{0,16},{8,24},{16,0},{24,8},{1,17},{9,25},{17,1},{25,9},{2,18},{10... | collective-permute-start | bytes 417800 | tf_op jit(solution)/shard_map/ppermute | solution.py:377
  24.6 0.5 %collective-permute-start.8 = (bf16[272,256]{1,0:T(8,128)(2,1)S(1)}, bf16[272,256]{1,0:T(8,128)(2,1)S(1)}, u32[]{:S(2)}, u32[]{:S(2)}) collective-permute-start(bf16[272,256]{1,0:T(8,128)(2,1)S(1)} %get-tuple-element.52), channel_id=1, source_target_pairs={{0,24},{8,16},{16,8},{24,0},{1,25},{9,17},{17,9},{25,1},{2,26},{10... | collective-permute-start | bytes 417800 | tf_op jit(solution)/shard_map/ppermute | solution.py:377
  25.1 2.1 %collective-permute-done.9.along = bf16[272,256]{1,0:T(8,128)(2,1)S(1)} collective-permute-done((bf16[272,256]{1,0:T(8,128)(2,1)S(1)}, bf16[272,256]{1,0:T(8,128)(2,1)S(1)}, u32[]{:S(2)}, u32[]{:S(2)}) %collective-permute-start.9) | collective-permute-done | bytes 139296 | tf_op jit(solution)/shard_map/ppermute | solution.py:377
  27.2 0.6 %own_merge.1.part = f32[512,512]{1,0:T(8,128)S(1)} custom-call(bf16[272,256]{1,0:T(8,128)(2,1)S(1)} %collective-permute-done.9.along, bf16[272,256]{1,0:T(8,128)(2,1)S(1)} %get-tuple-element.54.own, bf16[2,256,144]{2,1,0:T(8,128)(2,1)S(1)} %get-tuple-element.55.m3, bf16[512,256]{1,0:T(8,128)(2,1)S(1)} %get-tuple-element.56.m4, ...), custom_call_target="tpu_custom_call" | custom-call | flops 536870912 | bytes 2097152 | tf_op jit(solution)/shard_map/own_merge/pallas_call | solution.py:457
  27.8 3.4 %collective-permute-done.7.across = bf16[272,256]{1,0:T(8,128)(2,1)S(1)} collective-permute-done((bf16[272,256]{1,0:T(8,128)(2,1)S(1)}, bf16[272,256]{1,0:T(8,128)(2,1)S(1)}, u32[]{:S(2)}, u32[]{:S(2)}) %collective-permute-start.7) | collective-permute-done | bytes 139296 | tf_op jit(solution)/shard_map/ppermute | solution.py:377
  31.2 0.0 collective-permute-done.8.both
  31.2 1.4 %grp_merges.1 = bf16[2,512,256]{2,1,0:T(8,128)(2,1)} custom-call(bf16[272,256]{1,0:T(8,128)(2,1)S(1)} %collective-permute-done.7.across, bf16[272,256]{1,0:T(8,128)(2,1)S(1)} %collective-permute-done.8.both, f32[512,512]{1,0:T(8,128)S(1)} %own_merge.1.part, bf16[2,256,144]{2,1,0:T(8,128)(2,1)S(1)} %get-tuple-element.55.m3, ...), custom_call_target="tpu_custom_call" | custom-call | flops 536870912 | bytes 2097152 | tf_op jit(solution)/shard_map/grp_merges/pallas_call | solution.py:467
  (9 shorter events, 0.0 us)
Async XLA Ops:
  0.0 14.0 %copy-start = (bf16[8,64,512]{2,1,0:T(8,128)(2,1)S(1)}, bf16[8,64,512]{2,1,0:T(8,128)(2,1)}, u32[]{:S(2)}) copy-start(bf16[8,64,512]{2,1,0:T(8,128)(2,1)} %constant.5.clone.ranges) | copy-start | bytes 1572868
  0.0 14.0 %copy-start.2 = (f32[5,2,4,512]{3,2,1,0:T(4,128)S(1)}, f32[5,2,4,512]{3,2,1,0:T(4,128)}, u32[]{:S(2)}) copy-start(f32[5,2,4,512]{3,2,1,0:T(4,128)} %weights.1) | copy-start | bytes 245764
  0.0 14.0 %copy-start.1 = (s32[5,2,4,512]{3,2,1,0:T(4,128)S(1)}, s32[5,2,4,512]{3,2,1,0:T(4,128)}, u32[]{:S(2)}) copy-start(s32[5,2,4,512]{3,2,1,0:T(4,128)} %taps.1) | copy-start | bytes 245764
  2.0 9.2 %collective-permute-start = (bf16[288,128]{1,0:T(8,128)(2,1)S(1)}, bf16[288,128]{1,0:T(8,128)(2,1)S(1)}, u32[]{:S(2)}, u32[]{:S(2)}) collective-permute-start(bf16[288,128]{1,0:T(8,128)(2,1)S(1)} %get-tuple-element.33), channel_id=1, source_target_pairs={{0,6},{1,7},{2,4},{3,5},{4,2},{5,3},{6,0},{7,1},{8,14},{9,15},{10,... | collective-permute-start | bytes 221192 | tf_op jit(solution)/shard_map/ppermute | solution.py:377
  7.1 6.9 %collective-permute-start.1 = (bf16[288,128]{1,0:T(8,128)(2,1)S(1)}, bf16[288,128]{1,0:T(8,128)(2,1)S(1)}, u32[]{:S(2)}, u32[]{:S(2)}) collective-permute-start(bf16[288,128]{1,0:T(8,128)(2,1)S(1)} %get-tuple-element.34), channel_id=1, source_target_pairs={{0,7},{1,6},{2,5},{3,4},{4,3},{5,2},{6,1},{7,0},{8,15},{9,14},{10,... | collective-permute-start | bytes 221192 | tf_op jit(solution)/shard_map/ppermute | solution.py:377
  7.1 10.3 %collective-permute-start.2 = (bf16[288,128]{1,0:T(8,128)(2,1)S(1)}, bf16[288,128]{1,0:T(8,128)(2,1)S(1)}, u32[]{:S(2)}, u32[]{:S(2)}) collective-permute-start(bf16[288,128]{1,0:T(8,128)(2,1)S(1)} %get-tuple-element.35), channel_id=1, source_target_pairs={{0,5},{1,4},{2,7},{3,6},{4,1},{5,0},{6,3},{7,2},{8,13},{9,12},{10,... | collective-permute-start | bytes 221192 | tf_op jit(solution)/shard_map/ppermute | solution.py:377
  7.8 9.6 %collective-permute-start.3 = (bf16[288,128]{1,0:T(8,128)(2,1)S(1)}, bf16[288,128]{1,0:T(8,128)(2,1)S(1)}, u32[]{:S(2)}, u32[]{:S(2)}) collective-permute-start(bf16[288,128]{1,0:T(8,128)(2,1)S(1)} %get-tuple-element.36), channel_id=1, source_target_pairs={{0,3},{1,2},{2,1},{3,0},{4,7},{5,6},{6,5},{7,4},{8,11},{9,10},{10,... | collective-permute-start | bytes 221192 | tf_op jit(solution)/shard_map/ppermute | solution.py:377
  10.4 9.3 %collective-permute-start.4 = (bf16[288,128]{1,0:T(8,128)(2,1)S(1)}, bf16[288,128]{1,0:T(8,128)(2,1)S(1)}, u32[]{:S(2)}, u32[]{:S(2)}) collective-permute-start(bf16[288,128]{1,0:T(8,128)(2,1)S(1)} %get-tuple-element.37), channel_id=1, source_target_pairs={{0,4},{1,5},{2,6},{3,7},{4,0},{5,1},{6,2},{7,3},{8,12},{9,13},{10,... | collective-permute-start | bytes 221192 | tf_op jit(solution)/shard_map/ppermute | solution.py:377
  11.2 2.8 %copy-start.3 = (f32[5]{0:T(128)S(1)}, f32[5]{0:T(128)}, u32[]{:S(2)}) copy-start(f32[5]{0:T(128)} %shifts.1) | copy-start | bytes 64
  11.2 8.4 %collective-permute-start.5 = (bf16[288,128]{1,0:T(8,128)(2,1)S(1)}, bf16[288,128]{1,0:T(8,128)(2,1)S(1)}, u32[]{:S(2)}, u32[]{:S(2)}) collective-permute-start(bf16[288,128]{1,0:T(8,128)(2,1)S(1)} %get-tuple-element.38), channel_id=1, source_target_pairs={{0,2},{1,3},{2,0},{3,1},{4,6},{5,7},{6,4},{7,5},{8,10},{9,11},{10,... | collective-permute-start | bytes 221192 | tf_op jit(solution)/shard_map/ppermute | solution.py:377
  14.0 5.7 %collective-permute-start.6 = (bf16[288,128]{1,0:T(8,128)(2,1)S(1)}, bf16[288,128]{1,0:T(8,128)(2,1)S(1)}, u32[]{:S(2)}, u32[]{:S(2)}) collective-permute-start(bf16[288,128]{1,0:T(8,128)(2,1)S(1)} %get-tuple-element.39), channel_id=1, source_target_pairs={{0,1},{1,0},{2,3},{3,2},{4,5},{5,4},{6,7},{7,6},{8,9},{9,8},{10,11... | collective-permute-start | bytes 221192 | tf_op jit(solution)/shard_map/ppermute | solution.py:377
  21.6 5.7 %collective-permute-start.9 = (bf16[272,256]{1,0:T(8,128)(2,1)S(1)}, bf16[272,256]{1,0:T(8,128)(2,1)S(1)}, u32[]{:S(2)}, u32[]{:S(2)}) collective-permute-start(bf16[272,256]{1,0:T(8,128)(2,1)S(1)} %get-tuple-element.53), channel_id=1, source_target_pairs={{0,8},{8,0},{16,24},{24,16},{1,9},{9,1},{17,25},{25,17},{2,10},{10... | collective-permute-start | bytes 417800 | tf_op jit(solution)/shard_map/ppermute | solution.py:377
  23.1 8.0 %collective-permute-start.7 = (bf16[272,256]{1,0:T(8,128)(2,1)S(1)}, bf16[272,256]{1,0:T(8,128)(2,1)S(1)}, u32[]{:S(2)}, u32[]{:S(2)}) collective-permute-start(bf16[272,256]{1,0:T(8,128)(2,1)S(1)} %get-tuple-element.51), channel_id=1, source_target_pairs={{0,16},{8,24},{16,0},{24,8},{1,17},{9,25},{17,1},{25,9},{2,18},{10... | collective-permute-start | bytes 417800 | tf_op jit(solution)/shard_map/ppermute | solution.py:377
  24.6 6.5 %collective-permute-start.8 = (bf16[272,256]{1,0:T(8,128)(2,1)S(1)}, bf16[272,256]{1,0:T(8,128)(2,1)S(1)}, u32[]{:S(2)}, u32[]{:S(2)}) collective-permute-start(bf16[272,256]{1,0:T(8,128)(2,1)S(1)} %get-tuple-element.52), channel_id=1, source_target_pairs={{0,24},{8,16},{16,8},{24,0},{1,25},{9,17},{17,9},{25,1},{2,26},{10... | collective-permute-start | bytes 417800 | tf_op jit(solution)/shard_map/ppermute | solution.py:377

commit v6 on v5

--- a/solution.py
+++ b/solution.py
@@ -256,7 +256,7 @@
 
 
 def send_order(count):
-    return [6, 7, 5, 3, 4, 2, 1, 0] if count == SUBS else list(range(count - 1, -1, -1))
+    return [6, 7, 5, 2, 4, 3, 1, 0] if count == SUBS else list(range(count - 1, -1, -1))
 
 
 def dot(left, right):

time: 32.7 us -> 32.7 us (level)
  waiting for transfers between devices: 7.65 us -> 10.3 us
  starting transfers between devices: 15.5 us -> 12.9 us
    ppermute x10, waiting for transfers between devices: 7.65 us -> 10.3 us  [swapped(): lax.ppermute(block, axis, [(low, low ^ mask) for low in range(count)])]
    ppermute x10, starting transfers between devices: 15.5 us -> 12.9 us  [swapped(): lax.ppermute(block, axis, [(low, low ^ mask) for low in range(count)])]
  transfers between devices with their start and end apart: 10 -> 10, of which waited for: 3 -> 4; matrix products, arithmetic and copies ran while one was open for 0% -> 0% of each run, Pallas kernels for 12% -> 12%
where the time goes in v6:
time: 32.7 us; the launch traced here: 32.5 us
  starting transfers between devices  12.9 us (39%)
  waiting for transfers between devices  10.3 us (31%)
  Pallas kernels  9.22 us (28%)
    ppermute x10, starting transfers between devices, swapped(): lax.ppermute(block, axis, [(low, low ^ mask) for low in range(count)])  12.9 us
    ppermute x10, waiting for transfers between devices, swapped(): lax.ppermute(block, axis, [(low, low ^ mask) for low in range(count)])  10.3 us
    pallas_call x1, Pallas kernels, on_device(): pl.pallas_call(table_kernel, out_shape=[shape((wide2, wide2), bf16), shap...  3.43 us
    pallas_call x1, Pallas kernels, on_device(): pl.pallas_call(functools.partial(beam_kernel, pulses=pulses), out_shape=[...  1.95 us
    pallas_call x1, Pallas kernels, on_device(): pl.pallas_call(functools.partial(band_kernel, sources=n_band), out_shape=...  1.93 us
    pallas_call x1, Pallas kernels, on_device(): pl.pallas_call(grp_kernel, out_shape=shape((2, ANGLES, freq_count), bf16)...  1.35 us
  transfers between devices with their start and end apart: 10, of which 4 were waited for; matrix products, arithmetic and copies ran while one was open for 0% of the time, Pallas kernels for 12%

profile of v6, /device:TPU:0, one launch (start us, length us, event | category | flops | bytes accessed | tf_op | source)
XLA Modules:
  0.0 32.5 jit_solution(14067986767896937581)
XLA Ops:
  0.0 1.9 %beam.1 = (bf16[288,128]{1,0:T(8,128)(2,1)S(1)}, bf16[288,128]{1,0:T(8,128)(2,1)S(1)}, bf16[288,128]{1,0:T(8,128)(2,1)S(1)}, bf16[288,128]{1,0:T(8,128)(2,1)S(1)...) custom-call(bf16[2,32,4096]{2,1,0:T(8,128)(2,1)} %raw_far.1, ...), custom_call_target="tpu_custom_call" | custom-call | flops 150994944 | bytes 2097152 | tf_op jit(solution)/shard_map/beam/pallas_call | solution.py:391
  2.0 5.1 %collective-permute-start = (bf16[288,128]{1,0:T(8,128)(2,1)S(1)}, bf16[288,128]{1,0:T(8,128)(2,1)S(1)}, u32[]{:S(2)}, u32[]{:S(2)}) collective-permute-start(bf16[288,128]{1,0:T(8,128)(2,1)S(1)} %get-tuple-element.33), channel_id=1, source_target_pairs={{0,6},{1,7},{2,4},{3,5},{4,2},{5,3},{6,0},{7,1},{8,14},{9,15},{10,... | collective-permute-start | bytes 221192 | tf_op jit(solution)/shard_map/ppermute | solution.py:377
  7.1 0.0 collective-permute-start.1
  7.1 0.7 %collective-permute-start.2 = (bf16[288,128]{1,0:T(8,128)(2,1)S(1)}, bf16[288,128]{1,0:T(8,128)(2,1)S(1)}, u32[]{:S(2)}, u32[]{:S(2)}) collective-permute-start(bf16[288,128]{1,0:T(8,128)(2,1)S(1)} %get-tuple-element.35), channel_id=1, source_target_pairs={{0,5},{1,4},{2,7},{3,6},{4,1},{5,0},{6,3},{7,2},{8,13},{9,12},{10,... | collective-permute-start | bytes 221192 | tf_op jit(solution)/shard_map/ppermute | solution.py:377
  7.8 3.4 %collective-permute-start.3 = (bf16[288,128]{1,0:T(8,128)(2,1)S(1)}, bf16[288,128]{1,0:T(8,128)(2,1)S(1)}, u32[]{:S(2)}, u32[]{:S(2)}) collective-permute-start(bf16[288,128]{1,0:T(8,128)(2,1)S(1)} %get-tuple-element.36), channel_id=1, source_target_pairs={{0,2},{1,3},{2,0},{3,1},{4,6},{5,7},{6,4},{7,5},{8,10},{9,11},{10,... | collective-permute-start | bytes 221192 | tf_op jit(solution)/shard_map/ppermute | solution.py:377
  11.2 0.0 collective-permute-start.4
  11.2 0.0 collective-permute-done.refs_0_
  11.2 0.1 collective-permute-start.5
  11.3 2.3 %collective-permute-done.1.refs_1_ = bf16[288,128]{1,0:T(8,128)(2,1)S(1)} collective-permute-done((bf16[288,128]{1,0:T(8,128)(2,1)S(1)}, bf16[288,128]{1,0:T(8,128)(2,1)S(1)}, u32[]{:S(2)}, u32[]{:S(2)}) %collective-permute-start.1) | collective-permute-done | bytes 73760 | tf_op jit(solution)/shard_map/ppermute | solution.py:377
  13.6 0.1 collective-permute-start.6
  13.6 3.4 %tables.1 = (bf16[512,512]{1,0:T(8,128)(2,1)S(1)}, bf16[288,160]{1,0:T(8,128)(2,1)S(1)}, bf16[256,144]{1,0:T(8,128)(2,1)S(1)}, bf16[576,256]{1,0:T(8,128)(2,1)S(...) custom-call(f32[5]{0:T(128)S(1)} %copy-done.3, ...), custom_call_target="tpu_custom_call" | custom-call | flops 16777216 | bytes 8388608 | tf_op jit(solution)/shard_map/tables/pallas_call | solution.py:412
  17.1 0.0 collective-permute-done.3.refs_3_
  17.1 2.5 %collective-permute-done.4.refs_4_ = bf16[288,128]{1,0:T(8,128)(2,1)S(1)} collective-permute-done((bf16[288,128]{1,0:T(8,128)(2,1)S(1)}, bf16[288,128]{1,0:T(8,128)(2,1)S(1)}, u32[]{:S(2)}, u32[]{:S(2)}) %collective-permute-start.4) | collective-permute-done | bytes 73760 | tf_op jit(solution)/shard_map/ppermute | solution.py:377
  19.6 0.0 collective-permute-done.5.refs_5_
  19.6 0.0 collective-permute-done.6.refs_6_
  19.6 1.9 %band_merges.1 = (bf16[272,256]{1,0:T(8,128)(2,1)S(1)}, bf16[272,256]{1,0:T(8,128)(2,1)S(1)}, bf16[272,256]{1,0:T(8,128)(2,1)S(1)}, bf16[272,256]{1,0:T(8,128)(2,1)S(1)}) custom-call(bf16[288,128]{1,0:T(8,128)(2,1)S(1)} %collective-permute-done.refs_0_, bf16[288,128]{1,0:T(8,128)(2,1)S(1)} %collective-permute-done.1.refs_1_, ...), custom_call_target="tpu_custom_call" | custom-call | flops 2147483648 | bytes 4194304 | tf_op jit(solution)/shard_map/band_merges/pallas_call | solution.py:439
  21.6 1.6 %collective-permute-start.9 = (bf16[272,256]{1,0:T(8,128)(2,1)S(1)}, bf16[272,256]{1,0:T(8,128)(2,1)S(1)}, u32[]{:S(2)}, u32[]{:S(2)}) collective-permute-start(bf16[272,256]{1,0:T(8,128)(2,1)S(1)} %get-tuple-element.53), channel_id=1, source_target_pairs={{0,8},{8,0},{16,24},{24,16},{1,9},{9,1},{17,25},{25,17},{2,10},{10... | collective-permute-start | bytes 417800 | tf_op jit(solution)/shard_map/ppermute | solution.py:377
  23.1 1.5 %collective-permute-start.7 = (bf16[272,256]{1,0:T(8,128)(2,1)S(1)}, bf16[272,256]{1,0:T(8,128)(2,1)S(1)}, u32[]{:S(2)}, u32[]{:S(2)}) collective-permute-start(bf16[272,256]{1,0:T(8,128)(2,1)S(1)} %get-tuple-element.51), channel_id=1, source_target_pairs={{0,16},{8,24},{16,0},{24,8},{1,17},{9,25},{17,1},{25,9},{2,18},{10... | collective-permute-start | bytes 417800 | tf_op jit(solution)/shard_map/ppermute | solution.py:377
  24.6 0.5 %collective-permute-start.8 = (bf16[272,256]{1,0:T(8,128)(2,1)S(1)}, bf16[272,256]{1,0:T(8,128)(2,1)S(1)}, u32[]{:S(2)}, u32[]{:S(2)}) collective-permute-start(bf16[272,256]{1,0:T(8,128)(2,1)S(1)} %get-tuple-element.52), channel_id=1, source_target_pairs={{0,24},{8,16},{16,8},{24,0},{1,25},{9,17},{17,9},{25,1},{2,26},{10... | collective-permute-start | bytes 417800 | tf_op jit(solution)/shard_map/ppermute | solution.py:377
  25.1 2.1 %collective-permute-done.9.along = bf16[272,256]{1,0:T(8,128)(2,1)S(1)} collective-permute-done((bf16[272,256]{1,0:T(8,128)(2,1)S(1)}, bf16[272,256]{1,0:T(8,128)(2,1)S(1)}, u32[]{:S(2)}, u32[]{:S(2)}) %collective-permute-start.9) | collective-permute-done | bytes 139296 | tf_op jit(solution)/shard_map/ppermute | solution.py:377
  27.2 0.6 %own_merge.1.part = f32[512,512]{1,0:T(8,128)S(1)} custom-call(bf16[272,256]{1,0:T(8,128)(2,1)S(1)} %collective-permute-done.9.along, bf16[272,256]{1,0:T(8,128)(2,1)S(1)} %get-tuple-element.54.own, bf16[2,256,144]{2,1,0:T(8,128)(2,1)S(1)} %get-tuple-element.55.m3, bf16[512,256]{1,0:T(8,128)(2,1)S(1)} %get-tuple-element.56.m4, ...), custom_call_target="tpu_custom_call" | custom-call | flops 536870912 | bytes 2097152 | tf_op jit(solution)/shard_map/own_merge/pallas_call | solution.py:457
  27.8 3.4 %collective-permute-done.7.across = bf16[272,256]{1,0:T(8,128)(2,1)S(1)} collective-permute-done((bf16[272,256]{1,0:T(8,128)(2,1)S(1)}, bf16[272,256]{1,0:T(8,128)(2,1)S(1)}, u32[]{:S(2)}, u32[]{:S(2)}) %collective-permute-start.7) | collective-permute-done | bytes 139296 | tf_op jit(solution)/shard_map/ppermute | solution.py:377
  31.2 0.0 collective-permute-done.8.both
  31.2 1.3 %grp_merges.1 = bf16[2,512,256]{2,1,0:T(8,128)(2,1)} custom-call(bf16[272,256]{1,0:T(8,128)(2,1)S(1)} %collective-permute-done.7.across, bf16[272,256]{1,0:T(8,128)(2,1)S(1)} %collective-permute-done.8.both, f32[512,512]{1,0:T(8,128)S(1)} %own_merge.1.part, bf16[2,256,144]{2,1,0:T(8,128)(2,1)S(1)} %get-tuple-element.55.m3, ...), custom_call_target="tpu_custom_call" | custom-call | flops 536870912 | bytes 2097152 | tf_op jit(solution)/shard_map/grp_merges/pallas_call | solution.py:467
  (9 shorter events, 0.0 us)
Async XLA Ops:
  0.0 13.6 %copy-start = (bf16[8,64,512]{2,1,0:T(8,128)(2,1)S(1)}, bf16[8,64,512]{2,1,0:T(8,128)(2,1)}, u32[]{:S(2)}) copy-start(bf16[8,64,512]{2,1,0:T(8,128)(2,1)} %constant.5.clone.ranges) | copy-start | bytes 1572868
  0.0 13.6 %copy-start.2 = (f32[5,2,4,512]{3,2,1,0:T(4,128)S(1)}, f32[5,2,4,512]{3,2,1,0:T(4,128)}, u32[]{:S(2)}) copy-start(f32[5,2,4,512]{3,2,1,0:T(4,128)} %weights.1) | copy-start | bytes 245764
  0.0 13.6 %copy-start.1 = (s32[5,2,4,512]{3,2,1,0:T(4,128)S(1)}, s32[5,2,4,512]{3,2,1,0:T(4,128)}, u32[]{:S(2)}) copy-start(s32[5,2,4,512]{3,2,1,0:T(4,128)} %taps.1) | copy-start | bytes 245764
  2.0 9.2 %collective-permute-start = (bf16[288,128]{1,0:T(8,128)(2,1)S(1)}, bf16[288,128]{1,0:T(8,128)(2,1)S(1)}, u32[]{:S(2)}, u32[]{:S(2)}) collective-permute-start(bf16[288,128]{1,0:T(8,128)(2,1)S(1)} %get-tuple-element.33), channel_id=1, source_target_pairs={{0,6},{1,7},{2,4},{3,5},{4,2},{5,3},{6,0},{7,1},{8,14},{9,15},{10,... | collective-permute-start | bytes 221192 | tf_op jit(solution)/shard_map/ppermute | solution.py:377
  7.1 6.5 %collective-permute-start.1 = (bf16[288,128]{1,0:T(8,128)(2,1)S(1)}, bf16[288,128]{1,0:T(8,128)(2,1)S(1)}, u32[]{:S(2)}, u32[]{:S(2)}) collective-permute-start(bf16[288,128]{1,0:T(8,128)(2,1)S(1)} %get-tuple-element.34), channel_id=1, source_target_pairs={{0,7},{1,6},{2,5},{3,4},{4,3},{5,2},{6,1},{7,0},{8,15},{9,14},{10,... | collective-permute-start | bytes 221192 | tf_op jit(solution)/shard_map/ppermute | solution.py:377
  7.1 10.0 %collective-permute-start.2 = (bf16[288,128]{1,0:T(8,128)(2,1)S(1)}, bf16[288,128]{1,0:T(8,128)(2,1)S(1)}, u32[]{:S(2)}, u32[]{:S(2)}) collective-permute-start(bf16[288,128]{1,0:T(8,128)(2,1)S(1)} %get-tuple-element.35), channel_id=1, source_target_pairs={{0,5},{1,4},{2,7},{3,6},{4,1},{5,0},{6,3},{7,2},{8,13},{9,12},{10,... | collective-permute-start | bytes 221192 | tf_op jit(solution)/shard_map/ppermute | solution.py:377
  7.8 9.3 %collective-permute-start.3 = (bf16[288,128]{1,0:T(8,128)(2,1)S(1)}, bf16[288,128]{1,0:T(8,128)(2,1)S(1)}, u32[]{:S(2)}, u32[]{:S(2)}) collective-permute-start(bf16[288,128]{1,0:T(8,128)(2,1)S(1)} %get-tuple-element.36), channel_id=1, source_target_pairs={{0,2},{1,3},{2,0},{3,1},{4,6},{5,7},{6,4},{7,5},{8,10},{9,11},{10,... | collective-permute-start | bytes 221192 | tf_op jit(solution)/shard_map/ppermute | solution.py:377
  11.2 8.4 %collective-permute-start.4 = (bf16[288,128]{1,0:T(8,128)(2,1)S(1)}, bf16[288,128]{1,0:T(8,128)(2,1)S(1)}, u32[]{:S(2)}, u32[]{:S(2)}) collective-permute-start(bf16[288,128]{1,0:T(8,128)(2,1)S(1)} %get-tuple-element.37), channel_id=1, source_target_pairs={{0,4},{1,5},{2,6},{3,7},{4,0},{5,1},{6,2},{7,3},{8,12},{9,13},{10,... | collective-permute-start | bytes 221192 | tf_op jit(solution)/shard_map/ppermute | solution.py:377
  11.2 2.4 %copy-start.3 = (f32[5]{0:T(128)S(1)}, f32[5]{0:T(128)}, u32[]{:S(2)}) copy-start(f32[5]{0:T(128)} %shifts.1) | copy-start | bytes 64
  11.2 8.4 %collective-permute-start.5 = (bf16[288,128]{1,0:T(8,128)(2,1)S(1)}, bf16[288,128]{1,0:T(8,128)(2,1)S(1)}, u32[]{:S(2)}, u32[]{:S(2)}) collective-permute-start(bf16[288,128]{1,0:T(8,128)(2,1)S(1)} %get-tuple-element.38), channel_id=1, source_target_pairs={{0,3},{1,2},{2,1},{3,0},{4,7},{5,6},{6,5},{7,4},{8,11},{9,10},{10,... | collective-permute-start | bytes 221192 | tf_op jit(solution)/shard_map/ppermute | solution.py:377
  13.6 6.1 %collective-permute-start.6 = (bf16[288,128]{1,0:T(8,128)(2,1)S(1)}, bf16[288,128]{1,0:T(8,128)(2,1)S(1)}, u32[]{:S(2)}, u32[]{:S(2)}) collective-permute-start(bf16[288,128]{1,0:T(8,128)(2,1)S(1)} %get-tuple-element.39), channel_id=1, source_target_pairs={{0,1},{1,0},{2,3},{3,2},{4,5},{5,4},{6,7},{7,6},{8,9},{9,8},{10,11... | collective-permute-start | bytes 221192 | tf_op jit(solution)/shard_map/ppermute | solution.py:377
  21.6 5.7 %collective-permute-start.9 = (bf16[272,256]{1,0:T(8,128)(2,1)S(1)}, bf16[272,256]{1,0:T(8,128)(2,1)S(1)}, u32[]{:S(2)}, u32[]{:S(2)}) collective-permute-start(bf16[272,256]{1,0:T(8,128)(2,1)S(1)} %get-tuple-element.53), channel_id=1, source_target_pairs={{0,8},{8,0},{16,24},{24,16},{1,9},{9,1},{17,25},{25,17},{2,10},{10... | collective-permute-start | bytes 417800 | tf_op jit(solution)/shard_map/ppermute | solution.py:377
  23.1 8.0 %collective-permute-start.7 = (bf16[272,256]{1,0:T(8,128)(2,1)S(1)}, bf16[272,256]{1,0:T(8,128)(2,1)S(1)}, u32[]{:S(2)}, u32[]{:S(2)}) collective-permute-start(bf16[272,256]{1,0:T(8,128)(2,1)S(1)} %get-tuple-element.51), channel_id=1, source_target_pairs={{0,16},{8,24},{16,0},{24,8},{1,17},{9,25},{17,1},{25,9},{2,18},{10... | collective-permute-start | bytes 417800 | tf_op jit(solution)/shard_map/ppermute | solution.py:377
  24.6 6.5 %collective-permute-start.8 = (bf16[272,256]{1,0:T(8,128)(2,1)S(1)}, bf16[272,256]{1,0:T(8,128)(2,1)S(1)}, u32[]{:S(2)}, u32[]{:S(2)}) collective-permute-start(bf16[272,256]{1,0:T(8,128)(2,1)S(1)} %get-tuple-element.52), channel_id=1, source_target_pairs={{0,24},{8,16},{16,8},{24,0},{1,25},{9,17},{17,9},{25,1},{2,26},{10... | collective-permute-start | bytes 417800 | tf_op jit(solution)/shard_map/ppermute | solution.py:377

commit v7 on v5

--- a/solution.py
+++ b/solution.py
@@ -472,7 +472,7 @@
         scratch_shapes=[
             pltpu.VMEM((HALF, wide2), bf16),
             pltpu.VMEM((2, ANGLES, freq_count), bf16),
-            pltpu.SemaphoreType.DMA((4,)),
+            pltpu.SemaphoreType.DMA((2,)),
         ],
         compiler_params=PARAMS,
         cost_estimate=pl.CostEstimate(flops=1 << 29, bytes_accessed=1 << 21, transcendentals=0),

time: 32.7 us -> 32.7 us (level)
  no operation moved by 1% of the time
where the time goes in v7:
time: 32.7 us; the launch traced here: 32.5 us
  starting transfers between devices  15.5 us (47%)
  Pallas kernels  9.25 us (28%)
  waiting for transfers between devices  7.65 us (23%)
    ppermute x10, starting transfers between devices, swapped(): lax.ppermute(block, axis, [(low, low ^ mask) for low in range(count)])  15.5 us
    ppermute x10, waiting for transfers between devices, swapped(): lax.ppermute(block, axis, [(low, low ^ mask) for low in range(count)])  7.65 us
    pallas_call x1, Pallas kernels, on_device(): pl.pallas_call(table_kernel, out_shape=[shape((wide2, wide2), bf16), shap...  3.43 us
    pallas_call x1, Pallas kernels, on_device(): pl.pallas_call(functools.partial(beam_kernel, pulses=pulses), out_shape=[...  1.95 us
    pallas_call x1, Pallas kernels, on_device(): pl.pallas_call(functools.partial(band_kernel, sources=n_band), out_shape=...  1.93 us
    pallas_call x1, Pallas kernels, on_device(): pl.pallas_call(grp_kernel, out_shape=shape((2, ANGLES, freq_count), bf16)...  1.38 us
  transfers between devices with their start and end apart: 10, of which 3 were waited for; matrix products, arithmetic and copies ran while one was open for 0% of the time, Pallas kernels for 12%

profile of v7, /device:TPU:0, one launch (start us, length us, event | category | flops | bytes accessed | tf_op | source)
XLA Modules:
  0.0 32.5 jit_solution(10074546021698021989)
XLA Ops:
  0.0 1.9 %beam.1 = (bf16[288,128]{1,0:T(8,128)(2,1)S(1)}, bf16[288,128]{1,0:T(8,128)(2,1)S(1)}, bf16[288,128]{1,0:T(8,128)(2,1)S(1)}, bf16[288,128]{1,0:T(8,128)(2,1)S(1)...) custom-call(bf16[2,32,4096]{2,1,0:T(8,128)(2,1)} %raw_far.1, ...), custom_call_target="tpu_custom_call" | custom-call | flops 150994944 | bytes 2097152 | tf_op jit(solution)/shard_map/beam/pallas_call | solution.py:391
  2.0 5.1 %collective-permute-start = (bf16[288,128]{1,0:T(8,128)(2,1)S(1)}, bf16[288,128]{1,0:T(8,128)(2,1)S(1)}, u32[]{:S(2)}, u32[]{:S(2)}) collective-permute-start(bf16[288,128]{1,0:T(8,128)(2,1)S(1)} %get-tuple-element.33), channel_id=1, source_target_pairs={{0,6},{1,7},{2,4},{3,5},{4,2},{5,3},{6,0},{7,1},{8,14},{9,15},{10,... | collective-permute-start | bytes 221192 | tf_op jit(solution)/shard_map/ppermute | solution.py:377
  7.1 0.0 collective-permute-start.1
  7.1 0.7 %collective-permute-start.2 = (bf16[288,128]{1,0:T(8,128)(2,1)S(1)}, bf16[288,128]{1,0:T(8,128)(2,1)S(1)}, u32[]{:S(2)}, u32[]{:S(2)}) collective-permute-start(bf16[288,128]{1,0:T(8,128)(2,1)S(1)} %get-tuple-element.35), channel_id=1, source_target_pairs={{0,5},{1,4},{2,7},{3,6},{4,1},{5,0},{6,3},{7,2},{8,13},{9,12},{10,... | collective-permute-start | bytes 221192 | tf_op jit(solution)/shard_map/ppermute | solution.py:377
  7.8 2.5 %collective-permute-start.3 = (bf16[288,128]{1,0:T(8,128)(2,1)S(1)}, bf16[288,128]{1,0:T(8,128)(2,1)S(1)}, u32[]{:S(2)}, u32[]{:S(2)}) collective-permute-start(bf16[288,128]{1,0:T(8,128)(2,1)S(1)} %get-tuple-element.36), channel_id=1, source_target_pairs={{0,3},{1,2},{2,1},{3,0},{4,7},{5,6},{6,5},{7,4},{8,11},{9,10},{10,... | collective-permute-start | bytes 221192 | tf_op jit(solution)/shard_map/ppermute | solution.py:377
  10.4 0.8 %collective-permute-start.4 = (bf16[288,128]{1,0:T(8,128)(2,1)S(1)}, bf16[288,128]{1,0:T(8,128)(2,1)S(1)}, u32[]{:S(2)}, u32[]{:S(2)}) collective-permute-start(bf16[288,128]{1,0:T(8,128)(2,1)S(1)} %get-tuple-element.37), channel_id=1, source_target_pairs={{0,4},{1,5},{2,6},{3,7},{4,0},{5,1},{6,2},{7,3},{8,12},{9,13},{10,... | collective-permute-start | bytes 221192 | tf_op jit(solution)/shard_map/ppermute | solution.py:377
  11.2 0.0 collective-permute-done.refs_0_
  11.2 2.8 %collective-permute-start.5 = (bf16[288,128]{1,0:T(8,128)(2,1)S(1)}, bf16[288,128]{1,0:T(8,128)(2,1)S(1)}, u32[]{:S(2)}, u32[]{:S(2)}) collective-permute-start(bf16[288,128]{1,0:T(8,128)(2,1)S(1)} %get-tuple-element.38), channel_id=1, source_target_pairs={{0,2},{1,3},{2,0},{3,1},{4,6},{5,7},{6,4},{7,5},{8,10},{9,11},{10,... | collective-permute-start | bytes 221192 | tf_op jit(solution)/shard_map/ppermute | solution.py:377
  14.0 0.0 collective-permute-done.1.refs_1_
  14.0 0.0 collective-permute-start.6
  14.0 3.4 %tables.1 = (bf16[512,512]{1,0:T(8,128)(2,1)S(1)}, bf16[288,160]{1,0:T(8,128)(2,1)S(1)}, bf16[256,144]{1,0:T(8,128)(2,1)S(1)}, bf16[576,256]{1,0:T(8,128)(2,1)S(...) custom-call(f32[5]{0:T(128)S(1)} %copy-done.3, ...), custom_call_target="tpu_custom_call" | custom-call | flops 16777216 | bytes 8388608 | tf_op jit(solution)/shard_map/tables/pallas_call | solution.py:412
  17.4 0.0 collective-permute-done.2.refs_2_
  17.4 2.2 %collective-permute-done.4.refs_4_ = bf16[288,128]{1,0:T(8,128)(2,1)S(1)} collective-permute-done((bf16[288,128]{1,0:T(8,128)(2,1)S(1)}, bf16[288,128]{1,0:T(8,128)(2,1)S(1)}, u32[]{:S(2)}, u32[]{:S(2)}) %collective-permute-start.4) | collective-permute-done | bytes 73760 | tf_op jit(solution)/shard_map/ppermute | solution.py:377
  19.6 0.0 collective-permute-done.5.refs_5_
  19.6 0.0 collective-permute-done.6.refs_6_
  19.6 1.9 %band_merges.1 = (bf16[272,256]{1,0:T(8,128)(2,1)S(1)}, bf16[272,256]{1,0:T(8,128)(2,1)S(1)}, bf16[272,256]{1,0:T(8,128)(2,1)S(1)}, bf16[272,256]{1,0:T(8,128)(2,1)S(1)}) custom-call(bf16[288,128]{1,0:T(8,128)(2,1)S(1)} %collective-permute-done.refs_0_, bf16[288,128]{1,0:T(8,128)(2,1)S(1)} %collective-permute-done.1.refs_1_, ...), custom_call_target="tpu_custom_call" | custom-call | flops 2147483648 | bytes 4194304 | tf_op jit(solution)/shard_map/band_merges/pallas_call | solution.py:439
  21.6 1.6 %collective-permute-start.9 = (bf16[272,256]{1,0:T(8,128)(2,1)S(1)}, bf16[272,256]{1,0:T(8,128)(2,1)S(1)}, u32[]{:S(2)}, u32[]{:S(2)}) collective-permute-start(bf16[272,256]{1,0:T(8,128)(2,1)S(1)} %get-tuple-element.53), channel_id=1, source_target_pairs={{0,8},{8,0},{16,24},{24,16},{1,9},{9,1},{17,25},{25,17},{2,10},{10... | collective-permute-start | bytes 417800 | tf_op jit(solution)/shard_map/ppermute | solution.py:377
  23.1 1.5 %collective-permute-start.7 = (bf16[272,256]{1,0:T(8,128)(2,1)S(1)}, bf16[272,256]{1,0:T(8,128)(2,1)S(1)}, u32[]{:S(2)}, u32[]{:S(2)}) collective-permute-start(bf16[272,256]{1,0:T(8,128)(2,1)S(1)} %get-tuple-element.51), channel_id=1, source_target_pairs={{0,16},{8,24},{16,0},{24,8},{1,17},{9,25},{17,1},{25,9},{2,18},{10... | collective-permute-start | bytes 417800 | tf_op jit(solution)/shard_map/ppermute | solution.py:377
  24.6 0.5 %collective-permute-start.8 = (bf16[272,256]{1,0:T(8,128)(2,1)S(1)}, bf16[272,256]{1,0:T(8,128)(2,1)S(1)}, u32[]{:S(2)}, u32[]{:S(2)}) collective-permute-start(bf16[272,256]{1,0:T(8,128)(2,1)S(1)} %get-tuple-element.52), channel_id=1, source_target_pairs={{0,24},{8,16},{16,8},{24,0},{1,25},{9,17},{17,9},{25,1},{2,26},{10... | collective-permute-start | bytes 417800 | tf_op jit(solution)/shard_map/ppermute | solution.py:377
  25.1 2.1 %collective-permute-done.9.along = bf16[272,256]{1,0:T(8,128)(2,1)S(1)} collective-permute-done((bf16[272,256]{1,0:T(8,128)(2,1)S(1)}, bf16[272,256]{1,0:T(8,128)(2,1)S(1)}, u32[]{:S(2)}, u32[]{:S(2)}) %collective-permute-start.9) | collective-permute-done | bytes 139296 | tf_op jit(solution)/shard_map/ppermute | solution.py:377
  27.2 0.6 %own_merge.1.part = f32[512,512]{1,0:T(8,128)S(1)} custom-call(bf16[272,256]{1,0:T(8,128)(2,1)S(1)} %collective-permute-done.9.along, bf16[272,256]{1,0:T(8,128)(2,1)S(1)} %get-tuple-element.54.own, bf16[2,256,144]{2,1,0:T(8,128)(2,1)S(1)} %get-tuple-element.55.m3, bf16[512,256]{1,0:T(8,128)(2,1)S(1)} %get-tuple-element.56.m4, ...), custom_call_target="tpu_custom_call" | custom-call | flops 536870912 | bytes 2097152 | tf_op jit(solution)/shard_map/own_merge/pallas_call | solution.py:457
  27.8 3.4 %collective-permute-done.7.across = bf16[272,256]{1,0:T(8,128)(2,1)S(1)} collective-permute-done((bf16[272,256]{1,0:T(8,128)(2,1)S(1)}, bf16[272,256]{1,0:T(8,128)(2,1)S(1)}, u32[]{:S(2)}, u32[]{:S(2)}) %collective-permute-start.7) | collective-permute-done | bytes 139296 | tf_op jit(solution)/shard_map/ppermute | solution.py:377
  31.2 0.0 collective-permute-done.8.both
  31.2 1.4 %grp_merges.1 = bf16[2,512,256]{2,1,0:T(8,128)(2,1)} custom-call(bf16[272,256]{1,0:T(8,128)(2,1)S(1)} %collective-permute-done.7.across, bf16[272,256]{1,0:T(8,128)(2,1)S(1)} %collective-permute-done.8.both, f32[512,512]{1,0:T(8,128)S(1)} %own_merge.1.part, bf16[2,256,144]{2,1,0:T(8,128)(2,1)S(1)} %get-tuple-element.55.m3, ...), custom_call_target="tpu_custom_call" | custom-call | flops 536870912 | bytes 2097152 | tf_op jit(solution)/shard_map/grp_merges/pallas_call | solution.py:467
  (9 shorter events, 0.0 us)
Async XLA Ops:
  0.0 14.0 %copy-start = (bf16[8,64,512]{2,1,0:T(8,128)(2,1)S(1)}, bf16[8,64,512]{2,1,0:T(8,128)(2,1)}, u32[]{:S(2)}) copy-start(bf16[8,64,512]{2,1,0:T(8,128)(2,1)} %constant.5.clone.ranges) | copy-start | bytes 1572868
  0.0 14.0 %copy-start.2 = (f32[5,2,4,512]{3,2,1,0:T(4,128)S(1)}, f32[5,2,4,512]{3,2,1,0:T(4,128)}, u32[]{:S(2)}) copy-start(f32[5,2,4,512]{3,2,1,0:T(4,128)} %weights.1) | copy-start | bytes 245764
  0.0 14.0 %copy-start.1 = (s32[5,2,4,512]{3,2,1,0:T(4,128)S(1)}, s32[5,2,4,512]{3,2,1,0:T(4,128)}, u32[]{:S(2)}) copy-start(s32[5,2,4,512]{3,2,1,0:T(4,128)} %taps.1) | copy-start | bytes 245764
  2.0 9.2 %collective-permute-start = (bf16[288,128]{1,0:T(8,128)(2,1)S(1)}, bf16[288,128]{1,0:T(8,128)(2,1)S(1)}, u32[]{:S(2)}, u32[]{:S(2)}) collective-permute-start(bf16[288,128]{1,0:T(8,128)(2,1)S(1)} %get-tuple-element.33), channel_id=1, source_target_pairs={{0,6},{1,7},{2,4},{3,5},{4,2},{5,3},{6,0},{7,1},{8,14},{9,15},{10,... | collective-permute-start | bytes 221192 | tf_op jit(solution)/shard_map/ppermute | solution.py:377
  7.1 6.9 %collective-permute-start.1 = (bf16[288,128]{1,0:T(8,128)(2,1)S(1)}, bf16[288,128]{1,0:T(8,128)(2,1)S(1)}, u32[]{:S(2)}, u32[]{:S(2)}) collective-permute-start(bf16[288,128]{1,0:T(8,128)(2,1)S(1)} %get-tuple-element.34), channel_id=1, source_target_pairs={{0,7},{1,6},{2,5},{3,4},{4,3},{5,2},{6,1},{7,0},{8,15},{9,14},{10,... | collective-permute-start | bytes 221192 | tf_op jit(solution)/shard_map/ppermute | solution.py:377
  7.1 10.3 %collective-permute-start.2 = (bf16[288,128]{1,0:T(8,128)(2,1)S(1)}, bf16[288,128]{1,0:T(8,128)(2,1)S(1)}, u32[]{:S(2)}, u32[]{:S(2)}) collective-permute-start(bf16[288,128]{1,0:T(8,128)(2,1)S(1)} %get-tuple-element.35), channel_id=1, source_target_pairs={{0,5},{1,4},{2,7},{3,6},{4,1},{5,0},{6,3},{7,2},{8,13},{9,12},{10,... | collective-permute-start | bytes 221192 | tf_op jit(solution)/shard_map/ppermute | solution.py:377
  7.8 9.6 %collective-permute-start.3 = (bf16[288,128]{1,0:T(8,128)(2,1)S(1)}, bf16[288,128]{1,0:T(8,128)(2,1)S(1)}, u32[]{:S(2)}, u32[]{:S(2)}) collective-permute-start(bf16[288,128]{1,0:T(8,128)(2,1)S(1)} %get-tuple-element.36), channel_id=1, source_target_pairs={{0,3},{1,2},{2,1},{3,0},{4,7},{5,6},{6,5},{7,4},{8,11},{9,10},{10,... | collective-permute-start | bytes 221192 | tf_op jit(solution)/shard_map/ppermute | solution.py:377
  10.4 9.3 %collective-permute-start.4 = (bf16[288,128]{1,0:T(8,128)(2,1)S(1)}, bf16[288,128]{1,0:T(8,128)(2,1)S(1)}, u32[]{:S(2)}, u32[]{:S(2)}) collective-permute-start(bf16[288,128]{1,0:T(8,128)(2,1)S(1)} %get-tuple-element.37), channel_id=1, source_target_pairs={{0,4},{1,5},{2,6},{3,7},{4,0},{5,1},{6,2},{7,3},{8,12},{9,13},{10,... | collective-permute-start | bytes 221192 | tf_op jit(solution)/shard_map/ppermute | solution.py:377
  11.2 2.8 %copy-start.3 = (f32[5]{0:T(128)S(1)}, f32[5]{0:T(128)}, u32[]{:S(2)}) copy-start(f32[5]{0:T(128)} %shifts.1) | copy-start | bytes 64
  11.2 8.4 %collective-permute-start.5 = (bf16[288,128]{1,0:T(8,128)(2,1)S(1)}, bf16[288,128]{1,0:T(8,128)(2,1)S(1)}, u32[]{:S(2)}, u32[]{:S(2)}) collective-permute-start(bf16[288,128]{1,0:T(8,128)(2,1)S(1)} %get-tuple-element.38), channel_id=1, source_target_pairs={{0,2},{1,3},{2,0},{3,1},{4,6},{5,7},{6,4},{7,5},{8,10},{9,11},{10,... | collective-permute-start | bytes 221192 | tf_op jit(solution)/shard_map/ppermute | solution.py:377
  14.0 5.7 %collective-permute-start.6 = (bf16[288,128]{1,0:T(8,128)(2,1)S(1)}, bf16[288,128]{1,0:T(8,128)(2,1)S(1)}, u32[]{:S(2)}, u32[]{:S(2)}) collective-permute-start(bf16[288,128]{1,0:T(8,128)(2,1)S(1)} %get-tuple-element.39), channel_id=1, source_target_pairs={{0,1},{1,0},{2,3},{3,2},{4,5},{5,4},{6,7},{7,6},{8,9},{9,8},{10,11... | collective-permute-start | bytes 221192 | tf_op jit(solution)/shard_map/ppermute | solution.py:377
  21.6 5.7 %collective-permute-start.9 = (bf16[272,256]{1,0:T(8,128)(2,1)S(1)}, bf16[272,256]{1,0:T(8,128)(2,1)S(1)}, u32[]{:S(2)}, u32[]{:S(2)}) collective-permute-start(bf16[272,256]{1,0:T(8,128)(2,1)S(1)} %get-tuple-element.53), channel_id=1, source_target_pairs={{0,8},{8,0},{16,24},{24,16},{1,9},{9,1},{17,25},{25,17},{2,10},{10... | collective-permute-start | bytes 417800 | tf_op jit(solution)/shard_map/ppermute | solution.py:377
  23.1 8.0 %collective-permute-start.7 = (bf16[272,256]{1,0:T(8,128)(2,1)S(1)}, bf16[272,256]{1,0:T(8,128)(2,1)S(1)}, u32[]{:S(2)}, u32[]{:S(2)}) collective-permute-start(bf16[272,256]{1,0:T(8,128)(2,1)S(1)} %get-tuple-element.51), channel_id=1, source_target_pairs={{0,16},{8,24},{16,0},{24,8},{1,17},{9,25},{17,1},{25,9},{2,18},{10... | collective-permute-start | bytes 417800 | tf_op jit(solution)/shard_map/ppermute | solution.py:377
  24.6 6.5 %collective-permute-start.8 = (bf16[272,256]{1,0:T(8,128)(2,1)S(1)}, bf16[272,256]{1,0:T(8,128)(2,1)S(1)}, u32[]{:S(2)}, u32[]{:S(2)}) collective-permute-start(bf16[272,256]{1,0:T(8,128)(2,1)S(1)} %get-tuple-element.52), channel_id=1, source_target_pairs={{0,24},{8,16},{16,8},{24,0},{1,25},{9,17},{17,9},{25,1},{2,26},{10... | collective-permute-start | bytes 417800 | tf_op jit(solution)/shard_map/ppermute | solution.py:377
